TPU v7x, 32 devices: a whole 2x2x4 slice. The times are simulated.
32 devices in a mesh: groups: 1, node: 32 (over z, y, x, core).
Axes of the slice: x: 2, y: 2, z: 4, core: 2. Of those that a mesh axis runs over, the one named last changes fastest.
Arguments:
- hidden_in: bfloat16 [128, 4096], P(('groups', 'node')), may hold values from -6 to 6
- queries: bfloat16 [128, 8192], P(('groups', 'node')), may hold values from -90 to 90
- new_kv: bfloat16 [128, 2, 512], P(('groups', 'node')), may hold values from -5 to 5
- kv_cache: bfloat16 [128, 2, 256, 512], P(('groups', 'node')), may hold values from -5 to 5
- lengths: int32 [128], P(('groups', 'node')), may hold values from 1 to 256, as said below
- w_out: bfloat16 [8192, 4096], P('node'), may hold values from -0.25 to 0.25
- w_gate: bfloat16 [32, 4096, 384], P('node'), may hold values from -0.09375 to 0.09375
- w_up: bfloat16 [32, 4096, 384], P('node'), may hold values from -0.09375 to 0.09375
- w_down: bfloat16 [32, 384, 4096], P('node'), may hold values from -0.21875 to 0.21875
- mlp_gain: float32 [4096], replicated, may hold values from 0.1 to 1.9
- expert_ids: int32 [128, 8], P(('groups', 'node')), may hold values from 0 to 15, all different within a row; in each aligned block of 4 rows (0 to 3, 4 to 7, ...) at most 2 rows name the same one
- route_weight: float32 [128, 8], P(('groups', 'node')), may hold values from 0.05 to 0.4
Outputs:
- attn_out: bfloat16 [128, 4096], P(('groups', 'node'))
- layer_out: bfloat16 [128, 4096], P(('groups', 'node'))
Inputs may be any that keep to these rules, and one draw needn't show every extreme that they name: `expert_ids`: each row names 8 different experts; within the rows of one device no expert is named more than 2 times, and exactly 2 times in some devices' rows. `lengths`: the largest value 256 is reached in every draw; positions at or past a row's length hold stale entries.
All inputs are finite; a program needn't handle non-finite values.
Results may differ from a plain program's by a relative error of at most 0.008.
Values may be sent and summed in bfloat16 or wider, within the bound.
No kernel may reach another device: no remote copies, remote signals or barrier semaphores. Data moves between devices by JAX's collectives and lax.ppermute only.
A program may use at most 64 MiB of HBM per device.

v0:
```python
import math

import jax
import jax.numpy as jnp
from jax import lax
from jax.sharding import PartitionSpec as P

HEAD = 128


def softmax_context(queries, new_kv, kv_cache, lengths):
    row_count = queries.shape[0]
    kv_width = new_kv.shape[2]
    kv_heads = kv_width // HEAD
    group_size = queries.shape[1] // kv_width
    cache_len = kv_cache.shape[2]
    query_grid = queries.reshape(row_count, kv_heads, group_size, HEAD)
    cache_keys = kv_cache[:, 0].reshape(row_count, cache_len, kv_heads, HEAD)
    cache_values = kv_cache[:, 1].reshape(row_count, cache_len, kv_heads, HEAD)
    fresh_key = new_kv[:, 0].reshape(row_count, kv_heads, HEAD)
    fresh_value = new_kv[:, 1].reshape(row_count, kv_heads, HEAD)
    score_scale = 1.0 / math.sqrt(HEAD)
    old_scores = (
        jnp.einsum("rkgd,rlkd->rkgl", query_grid, cache_keys, preferred_element_type=jnp.float32)
        * score_scale
    )
    new_scores = (
        jnp.einsum("rkgd,rkd->rkg", query_grid, fresh_key, preferred_element_type=jnp.float32)
        * score_scale
    )
    positions = lax.broadcasted_iota(jnp.int32, (row_count, cache_len), 1)
    valid_mask = (positions < lengths[:, None])[:, None, None, :]
    old_scores = jnp.where(valid_mask, old_scores, -jnp.inf)
    row_max = jnp.maximum(jnp.max(old_scores, axis=-1), new_scores)
    old_exp = jnp.exp(old_scores - row_max[..., None])
    new_exp = jnp.exp(new_scores - row_max)
    denom_sum = jnp.sum(old_exp, axis=-1) + new_exp
    old_probs = (old_exp / denom_sum[..., None]).astype(jnp.bfloat16)
    new_probs = (new_exp / denom_sum).astype(jnp.bfloat16)
    context = jnp.einsum(
        "rkgl,rlkd->rkgd", old_probs, cache_values, preferred_element_type=jnp.float32
    )
    context = (
        context
        + new_probs.astype(jnp.float32)[..., None] * fresh_value.astype(jnp.float32)[:, :, None, :]
    )
    return context.reshape(row_count, kv_heads * group_size * HEAD).astype(jnp.bfloat16)


def route_tables(expert_ids, route_weight, expert_count, capacity):
    row_count, top_count = expert_ids.shape
    pair_count = row_count * top_count
    flat_ids = expert_ids.reshape(pair_count)
    onehot = (
        flat_ids[:, None] == lax.broadcasted_iota(jnp.int32, (pair_count, expert_count), 1)
    ).astype(jnp.int32)
    running = jnp.cumsum(onehot, axis=0) - onehot
    slot_rank = jnp.sum(running * onehot, axis=1)
    target = flat_ids * capacity + slot_rank
    select = (
        lax.broadcasted_iota(jnp.int32, (expert_count * capacity, pair_count), 0) == target[None, :]
    )
    owner_map = lax.broadcasted_iota(
        jnp.int32, (pair_count, row_count), 0
    ) // top_count == lax.broadcasted_iota(jnp.int32, (pair_count, row_count), 1)
    gather_matrix = jnp.dot(
        select.astype(jnp.bfloat16),
        owner_map.astype(jnp.bfloat16),
        preferred_element_type=jnp.float32,
    ).astype(jnp.bfloat16)
    weighted_owner = owner_map.astype(jnp.float32).T * route_weight.reshape(pair_count)[None, :]
    combine_matrix = jnp.dot(
        weighted_owner, select.astype(jnp.float32).T, precision=lax.Precision.HIGHEST
    )
    return (gather_matrix, combine_matrix)


def expert_rows(rows_in, w_gate, w_up, w_down):
    gate_val = jnp.dot(rows_in, w_gate[0], preferred_element_type=jnp.float32)
    up_val = jnp.dot(rows_in, w_up[0], preferred_element_type=jnp.float32)
    activation = (jax.nn.silu(gate_val) * up_val).astype(jnp.bfloat16)
    return jnp.dot(activation, w_down[0], preferred_element_type=jnp.float32).astype(jnp.bfloat16)


def body(
    hidden_in,
    queries,
    new_kv,
    kv_cache,
    lengths,
    w_out,
    w_gate,
    w_up,
    w_down,
    mlp_gain,
    expert_ids,
    route_weight,
):
    device_count = lax.axis_size("node")
    row_count = hidden_in.shape[0]
    model_width = hidden_in.shape[1]
    context = softmax_context(queries, new_kv, kv_cache, lengths)
    head_rows = lax.all_to_all(context, "node", split_axis=1, concat_axis=0, tiled=True)
    attn_out = lax.psum_scatter(
        jnp.dot(head_rows, w_out, preferred_element_type=jnp.float32),
        "node",
        scatter_dimension=0,
        tiled=True,
    ).astype(jnp.bfloat16)
    mixed_state = hidden_in.astype(jnp.float32) + attn_out.astype(jnp.float32)
    mean_square = jnp.mean(mixed_state * mixed_state, axis=-1, keepdims=True)
    normed = (mixed_state * lax.rsqrt(mean_square + 1e-06) * mlp_gain[None, :]).astype(jnp.bfloat16)
    expert_count = device_count // 2
    top_count = expert_ids.shape[1]
    capacity = max(2, (row_count * top_count + expert_count - 1) // expert_count)
    gather_matrix, combine_matrix = route_tables(expert_ids, route_weight, expert_count, capacity)
    outgoing = jnp.dot(gather_matrix, normed, preferred_element_type=jnp.float32).astype(
        jnp.bfloat16
    )
    doubled = jnp.broadcast_to(
        outgoing.reshape(expert_count, 1, capacity, model_width),
        (expert_count, 2, capacity, model_width),
    )
    doubled = doubled.reshape(device_count, capacity, model_width)
    arrived = lax.all_to_all(doubled, "node", split_axis=0, concat_axis=0, tiled=True)
    partial_value = expert_rows(
        arrived.reshape(device_count * capacity, model_width), w_gate, w_up, w_down
    )
    partial_value = partial_value.reshape(device_count, capacity, model_width)
    returned = lax.all_to_all(partial_value, "node", split_axis=0, concat_axis=0, tiled=True)
    paired = returned.reshape(expert_count, 2, capacity, model_width).astype(jnp.float32)
    expert_out = (
        (paired[:, 0] + paired[:, 1])
        .astype(jnp.bfloat16)
        .reshape(expert_count * capacity, model_width)
    )
    moe_sum = jnp.dot(
        combine_matrix, expert_out.astype(jnp.float32), precision=lax.Precision.HIGHEST
    )
    layer_out = (mixed_state + moe_sum).astype(jnp.bfloat16)
    return (attn_out, layer_out)


def solution(mesh):
    return jax.shard_map(
        body,
        mesh=mesh,
        in_specs=(
            P(("groups", "node"), None),
            P(("groups", "node"), None),
            P(("groups", "node"), None, None),
            P(("groups", "node"), None, None, None),
            P(("groups", "node")),
            P("node", None),
            P("node", None, None),
            P("node", None, None),
            P("node", None, None),
            P(),
            P(("groups", "node"), None),
            P(("groups", "node"), None),
        ),
        out_specs=(P(("groups", "node"), None), P(("groups", "node"), None)),
        check_vma=False,
    )
```

profile of v0, /device:TPU:0, one launch (start us, length us, event | category | flops | bytes accessed | tf_op | source)
XLA Modules:
  0.0 147.3 jit_solution(6001131324011533973)
XLA Ops:
  0.7 3.2 %fusion.52 = (bf16[4,1,256,512]{3,2,1,0:T(8,128)(2,1)}, bf16[4,1,256,512]{3,2,1,0:T(8,128)(2,1)}) fusion(bf16[4,2,256,512]{3,2,1,0:T(8,128)(2,1)} %param.15), kind=kLoop, calls=%fused_computation.72 | loop fusion | bytes 4194304 | tf_op jit(solution)/shard_map/slice | solution.py:18
  3.9 2.3 %copy.28 = bf16[4,1,256,512]{2,3,0,1:T(8,128)(2,1)} copy(bf16[4,1,256,512]{3,2,1,0:T(8,128)(2,1)} %get-tuple-element.4) | data formatting | bytes 2097152
  6.3 0.1 fusion.30
  6.4 1.6 %fusion.53 = (f32[4,4,16]{2,1,0:T(4,128)S(1)}, f32[4,4,16,256]{3,2,1,0:T(8,128)S(1)}) fusion(bf16[4,4,16,128]{3,2,1,0:T(8,128)(2,1)S(1)} %bitcast.46, bf16[4,256,4,128]{1,3,2,0:T(8,128)(2,1)} %bitcast.42, pred[4,256]{1,0:T(4,128)(4,1)S(1)} %iota_compare_fusion.8), kind=kOutput, calls=%fused_computation.73 | convolution fusion | flops 16973568 | bytes 1378304 | tf_op jit(solution)/shard_map/rkgd,rlkd->rkgl/dot_general | solution.py:24
  8.0 0.2 fusion.17
  8.2 2.3 %copy.29 = bf16[4,1,256,512]{2,3,0,1:T(8,128)(2,1)} copy(bf16[4,1,256,512]{3,2,1,0:T(8,128)(2,1)} %get-tuple-element.5) | data formatting | bytes 2097152
  10.5 1.6 %fusion.7 = bf16[4,4,16,128]{3,2,1,0:T(8,128)(2,1)S(1)} fusion(bf16[4,256,4,128]{1,3,2,0:T(8,128)(2,1)} %bitcast.44, f32[4,4,16,256]{3,2,1,0:T(8,128)S(1)} %get-tuple-element.9, f32[4,4,16]{2,1,0:T(4,128)S(1)} %get-tuple-element.7, f32[4,4,16]{2,1,0:T(4,128)S(1)} %multiply_maximum_fusion, f32[4,4,128]{2,1,0:T(4,128)S(1)} %bitcast.51, ...), kind=kOutput, calls=%fused_computation.12 | convolution fusion | flops 17072128 | bytes 1387520 | tf_op jit(solution)/shard_map/rkgl,rlkd->rkgd/dot_general | solution.py:40
  12.2 0.7 copy.23
  12.9 7.3 %all-to-all-start = ((bf16[4,32,256]{2,0,1:T(4,128)(2,1)}), bf16[4,32,256]{2,0,1:T(4,128)(2,1)S(1)}, u32[]{:S(2)}, u32[]{:S(2)}) async-start(bf16[4,32,256]{2,0,1:T(4,128)(2,1)} %copy.23), calls=%async_computation | async-start | bytes 131072 | tf_op jit(solution)/shard_map/all_to_all | solution.py:103
  20.2 0.1 reshape.80
  20.3 0.1 fusion.28
  20.4 0.2 select_reduce_fusion
  20.6 7.0 %all-to-all-done = bf16[4,32,256]{2,0,1:T(4,128)(2,1)S(1)} async-done(((bf16[4,32,256]{2,0,1:T(4,128)(2,1)}), bf16[4,32,256]{2,0,1:T(4,128)(2,1)S(1)}, u32[]{:S(2)}, u32[]{:S(2)}) %all-to-all-start) | async-done | bytes 65568 | tf_op jit(solution)/shard_map/all_to_all | solution.py:103
  27.7 3.4 %fusion.54 = f32[128,4096]{1,0:T(8,128)} fusion(bf16[128,256]{1,0:T(8,128)(2,1)S(1)} %all_to_all.20, bf16[256,4096]{1,0:T(8,128)(2,1)} %param.17), kind=kOutput, calls=%fused_computation.74 | convolution fusion | flops 268435456 | bytes 4259840 | tf_op jit(solution)/shard_map/dot_general | solution.py:105
  31.0 59.1 %all-reduce.2 = bf16[128,4096]{1,0:T(8,128)(2,1)} all-reduce(f32[128,4096]{1,0:T(8,128)} %fusion.54), channel_id=2, replica_groups=mesh['groups'=1,'node'=32] {'node'}, use_global_device_ids=true, to_apply=%region_2.3.clone | all-reduce | flops 524288 | bytes 3145728
  90.2 1.0 multiply_reduce_fusion
  91.2 1.2 convolution_convert_fusion.1
  92.4 1.1 broadcast_in_dim.18
  93.5 0.5 broadcast_in_dim.19
  94.0 18.8 %all_to_all.26 = bf16[32,2,4096]{2,1,0:T(2,128)(2,1)} all-to-all(bf16[32,2,4096]{2,1,0:T(2,128)(2,1)S(1)} %bitcast.43), channel_id=1, replica_groups=mesh['groups'=1,'node'=32] {'node'}, dimensions={0} | all-to-all | bytes 1048576 | tf_op jit(solution)/shard_map/all_to_all | solution.py:125
  112.9 2.0 %reshape.82 = bf16[64,4096]{1,0:T(8,128)(2,1)} reshape(bf16[32,2,4096]{2,1,0:T(2,128)(2,1)} %all_to_all.26) | data formatting | bytes 1048576 | tf_op jit(solution)/shard_map/reshape | solution.py:127
  114.9 2.6 %fusion.4 = f32[64,384]{1,0:T(8,128)S(1)} fusion(bf16[64,4096]{1,0:T(8,128)(2,1)} %reshape.82, bf16[1,4096,384]{2,1,0:T(8,128)(2,1)} %param.18), kind=kOutput, calls=%fused_computation.7 | convolution fusion | flops 201326592 | bytes 3768320 | tf_op jit(solution)/shard_map/dot_general | solution.py:79
  117.5 4.4 %convolution_convert_fusion = bf16[64,4096]{1,0:T(8,128)(2,1)} fusion(bf16[1,384,4096]{2,1,0:T(8,128)(2,1)S(1)} %copy-done, bf16[64,4096]{1,0:T(8,128)(2,1)} %reshape.82, bf16[1,4096,384]{2,1,0:T(8,128)(2,1)} %param.19, f32[64,384]{1,0:T(8,128)S(1)} %fusion.4), kind=kOutput, calls=%fused_computation | convolution fusion | flops 403062784 | bytes 7438336 | tf_op jit(solution)/shard_map/dot_general | solution.py:82
  121.9 2.2 %reshape.83 = bf16[32,2,4096]{2,1,0:T(2,128)(2,1)} reshape(bf16[64,4096]{1,0:T(8,128)(2,1)} %convolution_convert_fusion) | data formatting | bytes 1048576 | tf_op jit(solution)/shard_map/reshape | solution.py:129
  124.1 3.3 %all-to-all-start.2 = ((bf16[32,2,4096]{2,1,0:T(2,128)(2,1)}), bf16[32,2,4096]{2,1,0:T(2,128)(2,1)}, u32[]{:S(2)}, u32[]{:S(2)}) async-start(bf16[32,2,4096]{2,1,0:T(2,128)(2,1)} %reshape.83), calls=%async_computation.2 | async-start | bytes 1048576 | tf_op jit(solution)/shard_map/all_to_all | solution.py:130
  127.4 0.1 mul.81
  127.5 0.1 fusion.29
  127.6 15.3 %all-to-all-done.2 = bf16[32,2,4096]{2,1,0:T(2,128)(2,1)} async-done(((bf16[32,2,4096]{2,1,0:T(2,128)(2,1)}), bf16[32,2,4096]{2,1,0:T(2,128)(2,1)}, u32[]{:S(2)}, u32[]{:S(2)}) %all-to-all-start.2) | async-done | bytes 524320 | tf_op jit(solution)/shard_map/all_to_all | solution.py:130
  143.0 1.5 %convert.2 = f32[16,2,2,4096]{3,2,1,0:T(2,128)S(1)} convert(bf16[16,2,2,4096]{3,2,1,0:T(2,128)(2,1)} %bitcast.12) | non-fusion elementwise | flops 262144 | bytes 1572864 | tf_op jit(solution)/shard_map/convert_element_type | solution.py:131
  144.4 0.3 fusion.16
  144.7 0.8 convert_element_type.94
  145.5 1.8 %fusion = bf16[4,4096]{1,0:T(4,128)(2,1)} fusion(f32[4,32]{1,0:T(4,128)S(1)} %fusion.29, bf16[32,4096]{1,0:T(8,128)(2,1)} %convert_element_type.94, bf16[4,4096]{1,0:T(4,128)(2,1)S(1)} %get-tuple-element.3, bf16[4,4096]{1,0:T(4,128)(2,1)S(1)} %copy-done.1), kind=kOutput, calls=%fused_computation.3 | convolution fusion | flops 6373376 | bytes 360960 | tf_op jit(solution)/shard_map/dot_general | solution.py:137
  (30 shorter events, 0.3 us)
Async XLA Ops:
  0.6 116.9 %copy-start = (bf16[1,384,4096]{2,1,0:T(8,128)(2,1)S(1)}, bf16[1,384,4096]{2,1,0:T(8,128)(2,1)}, u32[]{:S(2)}) copy-start(bf16[1,384,4096]{2,1,0:T(8,128)(2,1)} %param.20) | copy-start | bytes 9437188
  0.6 5.5 %copy-start.3 = (bf16[4,8192]{1,0:T(4,128)(2,1)S(1)}, bf16[4,8192]{1,0:T(4,128)(2,1)}, u32[]{:S(2)}) copy-start(bf16[4,8192]{1,0:T(4,128)(2,1)} %param.13) | copy-start | bytes 196612
  0.7 5.5 %copy-start.8 = (s32[4]{0:T(128)S(1)}, s32[4]{0:T(128)}, u32[]{:S(2)}) copy-start(s32[4]{0:T(128)} %param.16) | copy-start | bytes 52
  0.7 5.6 %copy-start.5 = (bf16[4,2,512]{2,1,0:T(2,128)(2,1)S(1)}, bf16[4,2,512]{2,1,0:T(2,128)(2,1)}, u32[]{:S(2)}) copy-start(bf16[4,2,512]{2,1,0:T(2,128)(2,1)} %param.14) | copy-start | bytes 24580
  6.2 14.0 %copy-start.6 = (s32[4,8]{1,0:T(4,128)S(1)}, s32[4,8]{1,0:T(4,128)}, u32[]{:S(2)}) copy-start(s32[4,8]{1,0:T(4,128)} %param.22) | copy-start | bytes 388
  12.9 14.7 %all-to-all-start = ((bf16[4,32,256]{2,0,1:T(4,128)(2,1)}), bf16[4,32,256]{2,0,1:T(4,128)(2,1)S(1)}, u32[]{:S(2)}, u32[]{:S(2)}) async-start(bf16[4,32,256]{2,0,1:T(4,128)(2,1)} %copy.23), calls=%async_computation | async-start | bytes 131072 | tf_op jit(solution)/shard_map/all_to_all | solution.py:103
  27.6 62.5 %copy-start.1 = (bf16[4,4096]{1,0:T(4,128)(2,1)S(1)}, bf16[4,4096]{1,0:T(4,128)(2,1)}, u32[]{:S(2)}) copy-start(bf16[4,4096]{1,0:T(4,128)(2,1)} %param.12) | copy-start | bytes 98308
  27.6 63.5 %copy-start.4 = (f32[4096]{0:T(1024)S(1)}, f32[4096]{0:T(1024)}, u32[]{:S(2)}) copy-start(f32[4096]{0:T(1024)} %param.21) | copy-start | bytes 49156
  91.2 54.4 %copy-start.2 = (bf16[4,4096]{1,0:T(4,128)(2,1)}, bf16[4,4096]{1,0:T(4,128)(2,1)S(1)}, u32[]{:S(2)}) copy-start(bf16[4,4096]{1,0:T(4,128)(2,1)S(1)} %get-tuple-element.3) | copy-start | bytes 98308
  117.5 9.9 %copy-start.7 = (f32[4,8]{1,0:T(4,128)S(1)}, f32[4,8]{1,0:T(4,128)}, u32[]{:S(2)}) copy-start(f32[4,8]{1,0:T(4,128)} %param.23) | copy-start | bytes 388
  124.1 18.9 %all-to-all-start.2 = ((bf16[32,2,4096]{2,1,0:T(2,128)(2,1)}), bf16[32,2,4096]{2,1,0:T(2,128)(2,1)}, u32[]{:S(2)}, u32[]{:S(2)}) async-start(bf16[32,2,4096]{2,1,0:T(2,128)(2,1)} %reshape.83), calls=%async_computation.2 | async-start | bytes 1048576 | tf_op jit(solution)/shard_map/all_to_all | solution.py:130
where the time goes:
time: 148 us; the launch traced here: 147 us
  blocking collectives  77.9 us (53%)
  waiting for transfers between devices  22.3 us (15%)
  matrix products  16.9 us (11%)
  local copies, waits for them, and re-layouts  15.3 us (10%)
  starting transfers between devices  10.6 us (7%)
  other arithmetic  3.41 us (2%)
    unnamed x1, blocking collectives  59.1 us
    all_to_all x1, blocking collectives, body(): lax.all_to_all(doubled, 'node', split_axis=0, concat_axis=0, tiled=True)  18.8 us
    all_to_all x1, waiting for transfers between devices, body(): lax.all_to_all(partial_value, 'node', split_axis=0, concat_axis=0, tiled=...  15.3 us
    all_to_all x1, starting transfers between devices, body(): lax.all_to_all(context, 'node', split_axis=1, concat_axis=0, tiled=True)  7.3 us
    all_to_all x1, waiting for transfers between devices, body(): lax.all_to_all(context, 'node', split_axis=1, concat_axis=0, tiled=True)  6.96 us
    unnamed x21, local copies, waits for them, and re-layouts  4.62 us
    dot_general x1, matrix products, expert_rows(): jnp.dot(activation, w_down[0], preferred_element_type=jnp.float32)  4.4 us
    dot_general x1, matrix products, body(): jnp.dot(head_rows, w_out, preferred_element_type=jnp.float32)  3.4 us
  transfers between devices with their start and end apart: 2, of which 2 were waited for; matrix products, arithmetic and copies ran while one was open for 0% of the time, Pallas kernels for 0%

commit v1 on v0

v1 whole, which is shorter than its diff:
```python
import functools
import math

import jax
import jax.numpy as jnp
from jax import lax
from jax.experimental import pallas as pl
from jax.experimental.pallas import tpu as pltpu
from jax.sharding import PartitionSpec as P

HEAD = 128
LANE = 128
F32 = jnp.float32
BF16 = jnp.bfloat16


def vmem_spec():
    return pl.BlockSpec(memory_space=pltpu.VMEM)


def smem_spec():
    return pl.BlockSpec(memory_space=pltpu.SMEM)


def attention_kernel(
    cap, q_ref, new_ref, kv_ref, len_ref, ids_ref, out_ref, slot_ref, place_ref, q32, ctx, count
):
    row = pl.program_id(0)
    rows, heads, _ = ctx.shape
    experts = slot_ref.shape[0] // cap
    cache_len = kv_ref.shape[2]
    kv_heads = kv_ref.shape[3] // HEAD
    group = heads // kv_heads

    @pl.when(row == 0)
    def _():
        for h in range(heads):
            q32[pl.ds(h, rows, stride=heads), :] = q_ref[:, h * HEAD : (h + 1) * HEAD].astype(F32)
        for e in range(experts):
            count[e] = 0
        for e in range(experts * cap):
            slot_ref[e] = 0

    for k in range(ids_ref.shape[1]):
        expert = ids_ref[row, k]
        slot = expert * cap + count[expert]
        count[expert] = count[expert] + 1
        slot_ref[slot] = row
        place_ref[row, k] = slot

    length = len_ref[row]
    scale = 1.0 / math.sqrt(HEAD)
    valid = lax.broadcasted_iota(jnp.int32, (group, cache_len), 1) < length
    for g in range(kv_heads):
        cols = slice(g * HEAD, (g + 1) * HEAD)
        query = q32[pl.ds(pl.multiple_of(row * heads, heads) + g * group, group), :]
        old = lax.dot_general(
            query.astype(BF16),
            kv_ref[0, 0, :, cols],
            (((1,), (1,)), ((), ())),
            preferred_element_type=F32,
        )
        old = jnp.where(valid, old * scale, -jnp.inf)
        fresh_key = new_ref[0, 0:1, cols].astype(F32)
        fresh_value = new_ref[0, 1:2, cols].astype(F32)
        new = jnp.sum(query * fresh_key, axis=1, keepdims=True) * scale
        top = jnp.maximum(jnp.max(old, axis=1, keepdims=True), new)
        old = jnp.exp(old - top)
        new = jnp.exp(new - top)
        denom = jnp.sum(old, axis=1, keepdims=True) + new
        probs = (old / denom).astype(BF16)
        new = (new / denom).astype(BF16).astype(F32)
        value = jnp.dot(probs, kv_ref[0, 1, :, cols], preferred_element_type=F32)
        ctx[row, g * group : (g + 1) * group, :] = value + new * fresh_value

    @pl.when(row == rows - 1)
    def _():
        chips = out_ref.shape[0] // 2
        each = heads // chips
        for i in range(chips):
            block = jnp.concatenate(
                [ctx[r, i * each : (i + 1) * each, :] for r in range(rows)], axis=0
            ).astype(BF16)
            out_ref[2 * i] = block
            out_ref[2 * i + 1] = block


def attention(queries, new_kv, kv_cache, lengths, expert_ids, devices, cap):
    rows = queries.shape[0]
    heads = queries.shape[1] // HEAD
    each = heads // (devices // 2)
    experts = devices // 2
    return pl.pallas_call(
        functools.partial(attention_kernel, cap),
        grid=(rows,),
        in_specs=[
            vmem_spec(),
            pl.BlockSpec((1,) + new_kv.shape[1:], lambda i: (i, 0, 0)),
            pl.BlockSpec((1,) + kv_cache.shape[1:], lambda i: (i, 0, 0, 0)),
            smem_spec(),
            smem_spec(),
        ],
        out_specs=[
            pl.BlockSpec((devices, rows * each, LANE), lambda i: (0, 0, 0)),
            smem_spec(),
            smem_spec(),
        ],
        out_shape=[
            jax.ShapeDtypeStruct((devices, rows * each, LANE), BF16),
            jax.ShapeDtypeStruct((experts * cap,), jnp.int32),
            jax.ShapeDtypeStruct(expert_ids.shape, jnp.int32),
        ],
        scratch_shapes=[
            pltpu.VMEM((rows * heads, LANE), F32),
            pltpu.VMEM((rows, heads, LANE), F32),
            pltpu.SMEM((experts,), jnp.int32),
        ],
        compiler_params=pltpu.CompilerParams(vmem_limit_bytes=12 << 20),
    )(queries, new_kv, kv_cache, lengths, expert_ids)


def project_kernel(core_ref, ctx_ref, own_ref, peer_ref, out_ref, x32, o32):
    devices, per, _ = ctx_ref.shape
    x32[...] = ctx_ref[...].reshape(devices * per, LANE).astype(F32)
    core = core_ref[0]
    held = own_ref.shape[0] // LANE
    each = 2 * held
    sums = o32.shape[0] * LANE // own_ref.shape[1]

    def part(first, w_ref):
        left = jnp.concatenate(
            [x32[pl.ds(first + j, sums, stride=each), :].astype(BF16) for j in range(held)],
            axis=1,
        )
        return jnp.dot(left, w_ref[...], preferred_element_type=F32)

    total = part(core * held, own_ref) + part((1 - core) * held, peer_ref)
    chunks = own_ref.shape[1] // LANE
    for t in range(chunks):
        o32[pl.ds(t, sums, stride=chunks), :] = total[:, t * LANE : (t + 1) * LANE]
    out_ref[:, 0] = o32[...].reshape(devices, o32.shape[0] // devices, LANE).astype(BF16)


def project(core, gathered, w_own, w_peer, tiles):
    devices, per, _ = gathered.shape
    held, width = w_own.shape
    each = 2 * held // LANE
    rows = per // each
    tile = width // 2 // tiles
    chunks = tile // LANE
    w_spec = pl.BlockSpec((held, tile), lambda i, core: (0, core[0] * tiles + i))
    return pl.pallas_call(
        project_kernel,
        grid_spec=pltpu.PrefetchScalarGridSpec(
            num_scalar_prefetch=1,
            grid=(tiles,),
            in_specs=[
                pl.BlockSpec((devices, per, LANE), lambda i, core: (0, 0, 0)),
                w_spec,
                w_spec,
            ],
            out_specs=pl.BlockSpec(
                (devices, 1, rows * chunks, LANE), lambda i, core: (0, i, 0, 0)
            ),
            scratch_shapes=[
                pltpu.VMEM((devices * per, LANE), F32),
                pltpu.VMEM((devices * rows * chunks, LANE), F32),
            ],
        ),
        out_shape=jax.ShapeDtypeStruct((devices, tiles, rows * chunks, LANE), BF16),
        compiler_params=pltpu.CompilerParams(vmem_limit_bytes=14 << 20),
    )(core, gathered, w_own, w_peer)


def norm_kernel(
    cap, slot_ref, sums_ref, hidden_ref, gain_ref, attn_ref, mixed_ref, out_ref, a32, h32, normed
):
    devices, tiles, per, _ = sums_ref.shape
    rows, width = hidden_ref.shape
    chunks = per // rows
    total = width // LANE
    half = total // 2
    for c in range(2):
        for i in range(tiles):
            acc = sums_ref[c, i].astype(F32)
            for k in range(1, devices // 2):
                acc = acc + sums_ref[2 * k + c, i].astype(F32)
            for r in range(rows):
                first = r * total + c * half + i * chunks
                a32[first : first + chunks, :] = acc[r * chunks : (r + 1) * chunks]
    for t in range(total):
        cols = slice(t * LANE, (t + 1) * LANE)
        h32[pl.ds(t, rows, stride=total), :] = hidden_ref[:, cols].astype(F32)
        attn_ref[:, cols] = a32[pl.ds(t, rows, stride=total), :].astype(BF16)
    for r in range(rows):
        span = slice(r * total, (r + 1) * total)
        mixed = h32[span, :] + a32[span, :].astype(BF16).astype(F32)
        mixed_ref[span, :] = mixed
        square = jnp.sum(jnp.sum(mixed * mixed, axis=0, keepdims=True), axis=1, keepdims=True)
        scaled = mixed * lax.rsqrt(square / width + 1e-06) * gain_ref[...]
        normed[2 * r] = scaled[:half].astype(BF16)
        normed[2 * r + 1] = scaled[half:].astype(BF16)
    for e in range(devices // 2):
        for s in range(cap):
            row = slot_ref[e * cap + s]
            for c in range(2):
                out_ref[2 * e + c, s * half : (s + 1) * half, :] = normed[2 * row + c]


def norm_dispatch(slot_rows, sums, hidden_in, mlp_gain, cap):
    devices = sums.shape[0]
    rows, width = hidden_in.shape
    total = width // LANE
    return pl.pallas_call(
        functools.partial(norm_kernel, cap),
        in_specs=[smem_spec(), vmem_spec(), vmem_spec(), vmem_spec()],
        out_specs=[vmem_spec(), vmem_spec(), vmem_spec()],
        out_shape=[
            jax.ShapeDtypeStruct((rows, width), BF16),
            jax.ShapeDtypeStruct((rows * total, LANE), F32),
            jax.ShapeDtypeStruct((devices, cap * total // 2, LANE), BF16),
        ],
        scratch_shapes=[
            pltpu.VMEM((rows * total, LANE), F32),
            pltpu.VMEM((rows * total, LANE), F32),
            pltpu.VMEM((2 * rows, total // 2, LANE), BF16),
        ],
        compiler_params=pltpu.CompilerParams(vmem_limit_bytes=6 << 20),
    )(slot_rows, sums, hidden_in, mlp_gain.reshape(total, LANE))


def expert_kernel(
    core_ref, own_ref, peer_ref, gate_ref, up_ref, down_ref, keep_ref, send_ref, x32, x16
):
    devices, per, _ = own_ref.shape
    core = core_ref[0]
    arrived = x16.shape[1]
    half = x16.shape[2] // LANE
    for index, ref in enumerate((own_ref, peer_ref)):
        x32[...] = ref[...].reshape(devices * per, LANE).astype(F32)
        for t in range(half):
            x16[index, :, t * LANE : (t + 1) * LANE] = x32[
                pl.ds(t, arrived, stride=half), :
            ].astype(BF16)
    depth = half * LANE
    mine = pl.ds(pl.multiple_of(core * depth, depth), depth)
    other = pl.ds(pl.multiple_of((1 - core) * depth, depth), depth)

    def both(w_ref):
        return jnp.dot(x16[0], w_ref[0, mine, :], preferred_element_type=F32) + jnp.dot(
            x16[1], w_ref[0, other, :], preferred_element_type=F32
        )

    gate = both(gate_ref)
    up = both(up_ref)
    act = (gate / (1.0 + jnp.exp(-gate)) * up).astype(BF16)
    for cols, ref in ((other, send_ref), (mine, keep_ref)):
        result = jnp.dot(act, down_ref[0, :, cols], preferred_element_type=F32)
        for t in range(half):
            x32[pl.ds(t, arrived, stride=half), :] = result[:, t * LANE : (t + 1) * LANE]
        ref[...] = x32[...].reshape(devices, per, LANE).astype(BF16)


def experts(core, own, peer, w_gate, w_up, w_down, cap):
    devices, per, _ = own.shape
    half = per // cap
    shape = jax.ShapeDtypeStruct(own.shape, BF16)
    return pl.pallas_call(
        expert_kernel,
        in_specs=[smem_spec()] + [vmem_spec()] * 5,
        out_specs=[vmem_spec()] * 2,
        out_shape=[shape, shape],
        scratch_shapes=[
            pltpu.VMEM((devices * per, LANE), F32),
            pltpu.VMEM((2, devices * cap, half * LANE), BF16),
        ],
        compiler_params=pltpu.CompilerParams(vmem_limit_bytes=24 << 20),
    )(core, own, peer, w_gate, w_up, w_down)


def combine_kernel(cap, place_ref, weight_ref, back_ref, mixed_ref, out_ref, total32):
    rows, width = out_ref.shape
    total = width // LANE
    half = total // 2
    for r in range(rows):
        for c in range(2):
            first = r * total + c * half
            acc = None
            for k in range(place_ref.shape[1]):
                place = place_ref[r, k]
                expert = place // cap
                slot = place - expert * cap
                term = weight_ref[r, k] * back_ref[(2 * expert + c) * cap + slot].astype(F32)
                acc = term if acc is None else acc + term
            total32[first : first + half, :] = mixed_ref[first : first + half, :] + acc
    for t in range(total):
        out_ref[:, t * LANE : (t + 1) * LANE] = total32[pl.ds(t, rows, stride=total), :].astype(
            BF16
        )


def combine(places, route_weight, back, mixed, rows, width, cap):
    return pl.pallas_call(
        functools.partial(combine_kernel, cap),
        in_specs=[smem_spec(), smem_spec(), vmem_spec(), vmem_spec()],
        out_specs=vmem_spec(),
        out_shape=jax.ShapeDtypeStruct((rows, width), BF16),
        scratch_shapes=[pltpu.VMEM(mixed.shape, F32)],
        compiler_params=pltpu.CompilerParams(vmem_limit_bytes=6 << 20),
    )(places, route_weight, back, mixed)


def body(
    hidden_in,
    queries,
    new_kv,
    kv_cache,
    lengths,
    w_out,
    w_gate,
    w_up,
    w_down,
    mlp_gain,
    expert_ids,
    route_weight,
):
    devices = lax.axis_size("node")
    rows, width = hidden_in.shape
    expert_count = devices // 2
    cap = max(2, -(-rows * expert_ids.shape[1] // expert_count))
    core = (lax.axis_index("node") % 2).astype(jnp.int32).reshape(1)
    pairs = [(i, i ^ 1) for i in range(devices)]

    def swap(array):
        return lax.ppermute(array, "node", pairs)

    def exchange(array):
        return lax.all_to_all(array, "node", split_axis=0, concat_axis=0, tiled=True)

    w_peer = swap(w_out)
    context, slot_rows, places = attention(
        queries, new_kv, kv_cache, lengths, expert_ids, devices, cap
    )
    gathered = exchange(context)
    sums = exchange(project(core, gathered, w_out, w_peer, 2))
    attn_out, mixed, outgoing = norm_dispatch(slot_rows, sums, hidden_in, mlp_gain, cap)
    arrived = exchange(outgoing)
    keep, send = experts(core, arrived, swap(arrived), w_gate, w_up, w_down, cap)
    paired = (keep.astype(F32) + swap(send).astype(F32)).astype(BF16)
    back = exchange(paired)
    back = back.reshape(devices * cap, width // 2 // LANE, LANE)
    layer_out = combine(places, route_weight, back, mixed, rows, width, cap)
    return (attn_out, layer_out)


def solution(mesh):
    rows = P(("groups", "node"), None)
    return jax.shard_map(
        body,
        mesh=mesh,
        in_specs=(
            rows,
            rows,
            P(("groups", "node"), None, None),
            P(("groups", "node"), None, None, None),
            P(("groups", "node")),
            P("node", None),
            P("node", None, None),
            P("node", None, None),
            P("node", None, None),
            P(),
            rows,
            rows,
        ),
        out_specs=(rows, rows),
        check_vma=False,
    )
```

time: 148 us -> 85.6 us (0.58)
  blocking collectives: 77.9 us -> 43.6 us
  matrix products: 16.9 us -> 0 us
  Pallas kernels: 0 us -> 14.4 us
  waiting for transfers between devices: 22.3 us -> 11.2 us
  local copies, waits for them, and re-layouts: 15.3 us -> 7.54 us
  other arithmetic: 3.41 us -> 0.07 us
  starting transfers between devices: 10.6 us -> 7.68 us
    unnamed x1 -> x0, blocking collectives: 59.1 us -> none
    all_to_all x1 -> x3, blocking collectives: 18.8 us -> 43.6 us  [exchange(): lax.all_to_all(array, 'node', split_axis=0, concat_axis=0, tiled=True)]
    dot_general x9 -> x0, matrix products: 16.9 us -> none  [the longest x1 4.4 us: expert_rows(): jnp.dot(activation, w_down[0], preferred_element_type=jnp.float32)]
    pallas_call x0 -> x5, Pallas kernels: none -> 14.4 us  [the longest x1 7.05 us: attention(): pl.pallas_call(functools.partial(attention_kernel, cap), grid=(rows,), in...]
    all_to_all x2 -> x1, waiting for transfers between devices: 22.3 us -> 8.22 us  [exchange(): lax.all_to_all(array, 'node', split_axis=0, concat_axis=0, tiled=True)]
    reshape x3 -> x0, local copies, waits for them, and re-layouts: 4.27 us -> none  [the longest x1 2.16 us: body(): partial_value = partial_value.reshape(device_count, capacity, model_width)]
    all_to_all x2 -> x1, starting transfers between devices: 10.6 us -> 6.97 us  [exchange(): lax.all_to_all(array, 'node', split_axis=0, concat_axis=0, tiled=True)]
    slice x1 -> x0, local copies, waits for them, and re-layouts: 3.2 us -> none  [softmax_context(): cache_keys = kv_cache[:, 0].reshape(row_count, cache_len, kv_heads, HEAD)]
  transfers between devices with their start and end apart: 2 -> 4, of which waited for: 2 -> 3; matrix products, arithmetic and copies ran while one was open for 0% -> 0% of each run, Pallas kernels for 0% -> 8%
where the time goes in v1:
time: 85.6 us; the launch traced here: 85.1 us
  blocking collectives  43.6 us (51%)
  Pallas kernels  14.4 us (17%)
  waiting for transfers between devices  11.2 us (13%)
  starting transfers between devices  7.68 us (9%)
  local copies, waits for them, and re-layouts  7.54 us (9%)
    all_to_all x3, blocking collectives, exchange(): lax.all_to_all(array, 'node', split_axis=0, concat_axis=0, tiled=True)  43.6 us
    all_to_all x1, waiting for transfers between devices, exchange(): lax.all_to_all(array, 'node', split_axis=0, concat_axis=0, tiled=True)  8.22 us
    unnamed x24, local copies, waits for them, and re-layouts  7.54 us
    pallas_call x1, Pallas kernels, attention(): pl.pallas_call(functools.partial(attention_kernel, cap), grid=(rows,), in...  7.05 us
    all_to_all x1, starting transfers between devices, exchange(): lax.all_to_all(array, 'node', split_axis=0, concat_axis=0, tiled=True)  6.97 us
    ppermute x3, waiting for transfers between devices, swap(): return lax.ppermute(array, 'node', pairs)  2.94 us
    pallas_call x1, Pallas kernels, experts(): pl.pallas_call(expert_kernel, in_specs=[smem_spec()] + [vmem_spec()] * 5,...  2.53 us
    pallas_call x1, Pallas kernels, project(): pl.pallas_call(project_kernel, grid_spec=pltpu.PrefetchScalarGridSpec(num...  2.01 us
  transfers between devices with their start and end apart: 4, of which 3 were waited for; matrix products, arithmetic and copies ran while one was open for 0% of the time, Pallas kernels for 8%

profile of v1, /device:TPU:0, one launch (start us, length us, event | category | flops | bytes accessed | tf_op | source)
XLA Modules:
  0.0 85.1 jit_solution(10933477054578948220)
XLA Ops:
  0.6 0.5 collective-permute-start
  1.1 0.0 copy-start.4
  1.2 1.6 %copy-done.4 = bf16[4,2,256,512]{3,2,1,0:T(8,128)(2,1)S(1)} copy-done((bf16[4,2,256,512]{3,2,1,0:T(8,128)(2,1)S(1)}, bf16[4,2,256,512]{3,2,1,0:T(8,128)(2,1)}, u32[]{:S(2)}) %copy-start.4) | copy-done | bytes 2097176
  2.7 0.0 copy-start.5
  2.7 0.8 copy-done.5
  3.6 0.0 copy-start.8
  3.6 0.7 copy-done.8
  4.3 0.7 copy-done.10
  5.0 0.7 copy-done.11
  5.6 7.1 %shard_map.131 = (bf16[32,16,128]{2,1,0:T(8,128)(2,1)}, s32[32]{0:T(128)S(1)}, s32[4,8]{1,0:T(4,128)S(1)}) custom-call(bf16[4,8192]{1,0:T(4,128)(2,1)S(1)} %copy-done.5, bf16[4,2,512]{2,1,0:T(2,128)(2,1)S(1)} %copy-done.8, bf16[4,2,256,512]{3,2,1,0:T(8,128)(2,1)S(1)} %copy-done.4, s32[4]{0:T(128)S(1)} %copy-done.11, s32[4,8]{1,0:T(4,128)S(1)} %copy-done.10), custom_call_target="tpu_custom_call" | custom-call | tf_op jit(solution)/shard_map/pallas_call | solution.py:93
  12.7 7.0 %all-to-all-start = ((bf16[32,16,128]{2,1,0:T(8,128)(2,1)}), bf16[32,16,128]{2,1,0:T(8,128)(2,1)S(1)}, u32[]{:S(2)}, u32[]{:S(2)}) async-start(bf16[32,16,128]{2,1,0:T(8,128)(2,1)} %get-tuple-element.11), calls=%async_computation | async-start | bytes 262144 | tf_op jit(solution)/shard_map/all_to_all | solution.py:338
  19.7 8.2 %all-to-all-done.ctx_ref = bf16[32,16,128]{2,1,0:T(8,128)(2,1)S(1)} async-done(((bf16[32,16,128]{2,1,0:T(8,128)(2,1)}), bf16[32,16,128]{2,1,0:T(8,128)(2,1)S(1)}, u32[]{:S(2)}, u32[]{:S(2)}) %all-to-all-start) | async-done | bytes 131104 | tf_op jit(solution)/shard_map/all_to_all | solution.py:338
  27.9 0.0 collective-permute-done.peer_ref
  27.9 1.6 %copy-done.3 = bf16[256,4096]{1,0:T(8,128)(2,1)S(1)} copy-done((bf16[256,4096]{1,0:T(8,128)(2,1)S(1)}, bf16[256,4096]{1,0:T(8,128)(2,1)}, u32[]{:S(2)}) %copy-start.3) | copy-done | bytes 2097176
  29.5 2.0 %shard_map.132 = bf16[32,2,32,128]{3,2,1,0:T(8,128)(2,1)S(1)} custom-call(s32[1]{0:T(128)} %bitcast.core_ref, bf16[32,16,128]{2,1,0:T(8,128)(2,1)S(1)} %all-to-all-done.ctx_ref, bf16[256,4096]{1,0:T(8,128)(2,1)S(1)} %copy-done.3, bf16[256,4096]{1,0:T(8,128)(2,1)} %collective-permute-done.peer_ref), custom_call_target="tpu_custom_call" | custom-call | tf_op jit(solution)/shard_map/pallas_call | solution.py:152
  31.5 17.4 %all_to_all.20.sums_ref = bf16[32,2,32,128]{3,2,1,0:T(8,128)(2,1)S(1)} all-to-all(bf16[32,2,32,128]{3,2,1,0:T(8,128)(2,1)S(1)} %shard_map.132), channel_id=1, replica_groups=mesh['groups'=1,'node'=32] {'node'}, dimensions={0} | all-to-all | bytes 1048576 | tf_op jit(solution)/shard_map/all_to_all | solution.py:338
  48.9 0.8 copy-done.6
  49.7 0.7 copy-done.7
  50.4 1.3 %shard_map.133 = (bf16[4,4096]{1,0:T(4,128)(2,1)}, f32[128,128]{1,0:T(8,128)S(1)}, bf16[32,32,128]{2,1,0:T(8,128)(2,1)S(1)}) custom-call(s32[32]{0:T(128)S(1)} %get-tuple-element.10.slot_ref, bf16[32,2,32,128]{3,2,1,0:T(8,128)(2,1)S(1)} %all_to_all.20.sums_ref, bf16[4,4096]{1,0:T(4,128)(2,1)S(1)} %copy-done.6, f32[32,128]{1,0:T(8,128)S(1)} %bitcast.4), custom_call_target="tpu_custom_call" | custom-call | tf_op jit(solution)/shard_map/pallas_call | solution.py:214
  51.7 13.4 %all_to_all.21.own_ref = bf16[32,32,128]{2,1,0:T(8,128)(2,1)S(1)} all-to-all(bf16[32,32,128]{2,1,0:T(8,128)(2,1)S(1)} %get-tuple-element.14), channel_id=1, replica_groups=mesh['groups'=1,'node'=32] {'node'}, dimensions={0} | all-to-all | bytes 524288 | tf_op jit(solution)/shard_map/all_to_all | solution.py:338
  65.1 0.0 collective-permute-start.1
  65.1 1.5 %collective-permute-done.1.peer_ref = bf16[32,32,128]{2,1,0:T(8,128)(2,1)S(1)} collective-permute-done((bf16[32,32,128]{2,1,0:T(8,128)(2,1)S(1)}, bf16[32,32,128]{2,1,0:T(8,128)(2,1)S(1)}, u32[]{:S(2)}, u32[]{:S(2)}) %collective-permute-start.1) | collective-permute-done | bytes 262176 | tf_op jit(solution)/shard_map/ppermute | solution.py:335
  66.6 0.0 copy-done.2
  66.6 0.0 copy-done
  66.6 0.0 copy-done.1
  66.6 2.5 %shard_map.134 = (bf16[32,32,128]{2,1,0:T(8,128)(2,1)S(1)}, bf16[32,32,128]{2,1,0:T(8,128)(2,1)S(1)}) custom-call(s32[1]{0:T(128)} %bitcast.core_ref, bf16[32,32,128]{2,1,0:T(8,128)(2,1)S(1)} %all_to_all.21.own_ref, bf16[32,32,128]{2,1,0:T(8,128)(2,1)S(1)} %collective-permute-done.1.peer_ref, bf16[1,4096,384]{2,1,0:T(8,128)(2,1)S(1)} %copy-done, ...), custom_call_target="tpu_custom_call" | custom-call | tf_op jit(solution)/shard_map/pallas_call | solution.py:268
  69.2 0.2 collective-permute-start.2
  69.4 1.4 %collective-permute-done.2 = bf16[32,32,128]{2,1,0:T(8,128)(2,1)S(1)} collective-permute-done((bf16[32,32,128]{2,1,0:T(8,128)(2,1)S(1)}, bf16[32,32,128]{2,1,0:T(8,128)(2,1)S(1)}, u32[]{:S(2)}, u32[]{:S(2)}) %collective-permute-start.2) | collective-permute-done | bytes 262176 | tf_op jit(solution)/shard_map/ppermute | solution.py:335
  70.8 0.1 add_convert_fusion
  70.9 12.8 %all_to_all.22 = bf16[32,32,128]{2,1,0:T(8,128)(2,1)S(1)} all-to-all(bf16[32,32,128]{2,1,0:T(8,128)(2,1)S(1)} %add_convert_fusion), channel_id=1, replica_groups=mesh['groups'=1,'node'=32] {'node'}, dimensions={0} | all-to-all | bytes 524288 | tf_op jit(solution)/shard_map/all_to_all | solution.py:338
  83.7 0.0 copy-done.9
  83.7 1.4 %shard_map.135 = bf16[4,4096]{1,0:T(4,128)(2,1)} custom-call(s32[4,8]{1,0:T(4,128)S(1)} %get-tuple-element.13.place_ref, f32[4,8]{1,0:T(4,128)S(1)} %copy-done.9, bf16[64,16,128]{2,1,0:T(8,128)(2,1)S(1)} %bitcast.3, f32[128,128]{1,0:T(8,128)S(1)} %get-tuple-element.17.mixed_ref), custom_call_target="tpu_custom_call" | custom-call | tf_op jit(solution)/shard_map/pallas_call | solution.py:303
  (9 shorter events, 0.0 us)
Async XLA Ops:
  0.6 27.3 %collective-permute-start = (bf16[256,4096]{1,0:T(8,128)(2,1)}, bf16[256,4096]{1,0:T(8,128)(2,1)}, u32[]{:S(2)}, u32[]{:S(2)}) collective-permute-start(bf16[256,4096]{1,0:T(8,128)(2,1)} %own_ref.1), channel_id=1, source_target_pairs={{0,1},{1,0},{2,3},{3,2},{4,5},{5,4},{6,7},{7,6},{8,9},{9,8},{10,11... | collective-permute-start | bytes 6291464 | tf_op jit(solution)/shard_map/ppermute | solution.py:335
  1.1 1.6 %copy-start.4 = (bf16[4,2,256,512]{3,2,1,0:T(8,128)(2,1)S(1)}, bf16[4,2,256,512]{3,2,1,0:T(8,128)(2,1)}, u32[]{:S(2)}) copy-start(bf16[4,2,256,512]{3,2,1,0:T(8,128)(2,1)} %kv_ref.1) | copy-start | bytes 6291460
  2.7 0.8 copy-start.5
  3.6 0.7 copy-start.8
  4.3 0.7 copy-start.10
  5.0 0.7 copy-start.11
  5.6 61.0 %copy-start.2 = (bf16[1,384,4096]{2,1,0:T(8,128)(2,1)S(1)}, bf16[1,384,4096]{2,1,0:T(8,128)(2,1)}, u32[]{:S(2)}) copy-start(bf16[1,384,4096]{2,1,0:T(8,128)(2,1)} %down_ref.1) | copy-start | bytes 9437188
  12.7 15.2 %all-to-all-start = ((bf16[32,16,128]{2,1,0:T(8,128)(2,1)}), bf16[32,16,128]{2,1,0:T(8,128)(2,1)S(1)}, u32[]{:S(2)}, u32[]{:S(2)}) async-start(bf16[32,16,128]{2,1,0:T(8,128)(2,1)} %get-tuple-element.11), calls=%async_computation | async-start | bytes 262144 | tf_op jit(solution)/shard_map/all_to_all | solution.py:338
  27.9 1.6 %copy-start.3 = (bf16[256,4096]{1,0:T(8,128)(2,1)S(1)}, bf16[256,4096]{1,0:T(8,128)(2,1)}, u32[]{:S(2)}) copy-start(bf16[256,4096]{1,0:T(8,128)(2,1)} %own_ref.1) | copy-start | bytes 6291460
  29.5 37.2 %copy-start = (bf16[1,4096,384]{2,1,0:T(8,128)(2,1)S(1)}, bf16[1,4096,384]{2,1,0:T(8,128)(2,1)}, u32[]{:S(2)}) copy-start(bf16[1,4096,384]{2,1,0:T(8,128)(2,1)} %gate_ref.1) | copy-start | bytes 9437188
  29.5 37.2 %copy-start.1 = (bf16[1,4096,384]{2,1,0:T(8,128)(2,1)S(1)}, bf16[1,4096,384]{2,1,0:T(8,128)(2,1)}, u32[]{:S(2)}) copy-start(bf16[1,4096,384]{2,1,0:T(8,128)(2,1)} %up_ref.1) | copy-start | bytes 9437188
  48.9 0.8 copy-start.6
  49.7 0.7 copy-start.7
  65.1 18.6 %copy-start.9 = (f32[4,8]{1,0:T(4,128)S(1)}, f32[4,8]{1,0:T(4,128)}, u32[]{:S(2)}) copy-start(f32[4,8]{1,0:T(4,128)} %weight_ref.1) | copy-start | bytes 388
  65.1 1.5 %collective-permute-start.1 = (bf16[32,32,128]{2,1,0:T(8,128)(2,1)S(1)}, bf16[32,32,128]{2,1,0:T(8,128)(2,1)S(1)}, u32[]{:S(2)}, u32[]{:S(2)}) collective-permute-start(bf16[32,32,128]{2,1,0:T(8,128)(2,1)S(1)} %all_to_all.21.own_ref), channel_id=1, source_target_pairs={{0,1},{1,0},{2,3},{3,2},{4,5},{5,4},{6,7},{7,6},{8,9},{9,8},{10,11... | collective-permute-start | bytes 786440 | tf_op jit(solution)/shard_map/ppermute | solution.py:335
  69.2 1.6 %collective-permute-start.2 = (bf16[32,32,128]{2,1,0:T(8,128)(2,1)S(1)}, bf16[32,32,128]{2,1,0:T(8,128)(2,1)S(1)}, u32[]{:S(2)}, u32[]{:S(2)}) collective-permute-start(bf16[32,32,128]{2,1,0:T(8,128)(2,1)S(1)} %get-tuple-element.16), channel_id=1, source_target_pairs={{0,1},{1,0},{2,3},{3,2},{4,5},{5,4},{6,7},{7,6},{8,9},{9,8},{10,11... | collective-permute-start | bytes 786440 | tf_op jit(solution)/shard_map/ppermute | solution.py:335

commit v2 on v1

--- a/solution.py
+++ b/solution.py
@@ -23,160 +23,247 @@
 
 
 def attention_kernel(
-    cap, q_ref, new_ref, kv_ref, len_ref, ids_ref, out_ref, slot_ref, place_ref, q32, ctx, count
+    cap,
+    core_ref,
+    q_hbm,
+    new_hbm,
+    kv_hbm,
+    len_hbm,
+    ids_hbm,
+    hidden_hbm,
+    gain_hbm,
+    w_hbm,
+    out_ref,
+    slot_ref,
+    place_ref,
+    h32_ref,
+    gain_ref,
+    keep_ref,
+    send_ref,
+    qv,
+    nv,
+    kv,
+    hv,
+    lens,
+    ids,
+    q32,
+    ctx,
+    count,
+    sems,
 ):
-    row = pl.program_id(0)
     rows, heads, _ = ctx.shape
     experts = slot_ref.shape[0] // cap
-    cache_len = kv_ref.shape[2]
-    kv_heads = kv_ref.shape[3] // HEAD
+    cache_len = kv.shape[2]
+    kv_heads = kv.shape[3] // HEAD
     group = heads // kv_heads
-
-    @pl.when(row == 0)
-    def _():
-        for h in range(heads):
-            q32[pl.ds(h, rows, stride=heads), :] = q_ref[:, h * HEAD : (h + 1) * HEAD].astype(F32)
-        for e in range(experts):
-            count[e] = 0
-        for e in range(experts * cap):
-            slot_ref[e] = 0
-
-    for k in range(ids_ref.shape[1]):
-        expert = ids_ref[row, k]
-        slot = expert * cap + count[expert]
-        count[expert] = count[expert] + 1
-        slot_ref[slot] = row
-        place_ref[row, k] = slot
-
-    length = len_ref[row]
+    core = core_ref[0]
+    half = w_hbm.shape[1] // 2
+    mine = pl.ds(pl.multiple_of(core * half, half), half)
+    other = pl.ds(pl.multiple_of((1 - core) * half, half), half)
+    pairs = [(ids_hbm, ids), (len_hbm, lens), (q_hbm, qv), (new_hbm, nv)]
+    pairs += [(kv_hbm.at[r], kv.at[r]) for r in range(rows)]
+    pairs += [(hidden_hbm, hv), (gain_hbm, gain_ref)]
+    pairs += [(w_hbm.at[:, other], send_ref), (w_hbm.at[:, mine], keep_ref)]
+    copies = [
+        pltpu.make_async_copy(source, target, sems.at[i])
+        for i, (source, target) in enumerate(pairs)
+    ]
+    for copy in copies:
+        copy.start()
+    copies[2].wait()
+    for h in range(heads):
+        q32[pl.ds(h, rows, stride=heads), :] = qv[:, h * HEAD : (h + 1) * HEAD].astype(F32)
+    copies[0].wait()
+    for e in range(experts):
+        count[e] = 0
+    for e in range(experts * cap):
+        slot_ref[e] = 0
+    for row in range(rows):
+        for k in range(ids.shape[1]):
+            expert = ids[row, k]
+            used = count[expert]
+            count[expert] = used + 1
+            slot_ref[expert * cap + used] = row
+            place_ref[row, k] = expert * cap + used
+    copies[1].wait()
+    copies[3].wait()
+
     scale = 1.0 / math.sqrt(HEAD)
-    valid = lax.broadcasted_iota(jnp.int32, (group, cache_len), 1) < length
-    for g in range(kv_heads):
-        cols = slice(g * HEAD, (g + 1) * HEAD)
-        query = q32[pl.ds(pl.multiple_of(row * heads, heads) + g * group, group), :]
-        old = lax.dot_general(
-            query.astype(BF16),
-            kv_ref[0, 0, :, cols],
-            (((1,), (1,)), ((), ())),
-            preferred_element_type=F32,
-        )
-        old = jnp.where(valid, old * scale, -jnp.inf)
-        fresh_key = new_ref[0, 0:1, cols].astype(F32)
-        fresh_value = new_ref[0, 1:2, cols].astype(F32)
-        new = jnp.sum(query * fresh_key, axis=1, keepdims=True) * scale
+    spot = lax.broadcasted_iota(jnp.int32, (heads, cache_len), 1)
+    batch = 2 if rows % 2 == 0 else 1
+    for start in range(0, rows, batch):
+        chosen = range(start, start + batch)
+        for r in chosen:
+            copies[4 + r].wait()
+        old, new, value, fresh = [], [], [], []
+        for r in chosen:
+            query = q32[r * heads : (r + 1) * heads, :]
+            parts, fresh_key, fresh_value = [], [], []
+            for g in range(kv_heads):
+                cols = slice(g * HEAD, (g + 1) * HEAD)
+                parts.append(
+                    lax.dot_general(
+                        query[g * group : (g + 1) * group].astype(BF16),
+                        kv[r, 0, :, cols],
+                        (((1,), (1,)), ((), ())),
+                        preferred_element_type=F32,
+                    )
+                )
+                fresh_key.append(jnp.broadcast_to(nv[r, 0:1, cols].astype(F32), (group, HEAD)))
+                fresh_value.append(jnp.broadcast_to(nv[r, 1:2, cols].astype(F32), (group, HEAD)))
+            scores = jnp.concatenate(parts, axis=0) * scale
+            old.append(jnp.where(spot < lens[r], scores, -jnp.inf))
+            new.append(
+                jnp.sum(query * jnp.concatenate(fresh_key, axis=0), axis=1, keepdims=True) * scale
+            )
+            fresh.append(jnp.concatenate(fresh_value, axis=0))
+        old = jnp.concatenate(old, axis=0)
+        new = jnp.concatenate(new, axis=0)
         top = jnp.maximum(jnp.max(old, axis=1, keepdims=True), new)
         old = jnp.exp(old - top)
         new = jnp.exp(new - top)
         denom = jnp.sum(old, axis=1, keepdims=True) + new
         probs = (old / denom).astype(BF16)
         new = (new / denom).astype(BF16).astype(F32)
-        value = jnp.dot(probs, kv_ref[0, 1, :, cols], preferred_element_type=F32)
-        ctx[row, g * group : (g + 1) * group, :] = value + new * fresh_value
-
-    @pl.when(row == rows - 1)
-    def _():
-        chips = out_ref.shape[0] // 2
-        each = heads // chips
-        for i in range(chips):
-            block = jnp.concatenate(
-                [ctx[r, i * each : (i + 1) * each, :] for r in range(rows)], axis=0
-            ).astype(BF16)
-            out_ref[2 * i] = block
-            out_ref[2 * i + 1] = block
-
-
-def attention(queries, new_kv, kv_cache, lengths, expert_ids, devices, cap):
-    rows = queries.shape[0]
+        for i, r in enumerate(chosen):
+            for g in range(kv_heads):
+                first = i * heads + g * group
+                value.append(
+                    jnp.dot(
+                        probs[first : first + group],
+                        kv[r, 1, :, g * HEAD : (g + 1) * HEAD],
+                        preferred_element_type=F32,
+                    )
+                )
+        result = jnp.concatenate(value, axis=0) + new * jnp.concatenate(fresh, axis=0)
+        for i, r in enumerate(chosen):
+            ctx[r] = result[i * heads : (i + 1) * heads]
+
+    chips = out_ref.shape[0] // 2
+    each = heads // chips
+    for i in range(chips):
+        block = jnp.concatenate(
+            [ctx[r, i * each : (i + 1) * each, :] for r in range(rows)], axis=0
+        ).astype(BF16)
+        out_ref[2 * i] = block
+        out_ref[2 * i + 1] = block
+    copies[4 + rows].wait()
+    total = h32_ref.shape[0] // rows
+    for t in range(total):
+        cols = slice(t * LANE, (t + 1) * LANE)
+        h32_ref[pl.ds(t, rows, stride=total), :] = hv[:, cols].astype(F32)
+    for copy in copies[5 + rows :]:
+        copy.wait()
+
+
+def attention(
+    core, queries, new_kv, kv_cache, lengths, expert_ids, hidden_in, gain, w_out, devices, cap
+):
+    rows, width = hidden_in.shape
     heads = queries.shape[1] // HEAD
     each = heads // (devices // 2)
     experts = devices // 2
+    half = jax.ShapeDtypeStruct((w_out.shape[0], width // 2), BF16)
     return pl.pallas_call(
         functools.partial(attention_kernel, cap),
-        grid=(rows,),
-        in_specs=[
-            vmem_spec(),
-            pl.BlockSpec((1,) + new_kv.shape[1:], lambda i: (i, 0, 0)),
-            pl.BlockSpec((1,) + kv_cache.shape[1:], lambda i: (i, 0, 0, 0)),
-            smem_spec(),
-            smem_spec(),
-        ],
-        out_specs=[
-            pl.BlockSpec((devices, rows * each, LANE), lambda i: (0, 0, 0)),
-            smem_spec(),
-            smem_spec(),
-        ],
+        in_specs=[smem_spec()] + [pl.BlockSpec(memory_space=pltpu.HBM)] * 8,
+        out_specs=[vmem_spec(), smem_spec(), smem_spec()] + [vmem_spec()] * 4,
         out_shape=[
             jax.ShapeDtypeStruct((devices, rows * each, LANE), BF16),
             jax.ShapeDtypeStruct((experts * cap,), jnp.int32),
             jax.ShapeDtypeStruct(expert_ids.shape, jnp.int32),
+            jax.ShapeDtypeStruct((rows * width // LANE, LANE), F32),
+            jax.ShapeDtypeStruct(gain.shape, F32),
+            half,
+            half,
         ],
         scratch_shapes=[
+            pltpu.VMEM(queries.shape, BF16),
+            pltpu.VMEM(new_kv.shape, BF16),
+            pltpu.VMEM(kv_cache.shape, BF16),
+            pltpu.VMEM(hidden_in.shape, BF16),
+            pltpu.SMEM(lengths.shape, jnp.int32),
+            pltpu.SMEM(expert_ids.shape, jnp.int32),
             pltpu.VMEM((rows * heads, LANE), F32),
             pltpu.VMEM((rows, heads, LANE), F32),
             pltpu.SMEM((experts,), jnp.int32),
+            pltpu.SemaphoreType.DMA((8 + rows,)),
         ],
         compiler_params=pltpu.CompilerParams(vmem_limit_bytes=12 << 20),
-    )(queries, new_kv, kv_cache, lengths, expert_ids)
+    )(
+        core,
+        *(
+            pltpu.with_memory_space_constraint(array, pltpu.HBM)
+            for array in (
+                queries,
+                new_kv,
+                kv_cache,
+                lengths,
+                expert_ids,
+                hidden_in,
+                gain,
+                w_out,
+            )
+        ),
+    )
 
 
 def project_kernel(core_ref, ctx_ref, own_ref, peer_ref, out_ref, x32, o32):
     devices, per, _ = ctx_ref.shape
     x32[...] = ctx_ref[...].reshape(devices * per, LANE).astype(F32)
     core = core_ref[0]
-    held = own_ref.shape[0] // LANE
-    each = 2 * held
-    sums = o32.shape[0] * LANE // own_ref.shape[1]
-
-    def part(first, w_ref):
-        left = jnp.concatenate(
-            [x32[pl.ds(first + j, sums, stride=each), :].astype(BF16) for j in range(held)],
+    held, width = own_ref.shape
+    each = 2 * held // LANE
+    chunks = width // LANE
+    sums = o32.shape[0] // chunks
+
+    def left(first):
+        return jnp.concatenate(
+            [
+                x32[pl.ds(first + j, sums, stride=each), :].astype(BF16)
+                for j in range(held // LANE)
+            ],
             axis=1,
         )
-        return jnp.dot(left, w_ref[...], preferred_element_type=F32)
-
-    total = part(core * held, own_ref) + part((1 - core) * held, peer_ref)
-    chunks = own_ref.shape[1] // LANE
-    for t in range(chunks):
-        o32[pl.ds(t, sums, stride=chunks), :] = total[:, t * LANE : (t + 1) * LANE]
+
+    own_left = left(core * (held // LANE))
+    peer_left = left((1 - core) * (held // LANE))
+    step = 512
+    for first in range(0, width, step):
+        cols = slice(first, first + step)
+        total = jnp.dot(own_left, own_ref[:, cols], preferred_element_type=F32) + jnp.dot(
+            peer_left, peer_ref[:, cols], preferred_element_type=F32
+        )
+        for t in range(step // LANE):
+            o32[pl.ds(first // LANE + t, sums, stride=chunks), :] = total[
+                :, t * LANE : (t + 1) * LANE
+            ]
     out_ref[:, 0] = o32[...].reshape(devices, o32.shape[0] // devices, LANE).astype(BF16)
 
 
-def project(core, gathered, w_own, w_peer, tiles):
+def project(core, gathered, w_own, w_peer):
     devices, per, _ = gathered.shape
     held, width = w_own.shape
-    each = 2 * held // LANE
-    rows = per // each
-    tile = width // 2 // tiles
-    chunks = tile // LANE
-    w_spec = pl.BlockSpec((held, tile), lambda i, core: (0, core[0] * tiles + i))
+    rows = per // (2 * held // LANE)
+    chunks = width // LANE
     return pl.pallas_call(
         project_kernel,
-        grid_spec=pltpu.PrefetchScalarGridSpec(
-            num_scalar_prefetch=1,
-            grid=(tiles,),
-            in_specs=[
-                pl.BlockSpec((devices, per, LANE), lambda i, core: (0, 0, 0)),
-                w_spec,
-                w_spec,
-            ],
-            out_specs=pl.BlockSpec(
-                (devices, 1, rows * chunks, LANE), lambda i, core: (0, i, 0, 0)
-            ),
-            scratch_shapes=[
-                pltpu.VMEM((devices * per, LANE), F32),
-                pltpu.VMEM((devices * rows * chunks, LANE), F32),
-            ],
-        ),
-        out_shape=jax.ShapeDtypeStruct((devices, tiles, rows * chunks, LANE), BF16),
-        compiler_params=pltpu.CompilerParams(vmem_limit_bytes=14 << 20),
+        in_specs=[smem_spec()] + [vmem_spec()] * 3,
+        out_specs=vmem_spec(),
+        out_shape=jax.ShapeDtypeStruct((devices, 1, rows * chunks, LANE), BF16),
+        scratch_shapes=[
+            pltpu.VMEM((devices * per, LANE), F32),
+            pltpu.VMEM((devices * rows * chunks, LANE), F32),
+        ],
+        compiler_params=pltpu.CompilerParams(vmem_limit_bytes=12 << 20),
     )(core, gathered, w_own, w_peer)
 
 
 def norm_kernel(
-    cap, slot_ref, sums_ref, hidden_ref, gain_ref, attn_ref, mixed_ref, out_ref, a32, h32, normed
+    cap, slot_ref, sums_ref, h32_ref, gain_ref, attn_ref, mixed_ref, out_ref, a32, normed
 ):
     devices, tiles, per, _ = sums_ref.shape
-    rows, width = hidden_ref.shape
+    rows, width = attn_ref.shape
     chunks = per // rows
     total = width // LANE
     half = total // 2
@@ -190,11 +277,10 @@
                 a32[first : first + chunks, :] = acc[r * chunks : (r + 1) * chunks]
     for t in range(total):
         cols = slice(t * LANE, (t + 1) * LANE)
-        h32[pl.ds(t, rows, stride=total), :] = hidden_ref[:, cols].astype(F32)
         attn_ref[:, cols] = a32[pl.ds(t, rows, stride=total), :].astype(BF16)
     for r in range(rows):
         span = slice(r * total, (r + 1) * total)
-        mixed = h32[span, :] + a32[span, :].astype(BF16).astype(F32)
+        mixed = h32_ref[span, :] + a32[span, :].astype(BF16).astype(F32)
         mixed_ref[span, :] = mixed
         square = jnp.sum(jnp.sum(mixed * mixed, axis=0, keepdims=True), axis=1, keepdims=True)
         scaled = mixed * lax.rsqrt(square / width + 1e-06) * gain_ref[...]
@@ -207,26 +293,24 @@
                 out_ref[2 * e + c, s * half : (s + 1) * half, :] = normed[2 * row + c]
 
 
-def norm_dispatch(slot_rows, sums, hidden_in, mlp_gain, cap):
+def norm_dispatch(slot_rows, sums, h32, gain, rows, cap):
     devices = sums.shape[0]
-    rows, width = hidden_in.shape
-    total = width // LANE
+    total = gain.shape[0]
     return pl.pallas_call(
         functools.partial(norm_kernel, cap),
         in_specs=[smem_spec(), vmem_spec(), vmem_spec(), vmem_spec()],
         out_specs=[vmem_spec(), vmem_spec(), vmem_spec()],
         out_shape=[
-            jax.ShapeDtypeStruct((rows, width), BF16),
+            jax.ShapeDtypeStruct((rows, total * LANE), BF16),
             jax.ShapeDtypeStruct((rows * total, LANE), F32),
             jax.ShapeDtypeStruct((devices, cap * total // 2, LANE), BF16),
         ],
         scratch_shapes=[
             pltpu.VMEM((rows * total, LANE), F32),
-            pltpu.VMEM((rows * total, LANE), F32),
             pltpu.VMEM((2 * rows, total // 2, LANE), BF16),
         ],
         compiler_params=pltpu.CompilerParams(vmem_limit_bytes=6 << 20),
-    )(slot_rows, sums, hidden_in, mlp_gain.reshape(total, LANE))
+    )(slot_rows, sums, h32, gain)
 
 
 def expert_kernel(
@@ -337,13 +421,24 @@
     def exchange(array):
         return lax.all_to_all(array, "node", split_axis=0, concat_axis=0, tiled=True)
 
-    w_peer = swap(w_out)
-    context, slot_rows, places = attention(
-        queries, new_kv, kv_cache, lengths, expert_ids, devices, cap
+    gain = mlp_gain.reshape(width // LANE, LANE)
+    context, slot_rows, places, h32, gain, w_keep, w_send = attention(
+        core,
+        queries,
+        new_kv,
+        kv_cache,
+        lengths,
+        expert_ids,
+        hidden_in,
+        gain,
+        w_out,
+        devices,
+        cap,
     )
+    w_peer = swap(w_send)
     gathered = exchange(context)
-    sums = exchange(project(core, gathered, w_out, w_peer, 2))
-    attn_out, mixed, outgoing = norm_dispatch(slot_rows, sums, hidden_in, mlp_gain, cap)
+    sums = exchange(project(core, gathered, w_keep, w_peer))
+    attn_out, mixed, outgoing = norm_dispatch(slot_rows, sums, h32, gain, rows, cap)
     arrived = exchange(outgoing)
     keep, send = experts(core, arrived, swap(arrived), w_gate, w_up, w_down, cap)
     paired = (keep.astype(F32) + swap(send).astype(F32)).astype(BF16)

time: 85.6 us -> 72.7 us (0.85)
  blocking collectives: 43.6 us -> 58.6 us
  waiting for transfers between devices: 11.2 us -> 2.95 us
  local copies, waits for them, and re-layouts: 7.54 us -> 0.02 us
  starting transfers between devices: 7.68 us -> 0.71 us
  Pallas kernels: 14.4 us -> 9.42 us
    all_to_all x3 -> x4, blocking collectives: 43.6 us -> 58.6 us  [exchange(): lax.all_to_all(array, 'node', split_axis=0, concat_axis=0, tiled=True)]
    all_to_all x1 -> x0, waiting for transfers between devices: 8.22 us -> none  [exchange(): lax.all_to_all(array, 'node', split_axis=0, concat_axis=0, tiled=True)]
    unnamed x24 -> x8, local copies, waits for them, and re-layouts: 7.54 us -> 0.02 us
    all_to_all x1 -> x0, starting transfers between devices: 6.97 us -> none  [exchange(): lax.all_to_all(array, 'node', split_axis=0, concat_axis=0, tiled=True)]
    pallas_call x2, Pallas kernels: 9.06 us -> 4.16 us  [the longest x1 3.55 us: attention(): pl.pallas_call(functools.partial(attention_kernel, cap), in_specs=[smem_s...]
  transfers between devices with their start and end apart: 4 -> 3, of which waited for: 3 -> 2; matrix products, arithmetic and copies ran while one was open for 0% -> 0% of each run, Pallas kernels for 8% -> 0%
where the time goes in v2:
time: 72.7 us; the launch traced here: 72.5 us
  blocking collectives  58.6 us (81%)
  Pallas kernels  9.42 us (13%)
  waiting for transfers between devices  2.95 us (4%)
    all_to_all x4, blocking collectives, exchange(): lax.all_to_all(array, 'node', split_axis=0, concat_axis=0, tiled=True)  58.6 us
    pallas_call x1, Pallas kernels, attention(): pl.pallas_call(functools.partial(attention_kernel, cap), in_specs=[smem_s...  3.55 us
    ppermute x3, waiting for transfers between devices, swap(): return lax.ppermute(array, 'node', pairs)  2.95 us
    pallas_call x1, Pallas kernels, experts(): pl.pallas_call(expert_kernel, in_specs=[smem_spec()] + [vmem_spec()] * 5,...  2.54 us
  transfers between devices with their start and end apart: 3, of which 2 were waited for; matrix products, arithmetic and copies ran while one was open for 0% of the time, Pallas kernels for 0%

profile of v2, /device:TPU:0, one launch (start us, length us, event | category | flops | bytes accessed | tf_op | source)
XLA Modules:
  0.0 72.5 jit_solution(17276824279391075704)
XLA Ops:
  0.6 0.0 copy-start.1
  0.7 0.0 copy-start.2
  0.7 3.6 %shard_map.131 = (bf16[32,16,128]{2,1,0:T(8,128)(2,1)S(1)}, s32[32]{0:T(128)S(1)}, s32[4,8]{1,0:T(4,128)S(1)}, f32[128,128]{1,0:T(8,128)S(1)}, f32[32,128]{1,0:T...) custom-call(s32[1]{0:T(128)} %bitcast.core_ref, bf16[4,8192]{1,0:T(4,128)(2,1)} %q_hbm.1, ...), custom_call_target="tpu_custom_call" | custom-call | tf_op jit(solution)/shard_map/pallas_call | solution.py:167
  4.2 0.0 copy-start
  4.2 0.5 collective-permute-start
  4.8 15.0 %all_to_all.20.ctx_ref = bf16[32,16,128]{2,1,0:T(8,128)(2,1)S(1)} all-to-all(bf16[32,16,128]{2,1,0:T(8,128)(2,1)S(1)} %get-tuple-element.15), channel_id=1, replica_groups=mesh['groups'=1,'node'=32] {'node'}, dimensions={0} | all-to-all | bytes 262144 | tf_op jit(solution)/shard_map/all_to_all | solution.py:422
  19.7 0.0 collective-permute-done.peer_ref
  19.7 0.6 shard_map.132
  20.4 17.3 %all_to_all.21.sums_ref = bf16[32,1,64,128]{3,2,1,0:T(8,128)(2,1)S(1)} all-to-all(bf16[32,1,64,128]{3,2,1,0:T(8,128)(2,1)S(1)} %shard_map.132), channel_id=1, replica_groups=mesh['groups'=1,'node'=32] {'node'}, dimensions={0} | all-to-all | bytes 1048576 | tf_op jit(solution)/shard_map/all_to_all | solution.py:422
  37.7 1.3 %shard_map.133 = (bf16[4,4096]{1,0:T(4,128)(2,1)}, f32[128,128]{1,0:T(8,128)S(1)}, bf16[32,32,128]{2,1,0:T(8,128)(2,1)S(1)}) custom-call(s32[32]{0:T(128)S(1)} %get-tuple-element.14.slot_ref, bf16[32,1,64,128]{3,2,1,0:T(8,128)(2,1)S(1)} %all_to_all.21.sums_ref, f32[128,128]{1,0:T(8,128)S(1)} %get-tuple-element.18.h32_ref, ...), custom_call_target="tpu_custom_call" | custom-call | tf_op jit(solution)/shard_map/pallas_call | solution.py:299
  39.0 13.5 %all_to_all.22.own_ref = bf16[32,32,128]{2,1,0:T(8,128)(2,1)S(1)} all-to-all(bf16[32,32,128]{2,1,0:T(8,128)(2,1)S(1)} %get-tuple-element.22), channel_id=1, replica_groups=mesh['groups'=1,'node'=32] {'node'}, dimensions={0} | all-to-all | bytes 524288 | tf_op jit(solution)/shard_map/all_to_all | solution.py:422
  52.4 0.0 copy-start.3
  52.4 0.0 collective-permute-start.1
  52.4 1.5 %collective-permute-done.1.peer_ref = bf16[32,32,128]{2,1,0:T(8,128)(2,1)S(1)} collective-permute-done((bf16[32,32,128]{2,1,0:T(8,128)(2,1)S(1)}, bf16[32,32,128]{2,1,0:T(8,128)(2,1)S(1)}, u32[]{:S(2)}, u32[]{:S(2)}) %collective-permute-start.1) | collective-permute-done | bytes 262176 | tf_op jit(solution)/shard_map/ppermute | solution.py:419
  54.0 0.0 copy-done.1
  54.0 0.0 copy-done.2
  54.0 0.0 copy-done
  54.0 2.5 %shard_map.134 = (bf16[32,32,128]{2,1,0:T(8,128)(2,1)S(1)}, bf16[32,32,128]{2,1,0:T(8,128)(2,1)S(1)}) custom-call(s32[1]{0:T(128)} %bitcast.core_ref, bf16[32,32,128]{2,1,0:T(8,128)(2,1)S(1)} %all_to_all.22.own_ref, bf16[32,32,128]{2,1,0:T(8,128)(2,1)S(1)} %collective-permute-done.1.peer_ref, bf16[1,4096,384]{2,1,0:T(8,128)(2,1)S(1)} %copy-done, ...), custom_call_target="tpu_custom_call" | custom-call | tf_op jit(solution)/shard_map/pallas_call | solution.py:352
  56.5 0.2 collective-permute-start.2
  56.7 1.4 %collective-permute-done.2 = bf16[32,32,128]{2,1,0:T(8,128)(2,1)S(1)} collective-permute-done((bf16[32,32,128]{2,1,0:T(8,128)(2,1)S(1)}, bf16[32,32,128]{2,1,0:T(8,128)(2,1)S(1)}, u32[]{:S(2)}, u32[]{:S(2)}) %collective-permute-start.2) | collective-permute-done | bytes 262176 | tf_op jit(solution)/shard_map/ppermute | solution.py:419
  58.1 0.1 add_convert_fusion
  58.2 12.8 %all_to_all.23 = bf16[32,32,128]{2,1,0:T(8,128)(2,1)S(1)} all-to-all(bf16[32,32,128]{2,1,0:T(8,128)(2,1)S(1)} %add_convert_fusion), channel_id=1, replica_groups=mesh['groups'=1,'node'=32] {'node'}, dimensions={0} | all-to-all | bytes 524288 | tf_op jit(solution)/shard_map/all_to_all | solution.py:422
  71.0 0.0 copy-done.3
  71.0 1.4 %shard_map.135 = bf16[4,4096]{1,0:T(4,128)(2,1)} custom-call(s32[4,8]{1,0:T(4,128)S(1)} %get-tuple-element.21.place_ref, f32[4,8]{1,0:T(4,128)S(1)} %copy-done.3, bf16[64,16,128]{2,1,0:T(8,128)(2,1)S(1)} %bitcast.3, f32[128,128]{1,0:T(8,128)S(1)} %get-tuple-element.25.mixed_ref), custom_call_target="tpu_custom_call" | custom-call | tf_op jit(solution)/shard_map/pallas_call | solution.py:387
Async XLA Ops:
  0.6 53.3 %copy-start.1 = (bf16[1,4096,384]{2,1,0:T(8,128)(2,1)S(1)}, bf16[1,4096,384]{2,1,0:T(8,128)(2,1)}, u32[]{:S(2)}) copy-start(bf16[1,4096,384]{2,1,0:T(8,128)(2,1)} %up_ref.1) | copy-start | bytes 9437188
  0.7 53.3 %copy-start.2 = (bf16[1,384,4096]{2,1,0:T(8,128)(2,1)S(1)}, bf16[1,384,4096]{2,1,0:T(8,128)(2,1)}, u32[]{:S(2)}) copy-start(bf16[1,384,4096]{2,1,0:T(8,128)(2,1)} %down_ref.1) | copy-start | bytes 9437188
  4.2 49.8 %copy-start = (bf16[1,4096,384]{2,1,0:T(8,128)(2,1)S(1)}, bf16[1,4096,384]{2,1,0:T(8,128)(2,1)}, u32[]{:S(2)}) copy-start(bf16[1,4096,384]{2,1,0:T(8,128)(2,1)} %gate_ref.1) | copy-start | bytes 9437188
  4.2 15.5 %collective-permute-start = (bf16[256,2048]{1,0:T(8,128)(2,1)S(1)}, bf16[256,2048]{1,0:T(8,128)(2,1)S(1)}, u32[]{:S(2)}, u32[]{:S(2)}) collective-permute-start(bf16[256,2048]{1,0:T(8,128)(2,1)S(1)} %get-tuple-element.17), channel_id=1, source_target_pairs={{0,1},{1,0},{2,3},{3,2},{4,5},{5,4},{6,7},{7,6},{8,9},{9,8},{10,11... | collective-permute-start | bytes 3145736 | tf_op jit(solution)/shard_map/ppermute | solution.py:419
  52.4 18.6 %copy-start.3 = (f32[4,8]{1,0:T(4,128)S(1)}, f32[4,8]{1,0:T(4,128)}, u32[]{:S(2)}) copy-start(f32[4,8]{1,0:T(4,128)} %weight_ref.1) | copy-start | bytes 388
  52.4 1.5 %collective-permute-start.1 = (bf16[32,32,128]{2,1,0:T(8,128)(2,1)S(1)}, bf16[32,32,128]{2,1,0:T(8,128)(2,1)S(1)}, u32[]{:S(2)}, u32[]{:S(2)}) collective-permute-start(bf16[32,32,128]{2,1,0:T(8,128)(2,1)S(1)} %all_to_all.22.own_ref), channel_id=1, source_target_pairs={{0,1},{1,0},{2,3},{3,2},{4,5},{5,4},{6,7},{7,6},{8,9},{9,8},{10,11... | collective-permute-start | bytes 786440 | tf_op jit(solution)/shard_map/ppermute | solution.py:419
  56.5 1.6 %collective-permute-start.2 = (bf16[32,32,128]{2,1,0:T(8,128)(2,1)S(1)}, bf16[32,32,128]{2,1,0:T(8,128)(2,1)S(1)}, u32[]{:S(2)}, u32[]{:S(2)}) collective-permute-start(bf16[32,32,128]{2,1,0:T(8,128)(2,1)S(1)} %get-tuple-element.24), channel_id=1, source_target_pairs={{0,1},{1,0},{2,3},{3,2},{4,5},{5,4},{6,7},{7,6},{8,9},{9,8},{10,11... | collective-permute-start | bytes 786440 | tf_op jit(solution)/shard_map/ppermute | solution.py:419

commit v3 on v2

v3 whole, which is shorter than its diff:
```python
import functools
import math

import jax
import jax.numpy as jnp
from jax import lax
from jax.experimental import pallas as pl
from jax.experimental.pallas import tpu as pltpu
from jax.sharding import PartitionSpec as P

HEAD = 128
LANE = 128
F32 = jnp.float32
BF16 = jnp.bfloat16


def vmem_spec():
    return pl.BlockSpec(memory_space=pltpu.VMEM)


def attention_kernel(
    cap,
    q_hbm,
    new_hbm,
    kv_hbm,
    len_hbm,
    ids_hbm,
    route_hbm,
    hidden_hbm,
    gain_hbm,
    w_hbm,
    out_ref,
    weight_ref,
    pick_ref,
    h32_ref,
    gain_ref,
    keep_ref,
    send_ref,
    qv,
    nv,
    kv,
    hv,
    lens,
    ids,
    route,
    q32,
    ctx,
    count,
    sems,
):
    rows, heads, _ = ctx.shape
    slots = weight_ref.shape[0] // rows
    cache_len = kv.shape[2]
    kv_heads = kv.shape[3] // HEAD
    group = heads // kv_heads
    core = lax.axis_index("node") % 2
    half = w_hbm.shape[1] // 2
    mine = pl.ds(pl.multiple_of(core * half, half), half)
    other = pl.ds(pl.multiple_of((1 - core) * half, half), half)
    pairs = [(ids_hbm, ids), (len_hbm, lens), (q_hbm, qv), (new_hbm, nv)]
    pairs += [(kv_hbm.at[r], kv.at[r]) for r in range(rows)]
    pairs += [(hidden_hbm, hv), (gain_hbm, gain_ref), (route_hbm, route)]
    pairs += [(w_hbm.at[:, other], send_ref), (w_hbm.at[:, mine], keep_ref)]
    copies = [
        pltpu.make_async_copy(source, target, sems.at[i])
        for i, (source, target) in enumerate(pairs)
    ]
    for copy in copies:
        copy.start()
    copies[2].wait()
    for h in range(heads):
        q32[pl.ds(h, rows, stride=heads), :] = qv[:, h * HEAD : (h + 1) * HEAD].astype(F32)
    weight_ref[...] = jnp.zeros(weight_ref.shape, F32)
    pick_ref[...] = jnp.zeros(pick_ref.shape, F32)
    for e in range(slots // cap):
        count[e] = 0
    copies[0].wait()
    copies[6 + rows].wait()
    for row in range(rows):
        for k in range(ids.shape[1]):
            expert = ids[row, k]
            used = count[expert]
            count[expert] = used + 1
            slot = expert * cap + used
            weight_ref[pl.ds(row * slots + slot, 1), :] = jnp.full((1, LANE), route[row, k], F32)
            pick_ref[pl.ds(slot * rows + row, 1), :] = jnp.ones((1, LANE), F32)
    copies[1].wait()
    copies[3].wait()

    scale = 1.0 / math.sqrt(HEAD)
    spot = lax.broadcasted_iota(jnp.int32, (heads, cache_len), 1)
    batch = 2 if rows % 2 == 0 else 1
    for start in range(0, rows, batch):
        chosen = range(start, start + batch)
        for r in chosen:
            copies[4 + r].wait()
        old, new, value, fresh = [], [], [], []
        for r in chosen:
            query = q32[r * heads : (r + 1) * heads, :]
            parts, fresh_key, fresh_value = [], [], []
            for g in range(kv_heads):
                cols = slice(g * HEAD, (g + 1) * HEAD)
                parts.append(
                    lax.dot_general(
                        query[g * group : (g + 1) * group].astype(BF16),
                        kv[r, 0, :, cols],
                        (((1,), (1,)), ((), ())),
                        preferred_element_type=F32,
                    )
                )
                fresh_key.append(jnp.broadcast_to(nv[r, 0:1, cols].astype(F32), (group, HEAD)))
                fresh_value.append(jnp.broadcast_to(nv[r, 1:2, cols].astype(F32), (group, HEAD)))
            scores = jnp.concatenate(parts, axis=0) * scale
            old.append(jnp.where(spot < lens[r], scores, -jnp.inf))
            new.append(
                jnp.sum(query * jnp.concatenate(fresh_key, axis=0), axis=1, keepdims=True) * scale
            )
            fresh.append(jnp.concatenate(fresh_value, axis=0))
        old = jnp.concatenate(old, axis=0)
        new = jnp.concatenate(new, axis=0)
        top = jnp.maximum(jnp.max(old, axis=1, keepdims=True), new)
        old = jnp.exp(old - top)
        new = jnp.exp(new - top)
        denom = jnp.sum(old, axis=1, keepdims=True) + new
        probs = (old / denom).astype(BF16)
        new = (new / denom).astype(BF16).astype(F32)
        for i, r in enumerate(chosen):
            for g in range(kv_heads):
                first = i * heads + g * group
                value.append(
                    jnp.dot(
                        probs[first : first + group],
                        kv[r, 1, :, g * HEAD : (g + 1) * HEAD],
                        preferred_element_type=F32,
                    )
                )
        result = jnp.concatenate(value, axis=0) + new * jnp.concatenate(fresh, axis=0)
        for i, r in enumerate(chosen):
            ctx[r] = result[i * heads : (i + 1) * heads]

    chips = out_ref.shape[0] // 2
    each = heads // chips
    for i in range(chips):
        block = jnp.concatenate(
            [ctx[r, i * each : (i + 1) * each, :] for r in range(rows)], axis=0
        ).astype(BF16)
        out_ref[2 * i] = block
        out_ref[2 * i + 1] = block
    copies[4 + rows].wait()
    total = h32_ref.shape[0] // rows
    for t in range(total):
        cols = slice(t * LANE, (t + 1) * LANE)
        h32_ref[pl.ds(t, rows, stride=total), :] = hv[:, cols].astype(F32)
    copies[5 + rows].wait()
    for copy in copies[7 + rows :]:
        copy.wait()


def attention(
    queries, new_kv, kv_cache, lengths, expert_ids, route_weight, hidden_in, gain, w_out, devices, cap
):
    rows, width = hidden_in.shape
    heads = queries.shape[1] // HEAD
    each = heads // (devices // 2)
    experts = devices // 2
    half = jax.ShapeDtypeStruct((w_out.shape[0], width // 2), BF16)
    table = jax.ShapeDtypeStruct((rows * experts * cap, LANE), F32)
    arrays = (
        queries,
        new_kv,
        kv_cache,
        lengths,
        expert_ids,
        route_weight,
        hidden_in,
        gain,
        w_out,
    )
    return pl.pallas_call(
        functools.partial(attention_kernel, cap),
        in_specs=[pl.BlockSpec(memory_space=pltpu.HBM)] * len(arrays),
        out_specs=[vmem_spec()] * 7,
        out_shape=[
            jax.ShapeDtypeStruct((devices, rows * each, LANE), BF16),
            table,
            table,
            jax.ShapeDtypeStruct((rows * width // LANE, LANE), F32),
            jax.ShapeDtypeStruct(gain.shape, F32),
            half,
            half,
        ],
        scratch_shapes=[
            pltpu.VMEM(queries.shape, BF16),
            pltpu.VMEM(new_kv.shape, BF16),
            pltpu.VMEM(kv_cache.shape, BF16),
            pltpu.VMEM(hidden_in.shape, BF16),
            pltpu.SMEM(lengths.shape, jnp.int32),
            pltpu.SMEM(expert_ids.shape, jnp.int32),
            pltpu.SMEM(route_weight.shape, F32),
            pltpu.VMEM((rows * heads, LANE), F32),
            pltpu.VMEM((rows, heads, LANE), F32),
            pltpu.SMEM((experts,), jnp.int32),
            pltpu.SemaphoreType.DMA((9 + rows,)),
        ],
        compiler_params=pltpu.CompilerParams(vmem_limit_bytes=12 << 20),
    )(*(pltpu.with_memory_space_constraint(array, pltpu.HBM) for array in arrays))


def project_kernel(ctx_ref, own_ref, peer_ref, out_ref, x32, o32):
    devices, per, _ = ctx_ref.shape
    x32[...] = ctx_ref[...].reshape(devices * per, LANE).astype(F32)
    core = lax.axis_index("node") % 2
    held, width = own_ref.shape
    each = 2 * held // LANE
    chunks = width // LANE
    sums = o32.shape[0] // chunks

    def left(first):
        return jnp.concatenate(
            [
                x32[pl.ds(first + j, sums, stride=each), :].astype(BF16)
                for j in range(held // LANE)
            ],
            axis=1,
        )

    own_left = left(core * (held // LANE))
    peer_left = left((1 - core) * (held // LANE))
    step = 512
    for first in range(0, width, step):
        cols = slice(first, first + step)
        total = jnp.dot(own_left, own_ref[:, cols], preferred_element_type=F32) + jnp.dot(
            peer_left, peer_ref[:, cols], preferred_element_type=F32
        )
        for t in range(step // LANE):
            o32[pl.ds(first // LANE + t, sums, stride=chunks), :] = total[
                :, t * LANE : (t + 1) * LANE
            ]
    out_ref[:, 0] = o32[...].reshape(devices, o32.shape[0] // devices, LANE).astype(BF16)


def project(gathered, w_own, w_peer):
    devices, per, _ = gathered.shape
    held, width = w_own.shape
    rows = per // (2 * held // LANE)
    chunks = width // LANE
    return pl.pallas_call(
        project_kernel,
        in_specs=[vmem_spec()] * 3,
        out_specs=vmem_spec(),
        out_shape=jax.ShapeDtypeStruct((devices, 1, rows * chunks, LANE), BF16),
        scratch_shapes=[
            pltpu.VMEM((devices * per, LANE), F32),
            pltpu.VMEM((devices * rows * chunks, LANE), F32),
        ],
        compiler_params=pltpu.CompilerParams(vmem_limit_bytes=12 << 20),
    )(gathered, w_own, w_peer)


def norm_kernel(cap, sums_ref, h32_ref, gain_ref, pick_ref, attn_ref, mixed_ref, out_ref):
    devices, tiles, per, _ = sums_ref.shape
    total = gain_ref.shape[0]
    rows = h32_ref.shape[0] // total
    half = total // 2
    for c in range(2):
        acc = sums_ref[c, 0].astype(F32)
        for k in range(1, devices // 2):
            acc = acc + sums_ref[2 * k + c, 0].astype(F32)
        for r in range(rows):
            attn_ref[r * total + c * half : r * total + (c + 1) * half, :] = acc[
                r * half : (r + 1) * half
            ]
    normed = []
    for r in range(rows):
        span = slice(r * total, (r + 1) * total)
        mixed = h32_ref[span, :] + attn_ref[span, :].astype(BF16).astype(F32)
        mixed_ref[span, :] = mixed
        square = jnp.sum(jnp.sum(mixed * mixed, axis=0, keepdims=True), axis=1, keepdims=True)
        scaled = mixed * lax.rsqrt(square / width_of(total) + 1e-06) * gain_ref[...]
        normed.append(scaled)
    for slot in range(devices // 2 * cap):
        e, s = divmod(slot, cap)
        chosen = normed[0] * pick_ref[slot * rows : slot * rows + 1, :]
        for r in range(1, rows):
            chosen = chosen + normed[r] * pick_ref[slot * rows + r : slot * rows + r + 1, :]
        chosen = chosen.astype(BF16)
        for c in range(2):
            out_ref[2 * e + c, s * half : (s + 1) * half, :] = chosen[c * half : (c + 1) * half]


def width_of(chunks):
    return chunks * LANE


def norm_dispatch(sums, h32, gain, pick, cap):
    devices = sums.shape[0]
    total = gain.shape[0]
    state = jax.ShapeDtypeStruct(h32.shape, F32)
    return pl.pallas_call(
        functools.partial(norm_kernel, cap),
        in_specs=[vmem_spec()] * 4,
        out_specs=[vmem_spec()] * 3,
        out_shape=[
            state,
            state,
            jax.ShapeDtypeStruct((devices, cap * total // 2, LANE), BF16),
        ],
        compiler_params=pltpu.CompilerParams(vmem_limit_bytes=6 << 20),
    )(sums, h32, gain, pick)


def rows_from_chunks(ref, x32, x16):
    devices, per, _ = ref.shape
    arrived, width = x16.shape
    half = width // LANE
    x32[...] = ref[...].reshape(devices * per, LANE).astype(F32)
    for t in range(half):
        x16[:, t * LANE : (t + 1) * LANE] = x32[pl.ds(t, arrived, stride=half), :].astype(BF16)


def chunks_from_rows(result, x32, ref):
    arrived, width = result.shape
    half = width // LANE
    for t in range(half):
        x32[pl.ds(t, arrived, stride=half), :] = result[:, t * LANE : (t + 1) * LANE]
    ref[...] = x32[...].reshape(ref.shape).astype(BF16)


def half_of(which, size):
    return pl.ds(pl.multiple_of(which * size, size), size)


def own_kernel(own_ref, gate_ref, up_ref, gate_out, up_out, x32, x16):
    rows_from_chunks(own_ref, x32, x16)
    span = half_of(lax.axis_index("node") % 2, x16.shape[1])
    gate_out[...] = jnp.dot(x16[...], gate_ref[0, span, :], preferred_element_type=F32)
    up_out[...] = jnp.dot(x16[...], up_ref[0, span, :], preferred_element_type=F32)


def peer_kernel(
    peer_ref, gate_in, up_in, gate_ref, up_ref, down_ref, act_ref, send_ref, x32, x16
):
    rows_from_chunks(peer_ref, x32, x16)
    span = half_of(1 - lax.axis_index("node") % 2, x16.shape[1])
    gate = gate_in[...] + jnp.dot(x16[...], gate_ref[0, span, :], preferred_element_type=F32)
    up = up_in[...] + jnp.dot(x16[...], up_ref[0, span, :], preferred_element_type=F32)
    act = (gate / (1.0 + jnp.exp(-gate)) * up).astype(BF16)
    act_ref[...] = act
    result = jnp.dot(act, down_ref[0, :, span], preferred_element_type=F32)
    chunks_from_rows(result, x32, send_ref)


def keep_kernel(act_ref, down_ref, keep_ref, x32):
    size = down_ref.shape[2] // 2
    span = half_of(lax.axis_index("node") % 2, size)
    result = jnp.dot(act_ref[...], down_ref[0, :, span], preferred_element_type=F32)
    chunks_from_rows(result, x32, keep_ref)


def estimate(flops, moved):
    return pl.CostEstimate(flops=flops, bytes_accessed=moved, transcendentals=0)


def experts(own, swap, w_gate, w_up, w_down, cap):
    devices, per, _ = own.shape
    half = per // cap * LANE
    arrived = devices * cap
    hidden = w_gate.shape[2]
    chunked = jax.ShapeDtypeStruct(own.shape, BF16)
    sums = jax.ShapeDtypeStruct((arrived, hidden), F32)
    wide = pltpu.VMEM((devices * per, LANE), F32)
    narrow = pltpu.VMEM((arrived, half), BF16)
    params = pltpu.CompilerParams(vmem_limit_bytes=8 << 20)
    peer = swap(own)
    gate, up = pl.pallas_call(
        own_kernel,
        in_specs=[vmem_spec()] * 3,
        out_specs=[vmem_spec()] * 2,
        out_shape=[sums, sums],
        scratch_shapes=[wide, narrow],
        compiler_params=params,
        cost_estimate=estimate(4 * arrived * half * hidden, 4 * half * hidden),
    )(own, w_gate, w_up)
    act, send = pl.pallas_call(
        peer_kernel,
        in_specs=[vmem_spec()] * 6,
        out_specs=[vmem_spec()] * 2,
        out_shape=[jax.ShapeDtypeStruct((arrived, hidden), BF16), chunked],
        scratch_shapes=[wide, narrow],
        compiler_params=params,
        cost_estimate=estimate(6 * arrived * half * hidden, 6 * half * hidden),
    )(peer, gate, up, w_gate, w_up, w_down)
    received = swap(send)
    keep = pl.pallas_call(
        keep_kernel,
        in_specs=[vmem_spec()] * 2,
        out_specs=vmem_spec(),
        out_shape=chunked,
        scratch_shapes=[wide],
        compiler_params=params,
        cost_estimate=estimate(2 * arrived * half * hidden, 2 * half * hidden),
    )(act, w_down)
    return (keep.astype(F32) + received.astype(F32)).astype(BF16)


def combine_kernel(cap, weight_ref, back_ref, mixed_ref, a32_ref, attn_ref, out_ref, total32):
    rows, width = out_ref.shape
    total = width // LANE
    half = total // 2
    slots = weight_ref.shape[0] // rows
    for t in range(total):
        cols = slice(t * LANE, (t + 1) * LANE)
        attn_ref[:, cols] = a32_ref[pl.ds(t, rows, stride=total), :].astype(BF16)
    for c in range(2):
        acc = [
            mixed_ref[r * total + c * half : r * total + (c + 1) * half, :] for r in range(rows)
        ]
        for slot in range(slots):
            e, s = divmod(slot, cap)
            block = back_ref[2 * e + c, s * half : (s + 1) * half, :].astype(F32)
            for r in range(rows):
                acc[r] = acc[r] + weight_ref[r * slots + slot : r * slots + slot + 1, :] * block
        for r in range(rows):
            total32[r * total + c * half : r * total + (c + 1) * half, :] = acc[r]
    for t in range(total):
        out_ref[:, t * LANE : (t + 1) * LANE] = total32[pl.ds(t, rows, stride=total), :].astype(
            BF16
        )


def combine(weights, back, mixed, a32, rows, width, cap):
    shape = jax.ShapeDtypeStruct((rows, width), BF16)
    return pl.pallas_call(
        functools.partial(combine_kernel, cap),
        in_specs=[vmem_spec()] * 4,
        out_specs=[vmem_spec()] * 2,
        out_shape=[shape, shape],
        scratch_shapes=[pltpu.VMEM(mixed.shape, F32)],
        compiler_params=pltpu.CompilerParams(vmem_limit_bytes=6 << 20),
    )(weights, back, mixed, a32)


def body(
    hidden_in,
    queries,
    new_kv,
    kv_cache,
    lengths,
    w_out,
    w_gate,
    w_up,
    w_down,
    mlp_gain,
    expert_ids,
    route_weight,
):
    devices = lax.axis_size("node")
    rows, width = hidden_in.shape
    expert_count = devices // 2
    cap = max(2, -(-rows * expert_ids.shape[1] // expert_count))
    pairs = [(i, i ^ 1) for i in range(devices)]

    def swap(array):
        return lax.ppermute(array, "node", pairs)

    def exchange(array):
        return lax.all_to_all(array, "node", split_axis=0, concat_axis=0, tiled=True)

    gain = mlp_gain.reshape(width // LANE, LANE)
    context, weights, pick, h32, gain, w_keep, w_send = attention(
        queries,
        new_kv,
        kv_cache,
        lengths,
        expert_ids,
        route_weight,
        hidden_in,
        gain,
        w_out,
        devices,
        cap,
    )
    w_peer = swap(w_send)
    gathered = exchange(context)
    sums = exchange(project(gathered, w_keep, w_peer))
    a32, mixed, outgoing = norm_dispatch(sums, h32, gain, pick, cap)
    arrived = exchange(outgoing)
    back = exchange(experts(arrived, swap, w_gate, w_up, w_down, cap))
    return combine(weights, back, mixed, a32, rows, width, cap)


def solution(mesh):
    rows = P(("groups", "node"), None)
    return jax.shard_map(
        body,
        mesh=mesh,
        in_specs=(
            rows,
            rows,
            P(("groups", "node"), None, None),
            P(("groups", "node"), None, None, None),
            P(("groups", "node")),
            P("node", None),
            P("node", None, None),
            P("node", None, None),
            P("node", None, None),
            P(),
            rows,
            rows,
        ),
        out_specs=(rows, rows),
        check_vma=False,
    )
```

time: 72.7 us -> 69.4 us (0.955)
  Pallas kernels: 9.42 us -> 7.1 us
  waiting for transfers between devices: 2.95 us -> 1.79 us
    pallas_call x5 -> x7, Pallas kernels: 9.42 us -> 7.1 us  [the longest x1 2.94 us: attention(): pl.pallas_call(functools.partial(attention_kernel, cap), in_specs=[pl.Blo...]
    ppermute x3, waiting for transfers between devices: 2.95 us -> 1.79 us  [swap(): return lax.ppermute(array, 'node', pairs)]
  transfers between devices with their start and end apart: 3 -> 3, of which waited for: 2 -> 2; matrix products, arithmetic and copies ran while one was open for 0% -> 0% of each run, Pallas kernels for 0% -> 2%
where the time goes in v3:
time: 69.4 us; the launch traced here: 69.2 us
  blocking collectives  58.6 us (84%)
  Pallas kernels  7.1 us (10%)
  waiting for transfers between devices  1.79 us (3%)
  between operations  0.72 us (1%)
    all_to_all x4, blocking collectives, exchange(): lax.all_to_all(array, 'node', split_axis=0, concat_axis=0, tiled=True)  58.6 us
    pallas_call x1, Pallas kernels, attention(): pl.pallas_call(functools.partial(attention_kernel, cap), in_specs=[pl.Blo...  2.94 us
    ppermute x3, waiting for transfers between devices, swap(): return lax.ppermute(array, 'node', pairs)  1.79 us
  transfers between devices with their start and end apart: 3, of which 2 were waited for; matrix products, arithmetic and copies ran while one was open for 0% of the time, Pallas kernels for 2%

profile of v3, /device:TPU:0, one launch (start us, length us, event | category | flops | bytes accessed | tf_op | source)
XLA Modules:
  0.0 69.2 jit_solution(3283764866622827363)
XLA Ops:
  0.6 0.0 copy-start.1
  0.6 2.9 %shard_map.131 = (bf16[32,16,128]{2,1,0:T(8,128)(2,1)S(1)}, f32[128,128]{1,0:T(8,128)S(1)}, f32[128,128]{1,0:T(8,128)S(1)}, f32[128,128]{1,0:T(8,128)S(1)}, f32[...) custom-call(bf16[4,8192]{1,0:T(4,128)(2,1)} %q_hbm.1, bf16[4,2,512]{2,1,0:T(2,128)(2,1)} %new_hbm.1, ...), custom_call_target="tpu_custom_call" | custom-call | tf_op jit(solution)/shard_map/pallas_call | solution.py:179
  3.6 0.0 copy-start
  3.6 0.5 collective-permute-start
  4.1 15.0 %all_to_all.20.ctx_ref = bf16[32,16,128]{2,1,0:T(8,128)(2,1)S(1)} all-to-all(bf16[32,16,128]{2,1,0:T(8,128)(2,1)S(1)} %get-tuple-element.17), channel_id=1, replica_groups=mesh['groups'=1,'node'=32] {'node'}, dimensions={0} | all-to-all | bytes 262144 | tf_op jit(solution)/shard_map/all_to_all | solution.py:467
  19.1 0.0 collective-permute-done.peer_ref
  19.1 0.6 shard_map.132
  19.7 17.3 %all_to_all.21.sums_ref = bf16[32,1,64,128]{3,2,1,0:T(8,128)(2,1)S(1)} all-to-all(bf16[32,1,64,128]{3,2,1,0:T(8,128)(2,1)S(1)} %shard_map.132), channel_id=1, replica_groups=mesh['groups'=1,'node'=32] {'node'}, dimensions={0} | all-to-all | bytes 1048576 | tf_op jit(solution)/shard_map/all_to_all | solution.py:467
  37.0 0.3 shard_map.133
  37.3 13.5 %all_to_all.22.own_ref = bf16[32,32,128]{2,1,0:T(8,128)(2,1)S(1)} all-to-all(bf16[32,32,128]{2,1,0:T(8,128)(2,1)S(1)} %get-tuple-element.23), channel_id=1, replica_groups=mesh['groups'=1,'node'=32] {'node'}, dimensions={0} | all-to-all | bytes 524288 | tf_op jit(solution)/shard_map/all_to_all | solution.py:467
  50.8 0.0 copy-start.2
  50.8 0.0 collective-permute-start.1
  50.8 0.0 copy-done.1
  50.8 0.0 copy-done
  50.8 0.8 %shard_map.134 = (f32[64,384]{1,0:T(8,128)S(1)}, f32[64,384]{1,0:T(8,128)S(1)}) custom-call(bf16[32,32,128]{2,1,0:T(8,128)(2,1)S(1)} %all_to_all.22.own_ref, bf16[1,4096,384]{2,1,0:T(8,128)(2,1)S(1)} %copy-done, bf16[1,4096,384]{2,1,0:T(8,128)(2,1)S(1)} %copy-done.1), custom_call_target="tpu_custom_call" | custom-call | flops 201326592 | bytes 3145728 | tf_op jit(solution)/shard_map/pallas_call | solution.py:375
  51.6 0.7 %collective-permute-done.1.peer_ref = bf16[32,32,128]{2,1,0:T(8,128)(2,1)S(1)} collective-permute-done((bf16[32,32,128]{2,1,0:T(8,128)(2,1)S(1)}, bf16[32,32,128]{2,1,0:T(8,128)(2,1)S(1)}, u32[]{:S(2)}, u32[]{:S(2)}) %collective-permute-start.1) | collective-permute-done | bytes 262176 | tf_op jit(solution)/shard_map/ppermute | solution.py:464
  52.3 0.4 copy-done.2
  52.7 1.2 %shard_map.135 = (bf16[64,384]{1,0:T(8,128)(2,1)S(1)}, bf16[32,32,128]{2,1,0:T(8,128)(2,1)S(1)}) custom-call(bf16[32,32,128]{2,1,0:T(8,128)(2,1)S(1)} %collective-permute-done.1.peer_ref, f32[64,384]{1,0:T(8,128)S(1)} %get-tuple-element.24.gate_in, f32[64,384]{1,0:T(8,128)S(1)} %get-tuple-element.25.up_in, bf16[1,4096,384]{2,1,0:T(8,128)(2,1)S(1)} %copy-done, ...), custom_call_target="tpu_custom_call" | custom-call | flops 301989888 | bytes 4718592 | tf_op jit(solution)/shard_map/pallas_call | solution.py:384
  53.9 0.1 collective-permute-start.2
  54.0 0.5 shard_map.136
  54.4 1.1 %collective-permute-done.2 = bf16[32,32,128]{2,1,0:T(8,128)(2,1)S(1)} collective-permute-done((bf16[32,32,128]{2,1,0:T(8,128)(2,1)S(1)}, bf16[32,32,128]{2,1,0:T(8,128)(2,1)S(1)}, u32[]{:S(2)}, u32[]{:S(2)}) %collective-permute-start.2) | collective-permute-done | bytes 262176 | tf_op jit(solution)/shard_map/ppermute | solution.py:464
  55.5 0.1 add_convert_fusion
  55.6 12.8 %all_to_all.23.back_ref = bf16[32,32,128]{2,1,0:T(8,128)(2,1)S(1)} all-to-all(bf16[32,32,128]{2,1,0:T(8,128)(2,1)S(1)} %add_convert_fusion), channel_id=1, replica_groups=mesh['groups'=1,'node'=32] {'node'}, dimensions={0} | all-to-all | bytes 524288 | tf_op jit(solution)/shard_map/all_to_all | solution.py:467
  68.4 0.8 %shard_map.137 = (bf16[4,4096]{1,0:T(4,128)(2,1)}, bf16[4,4096]{1,0:T(4,128)(2,1)}) custom-call(f32[128,128]{1,0:T(8,128)S(1)} %get-tuple-element.16.weight_ref, bf16[32,32,128]{2,1,0:T(8,128)(2,1)S(1)} %all_to_all.23.back_ref, f32[128,128]{1,0:T(8,128)S(1)} %get-tuple-element.28.mixed_ref, f32[128,128]{1,0:T(8,128)S(1)} %get-tuple-element.29.a32_ref), custom_call_target="tpu_custom_call" | custom-call | tf_op jit(solution)/shard_map/pallas_call | solution.py:433
Async XLA Ops:
  0.6 50.2 %copy-start.1 = (bf16[1,4096,384]{2,1,0:T(8,128)(2,1)S(1)}, bf16[1,4096,384]{2,1,0:T(8,128)(2,1)}, u32[]{:S(2)}) copy-start(bf16[1,4096,384]{2,1,0:T(8,128)(2,1)} %up_ref.3) | copy-start | bytes 9437188
  3.6 47.2 %copy-start = (bf16[1,4096,384]{2,1,0:T(8,128)(2,1)S(1)}, bf16[1,4096,384]{2,1,0:T(8,128)(2,1)}, u32[]{:S(2)}) copy-start(bf16[1,4096,384]{2,1,0:T(8,128)(2,1)} %gate_ref.3) | copy-start | bytes 9437188
  3.6 15.5 %collective-permute-start = (bf16[256,2048]{1,0:T(8,128)(2,1)S(1)}, bf16[256,2048]{1,0:T(8,128)(2,1)S(1)}, u32[]{:S(2)}, u32[]{:S(2)}) collective-permute-start(bf16[256,2048]{1,0:T(8,128)(2,1)S(1)} %get-tuple-element.19), channel_id=1, source_target_pairs={{0,1},{1,0},{2,3},{3,2},{4,5},{5,4},{6,7},{7,6},{8,9},{9,8},{10,11... | collective-permute-start | bytes 3145736 | tf_op jit(solution)/shard_map/ppermute | solution.py:464
  50.8 1.9 %copy-start.2 = (bf16[1,384,4096]{2,1,0:T(8,128)(2,1)S(1)}, bf16[1,384,4096]{2,1,0:T(8,128)(2,1)}, u32[]{:S(2)}) copy-start(bf16[1,384,4096]{2,1,0:T(8,128)(2,1)} %down_ref.3) | copy-start | bytes 9437188
  50.8 1.5 %collective-permute-start.1 = (bf16[32,32,128]{2,1,0:T(8,128)(2,1)S(1)}, bf16[32,32,128]{2,1,0:T(8,128)(2,1)S(1)}, u32[]{:S(2)}, u32[]{:S(2)}) collective-permute-start(bf16[32,32,128]{2,1,0:T(8,128)(2,1)S(1)} %all_to_all.22.own_ref), channel_id=1, source_target_pairs={{0,1},{1,0},{2,3},{3,2},{4,5},{5,4},{6,7},{7,6},{8,9},{9,8},{10,11... | collective-permute-start | bytes 786440 | tf_op jit(solution)/shard_map/ppermute | solution.py:464
  53.9 1.6 %collective-permute-start.2 = (bf16[32,32,128]{2,1,0:T(8,128)(2,1)S(1)}, bf16[32,32,128]{2,1,0:T(8,128)(2,1)S(1)}, u32[]{:S(2)}, u32[]{:S(2)}) collective-permute-start(bf16[32,32,128]{2,1,0:T(8,128)(2,1)S(1)} %get-tuple-element.27), channel_id=1, source_target_pairs={{0,1},{1,0},{2,3},{3,2},{4,5},{5,4},{6,7},{7,6},{8,9},{9,8},{10,11... | collective-permute-start | bytes 786440 | tf_op jit(solution)/shard_map/ppermute | solution.py:464

commit v4 on v3

--- a/solution.py
+++ b/solution.py
@@ -35,7 +35,6 @@
     h32_ref,
     gain_ref,
     keep_ref,
-    send_ref,
     qv,
     nv,
     kv,
@@ -56,18 +55,19 @@
     core = lax.axis_index("node") % 2
     half = w_hbm.shape[1] // 2
     mine = pl.ds(pl.multiple_of(core * half, half), half)
-    other = pl.ds(pl.multiple_of((1 - core) * half, half), half)
     pairs = [(ids_hbm, ids), (len_hbm, lens), (q_hbm, qv), (new_hbm, nv)]
     pairs += [(kv_hbm.at[r], kv.at[r]) for r in range(rows)]
     pairs += [(hidden_hbm, hv), (gain_hbm, gain_ref), (route_hbm, route)]
-    pairs += [(w_hbm.at[:, other], send_ref), (w_hbm.at[:, mine], keep_ref)]
+    pairs += [(w_hbm.at[:, mine], keep_ref)]
     copies = [
         pltpu.make_async_copy(source, target, sems.at[i])
         for i, (source, target) in enumerate(pairs)
     ]
-    for copy in copies:
+    for copy in copies[: 7 + rows]:
         copy.start()
     copies[2].wait()
+    for copy in copies[7 + rows :]:
+        copy.start()
     for h in range(heads):
         q32[pl.ds(h, rows, stride=heads), :] = qv[:, h * HEAD : (h + 1) * HEAD].astype(F32)
     weight_ref[...] = jnp.zeros(weight_ref.shape, F32)
@@ -89,7 +89,7 @@
 
     scale = 1.0 / math.sqrt(HEAD)
     spot = lax.broadcasted_iota(jnp.int32, (heads, cache_len), 1)
-    batch = 2 if rows % 2 == 0 else 1
+    batch = rows
     for start in range(0, rows, batch):
         chosen = range(start, start + batch)
         for r in chosen:
@@ -121,9 +121,9 @@
         top = jnp.maximum(jnp.max(old, axis=1, keepdims=True), new)
         old = jnp.exp(old - top)
         new = jnp.exp(new - top)
-        denom = jnp.sum(old, axis=1, keepdims=True) + new
-        probs = (old / denom).astype(BF16)
-        new = (new / denom).astype(BF16).astype(F32)
+        share = 1.0 / (jnp.sum(old, axis=1, keepdims=True) + new)
+        probs = (old * share).astype(BF16)
+        new = (new * share).astype(BF16).astype(F32)
         for i, r in enumerate(chosen):
             for g in range(kv_heads):
                 first = i * heads + g * group
@@ -179,14 +179,13 @@
     return pl.pallas_call(
         functools.partial(attention_kernel, cap),
         in_specs=[pl.BlockSpec(memory_space=pltpu.HBM)] * len(arrays),
-        out_specs=[vmem_spec()] * 7,
+        out_specs=[vmem_spec()] * 6,
         out_shape=[
             jax.ShapeDtypeStruct((devices, rows * each, LANE), BF16),
             table,
             table,
             jax.ShapeDtypeStruct((rows * width // LANE, LANE), F32),
             jax.ShapeDtypeStruct(gain.shape, F32),
-            half,
             half,
         ],
         scratch_shapes=[
@@ -200,7 +199,7 @@
             pltpu.VMEM((rows * heads, LANE), F32),
             pltpu.VMEM((rows, heads, LANE), F32),
             pltpu.SMEM((experts,), jnp.int32),
-            pltpu.SemaphoreType.DMA((9 + rows,)),
+            pltpu.SemaphoreType.DMA((8 + rows,)),
         ],
         compiler_params=pltpu.CompilerParams(vmem_limit_bytes=12 << 20),
     )(*(pltpu.with_memory_space_constraint(array, pltpu.HBM) for array in arrays))
@@ -224,13 +223,16 @@
             axis=1,
         )
 
+    def half_cols(first, step):
+        return pl.ds(pl.multiple_of(core * width + first, LANE), step)
+
     own_left = left(core * (held // LANE))
     peer_left = left((1 - core) * (held // LANE))
     step = 512
     for first in range(0, width, step):
         cols = slice(first, first + step)
         total = jnp.dot(own_left, own_ref[:, cols], preferred_element_type=F32) + jnp.dot(
-            peer_left, peer_ref[:, cols], preferred_element_type=F32
+            peer_left, peer_ref[:, half_cols(first, step)], preferred_element_type=F32
         )
         for t in range(step // LANE):
             o32[pl.ds(first // LANE + t, sums, stride=chunks), :] = total[
@@ -330,7 +332,7 @@
     return pl.ds(pl.multiple_of(which * size, size), size)
 
 
-def own_kernel(own_ref, gate_ref, up_ref, gate_out, up_out, x32, x16):
+def own_kernel(own_ref, gate_ref, up_ref, down_ref, gate_out, up_out, x32, x16):
     rows_from_chunks(own_ref, x32, x16)
     span = half_of(lax.axis_index("node") % 2, x16.shape[1])
     gate_out[...] = jnp.dot(x16[...], gate_ref[0, span, :], preferred_element_type=F32)
@@ -374,13 +376,13 @@
     peer = swap(own)
     gate, up = pl.pallas_call(
         own_kernel,
-        in_specs=[vmem_spec()] * 3,
+        in_specs=[vmem_spec()] * 4,
         out_specs=[vmem_spec()] * 2,
         out_shape=[sums, sums],
         scratch_shapes=[wide, narrow],
         compiler_params=params,
         cost_estimate=estimate(4 * arrived * half * hidden, 4 * half * hidden),
-    )(own, w_gate, w_up)
+    )(own, w_gate, w_up, w_down)
     act, send = pl.pallas_call(
         peer_kernel,
         in_specs=[vmem_spec()] * 6,
@@ -467,7 +469,7 @@
         return lax.all_to_all(array, "node", split_axis=0, concat_axis=0, tiled=True)
 
     gain = mlp_gain.reshape(width // LANE, LANE)
-    context, weights, pick, h32, gain, w_keep, w_send = attention(
+    context, weights, pick, h32, gain, w_keep = attention(
         queries,
         new_kv,
         kv_cache,
@@ -480,7 +482,7 @@
         devices,
         cap,
     )
-    w_peer = swap(w_send)
+    w_peer = swap(w_out)
     gathered = exchange(context)
     sums = exchange(project(gathered, w_keep, w_peer))
     a32, mixed, outgoing = norm_dispatch(sums, h32, gain, pick, cap)

time: 69.4 us -> 68.9 us (level)
  transfers between devices with their start and end apart: 3 -> 3, of which waited for: 2 -> 2; matrix products, arithmetic and copies ran while one was open for 0% -> 0% of each run, Pallas kernels for 2% -> 6%
where the time goes in v4:
time: 68.9 us; the launch traced here: 68.7 us
  blocking collectives  58.6 us (85%)
  Pallas kernels  6.93 us (10%)
  waiting for transfers between devices  1.69 us (2%)
  starting transfers between devices  0.72 us (1%)
  between operations  0.72 us (1%)
    all_to_all x4, blocking collectives, exchange(): lax.all_to_all(array, 'node', split_axis=0, concat_axis=0, tiled=True)  58.6 us
    pallas_call x1, Pallas kernels, attention(): pl.pallas_call(functools.partial(attention_kernel, cap), in_specs=[pl.Blo...  2.76 us
    ppermute x3, waiting for transfers between devices, swap(): return lax.ppermute(array, 'node', pairs)  1.69 us
  transfers between devices with their start and end apart: 3, of which 2 were waited for; matrix products, arithmetic and copies ran while one was open for 0% of the time, Pallas kernels for 6%

profile of v4, /device:TPU:0, one launch (start us, length us, event | category | flops | bytes accessed | tf_op | source)
XLA Modules:
  0.0 68.7 jit_solution(9814088258781007134)
XLA Ops:
  0.6 0.5 collective-permute-start
  1.2 0.0 copy-start.2
  1.2 2.8 %shard_map.131 = (bf16[32,16,128]{2,1,0:T(8,128)(2,1)S(1)}, f32[128,128]{1,0:T(8,128)S(1)}, f32[128,128]{1,0:T(8,128)S(1)}, f32[128,128]{1,0:T(8,128)S(1)}, f32[...) custom-call(bf16[4,8192]{1,0:T(4,128)(2,1)} %q_hbm.1, bf16[4,2,512]{2,1,0:T(2,128)(2,1)} %new_hbm.1, ...), custom_call_target="tpu_custom_call" | custom-call | tf_op jit(solution)/shard_map/pallas_call | solution.py:179
  3.9 0.0 copy-start
  3.9 0.0 copy-start.1
  3.9 15.0 %all_to_all.20.ctx_ref = bf16[32,16,128]{2,1,0:T(8,128)(2,1)S(1)} all-to-all(bf16[32,16,128]{2,1,0:T(8,128)(2,1)S(1)} %get-tuple-element.16), channel_id=1, replica_groups=mesh['groups'=1,'node'=32] {'node'}, dimensions={0} | all-to-all | bytes 262144 | tf_op jit(solution)/shard_map/all_to_all | solution.py:469
  18.9 0.0 collective-permute-done.peer_ref
  18.9 0.6 shard_map.132
  19.6 17.3 %all_to_all.21.sums_ref = bf16[32,1,64,128]{3,2,1,0:T(8,128)(2,1)S(1)} all-to-all(bf16[32,1,64,128]{3,2,1,0:T(8,128)(2,1)S(1)} %shard_map.132), channel_id=1, replica_groups=mesh['groups'=1,'node'=32] {'node'}, dimensions={0} | all-to-all | bytes 1048576 | tf_op jit(solution)/shard_map/all_to_all | solution.py:469
  36.9 0.3 shard_map.133
  37.2 13.5 %all_to_all.22.own_ref = bf16[32,32,128]{2,1,0:T(8,128)(2,1)S(1)} all-to-all(bf16[32,32,128]{2,1,0:T(8,128)(2,1)S(1)} %get-tuple-element.21), channel_id=1, replica_groups=mesh['groups'=1,'node'=32] {'node'}, dimensions={0} | all-to-all | bytes 524288 | tf_op jit(solution)/shard_map/all_to_all | solution.py:469
  50.7 0.0 collective-permute-start.1
  50.7 0.0 copy-done.2
  50.7 0.0 copy-done
  50.7 0.0 copy-done.1
  50.7 0.8 %shard_map.134 = (f32[64,384]{1,0:T(8,128)S(1)}, f32[64,384]{1,0:T(8,128)S(1)}) custom-call(bf16[32,32,128]{2,1,0:T(8,128)(2,1)S(1)} %all_to_all.22.own_ref, bf16[1,4096,384]{2,1,0:T(8,128)(2,1)S(1)} %copy-done.1, bf16[1,4096,384]{2,1,0:T(8,128)(2,1)S(1)} %copy-done.2, bf16[1,384,4096]{2,1,0:T(8,128)(2,1)S(1)} %copy-done), custom_call_target="tpu_custom_call" | custom-call | flops 201326592 | bytes 3145728 | tf_op jit(solution)/shard_map/pallas_call | solution.py:377
  51.5 0.7 %collective-permute-done.1.peer_ref = bf16[32,32,128]{2,1,0:T(8,128)(2,1)S(1)} collective-permute-done((bf16[32,32,128]{2,1,0:T(8,128)(2,1)S(1)}, bf16[32,32,128]{2,1,0:T(8,128)(2,1)S(1)}, u32[]{:S(2)}, u32[]{:S(2)}) %collective-permute-start.1) | collective-permute-done | bytes 262176 | tf_op jit(solution)/shard_map/ppermute | solution.py:466
  52.2 1.2 %shard_map.135 = (bf16[64,384]{1,0:T(8,128)(2,1)S(1)}, bf16[32,32,128]{2,1,0:T(8,128)(2,1)S(1)}) custom-call(bf16[32,32,128]{2,1,0:T(8,128)(2,1)S(1)} %collective-permute-done.1.peer_ref, f32[64,384]{1,0:T(8,128)S(1)} %get-tuple-element.22.gate_in, f32[64,384]{1,0:T(8,128)S(1)} %get-tuple-element.23.up_in, bf16[1,4096,384]{2,1,0:T(8,128)(2,1)S(1)} %copy-done.1, ...), custom_call_target="tpu_custom_call" | custom-call | flops 301989888 | bytes 4718592 | tf_op jit(solution)/shard_map/pallas_call | solution.py:386
  53.4 0.2 collective-permute-start.2
  53.6 0.4 shard_map.136
  54.0 0.9 %collective-permute-done.2 = bf16[32,32,128]{2,1,0:T(8,128)(2,1)S(1)} collective-permute-done((bf16[32,32,128]{2,1,0:T(8,128)(2,1)S(1)}, bf16[32,32,128]{2,1,0:T(8,128)(2,1)S(1)}, u32[]{:S(2)}, u32[]{:S(2)}) %collective-permute-start.2) | collective-permute-done | bytes 262176 | tf_op jit(solution)/shard_map/ppermute | solution.py:466
  55.0 0.1 add_convert_fusion
  55.1 12.8 %all_to_all.23.back_ref = bf16[32,32,128]{2,1,0:T(8,128)(2,1)S(1)} all-to-all(bf16[32,32,128]{2,1,0:T(8,128)(2,1)S(1)} %add_convert_fusion), channel_id=1, replica_groups=mesh['groups'=1,'node'=32] {'node'}, dimensions={0} | all-to-all | bytes 524288 | tf_op jit(solution)/shard_map/all_to_all | solution.py:469
  67.9 0.9 %shard_map.137 = (bf16[4,4096]{1,0:T(4,128)(2,1)}, bf16[4,4096]{1,0:T(4,128)(2,1)}) custom-call(f32[128,128]{1,0:T(8,128)S(1)} %get-tuple-element.15.weight_ref, bf16[32,32,128]{2,1,0:T(8,128)(2,1)S(1)} %all_to_all.23.back_ref, f32[128,128]{1,0:T(8,128)S(1)} %get-tuple-element.26.mixed_ref, f32[128,128]{1,0:T(8,128)S(1)} %get-tuple-element.27.a32_ref), custom_call_target="tpu_custom_call" | custom-call | tf_op jit(solution)/shard_map/pallas_call | solution.py:435
Async XLA Ops:
  0.6 18.3 %collective-permute-start = (bf16[256,4096]{1,0:T(8,128)(2,1)}, bf16[256,4096]{1,0:T(8,128)(2,1)S(1)}, u32[]{:S(2)}, u32[]{:S(2)}) collective-permute-start(bf16[256,4096]{1,0:T(8,128)(2,1)} %w_hbm.1), channel_id=1, source_target_pairs={{0,1},{1,0},{2,3},{3,2},{4,5},{5,4},{6,7},{7,6},{8,9},{9,8},{10,11... | collective-permute-start | bytes 6291464 | tf_op jit(solution)/shard_map/ppermute | solution.py:466
  1.2 49.5 %copy-start.2 = (bf16[1,4096,384]{2,1,0:T(8,128)(2,1)S(1)}, bf16[1,4096,384]{2,1,0:T(8,128)(2,1)}, u32[]{:S(2)}) copy-start(bf16[1,4096,384]{2,1,0:T(8,128)(2,1)} %up_ref.3) | copy-start | bytes 9437188
  3.9 46.8 %copy-start = (bf16[1,384,4096]{2,1,0:T(8,128)(2,1)S(1)}, bf16[1,384,4096]{2,1,0:T(8,128)(2,1)}, u32[]{:S(2)}) copy-start(bf16[1,384,4096]{2,1,0:T(8,128)(2,1)} %down_ref.5) | copy-start | bytes 9437188
  3.9 46.7 %copy-start.1 = (bf16[1,4096,384]{2,1,0:T(8,128)(2,1)S(1)}, bf16[1,4096,384]{2,1,0:T(8,128)(2,1)}, u32[]{:S(2)}) copy-start(bf16[1,4096,384]{2,1,0:T(8,128)(2,1)} %gate_ref.3) | copy-start | bytes 9437188
  50.7 1.5 %collective-permute-start.1 = (bf16[32,32,128]{2,1,0:T(8,128)(2,1)S(1)}, bf16[32,32,128]{2,1,0:T(8,128)(2,1)S(1)}, u32[]{:S(2)}, u32[]{:S(2)}) collective-permute-start(bf16[32,32,128]{2,1,0:T(8,128)(2,1)S(1)} %all_to_all.22.own_ref), channel_id=1, source_target_pairs={{0,1},{1,0},{2,3},{3,2},{4,5},{5,4},{6,7},{7,6},{8,9},{9,8},{10,11... | collective-permute-start | bytes 786440 | tf_op jit(solution)/shard_map/ppermute | solution.py:466
  53.4 1.6 %collective-permute-start.2 = (bf16[32,32,128]{2,1,0:T(8,128)(2,1)S(1)}, bf16[32,32,128]{2,1,0:T(8,128)(2,1)S(1)}, u32[]{:S(2)}, u32[]{:S(2)}) collective-permute-start(bf16[32,32,128]{2,1,0:T(8,128)(2,1)S(1)} %get-tuple-element.25), channel_id=1, source_target_pairs={{0,1},{1,0},{2,3},{3,2},{4,5},{5,4},{6,7},{7,6},{8,9},{9,8},{10,11... | collective-permute-start | bytes 786440 | tf_op jit(solution)/shard_map/ppermute | solution.py:466

commit v5 on v4

--- a/solution.py
+++ b/solution.py
@@ -238,7 +238,9 @@
             o32[pl.ds(first // LANE + t, sums, stride=chunks), :] = total[
                 :, t * LANE : (t + 1) * LANE
             ]
-    out_ref[:, 0] = o32[...].reshape(devices, o32.shape[0] // devices, LANE).astype(BF16)
+    sides = o32[...].reshape(2, devices // 2, o32.shape[0] // devices, LANE).astype(BF16)
+    for side in range(2):
+        out_ref[:, side] = sides[side]
 
 
 def project(gathered, w_own, w_peer):
@@ -250,7 +252,7 @@
         project_kernel,
         in_specs=[vmem_spec()] * 3,
         out_specs=vmem_spec(),
-        out_shape=jax.ShapeDtypeStruct((devices, 1, rows * chunks, LANE), BF16),
+        out_shape=jax.ShapeDtypeStruct((devices // 2, 2, rows * chunks, LANE), BF16),
         scratch_shapes=[
             pltpu.VMEM((devices * per, LANE), F32),
             pltpu.VMEM((devices * rows * chunks, LANE), F32),
@@ -259,56 +261,113 @@
     )(gathered, w_own, w_peer)
 
 
-def norm_kernel(cap, sums_ref, h32_ref, gain_ref, pick_ref, attn_ref, mixed_ref, out_ref):
-    devices, tiles, per, _ = sums_ref.shape
+def my_side():
+    return lax.axis_index("node") // (lax.axis_size("node") // 2)
+
+
+def share_kernel(sums_ref, h32_ref, pick_ref, part_ref, pay_ref):
+    devices, _, per, _ = sums_ref.shape
+    size = h32_ref.shape[0]
+    rows = pick_ref.shape[0] // (pay_ref.shape[0] - 2 * size) // 2
+    total = size // rows
+    half = total // 2
+    side = my_side()
+    for c in range(2):
+        for h in range(2):
+            acc = sums_ref[c, h].astype(F32)
+            for k in range(1, devices // 2):
+                acc = acc + sums_ref[2 * k + c, h].astype(F32)
+            for r in range(rows):
+                first = r * total + c * half
+                part_ref[h, first : first + half, :] = acc[r * half : (r + 1) * half]
+    pay_ref[:size] = part_ref[1 - side].astype(BF16)
+    pay_ref[size : 2 * size] = (part_ref[side] + h32_ref[...]).astype(BF16)
+    slots = pay_ref.shape[0] - 2 * size
+    lane = lax.broadcasted_iota(jnp.int32, (slots, LANE), 1)
+    tile = jnp.zeros((slots, LANE), F32)
+    for r in range(rows):
+        chosen = pick_ref[pl.ds((1 - side) * slots * rows + r, slots, stride=rows), :]
+        tile = jnp.where(lane // (LANE // rows) == r, chosen, tile)
+    pay_ref[2 * size :] = tile.astype(BF16)
+
+
+def share(sums, h32, pick, slots):
+    size = h32.shape[0]
+    return pl.pallas_call(
+        share_kernel,
+        in_specs=[vmem_spec()] * 3,
+        out_specs=[vmem_spec()] * 2,
+        out_shape=[
+            jax.ShapeDtypeStruct((2, size, LANE), F32),
+            jax.ShapeDtypeStruct((2 * size + slots, LANE), BF16),
+        ],
+        compiler_params=pltpu.CompilerParams(vmem_limit_bytes=6 << 20),
+    )(sums, h32, pick)
+
+
+def norm_kernel(
+    cap, part_ref, pay_ref, h32_ref, gain_ref, pick_ref, attn_ref, mixed_ref, out_ref
+):
     total = gain_ref.shape[0]
-    rows = h32_ref.shape[0] // total
+    size = h32_ref.shape[0]
+    rows = size // total
     half = total // 2
-    for c in range(2):
-        acc = sums_ref[c, 0].astype(F32)
-        for k in range(1, devices // 2):
-            acc = acc + sums_ref[2 * k + c, 0].astype(F32)
+    slots = pay_ref.shape[0] - 2 * size
+    side = my_side()
+    attn = part_ref[side] + pay_ref[:size].astype(F32)
+    attn_ref[...] = attn
+    own = h32_ref[...] + attn.astype(BF16).astype(F32)
+    mixed_ref[...] = own
+    mirror = part_ref[1 - side] + pay_ref[size : 2 * size].astype(F32)
+
+    def normed(state):
+        result = []
         for r in range(rows):
-            attn_ref[r * total + c * half : r * total + (c + 1) * half, :] = acc[
-                r * half : (r + 1) * half
-            ]
-    normed = []
-    for r in range(rows):
-        span = slice(r * total, (r + 1) * total)
-        mixed = h32_ref[span, :] + attn_ref[span, :].astype(BF16).astype(F32)
-        mixed_ref[span, :] = mixed
-        square = jnp.sum(jnp.sum(mixed * mixed, axis=0, keepdims=True), axis=1, keepdims=True)
-        scaled = mixed * lax.rsqrt(square / width_of(total) + 1e-06) * gain_ref[...]
-        normed.append(scaled)
-    for slot in range(devices // 2 * cap):
-        e, s = divmod(slot, cap)
-        chosen = normed[0] * pick_ref[slot * rows : slot * rows + 1, :]
-        for r in range(1, rows):
-            chosen = chosen + normed[r] * pick_ref[slot * rows + r : slot * rows + r + 1, :]
-        chosen = chosen.astype(BF16)
-        for c in range(2):
-            out_ref[2 * e + c, s * half : (s + 1) * half, :] = chosen[c * half : (c + 1) * half]
+            mixed = state[r * total : (r + 1) * total]
+            square = jnp.sum(jnp.sum(mixed * mixed, axis=0, keepdims=True), axis=1, keepdims=True)
+            result.append(mixed * lax.rsqrt(square / width_of(total) + 1e-06) * gain_ref[...])
+        return result
+
+    tile = pay_ref[2 * size :].astype(F32)
+    lane = lax.broadcasted_iota(jnp.int32, (slots, LANE), 1)
+    taken = [
+        jnp.max(jnp.where(lane // (LANE // rows) == r, tile, 0.0), axis=1, keepdims=True)
+        for r in range(rows)
+    ]
+    first = side * slots * rows
+    kept = [pick_ref[pl.ds(first + r, slots, stride=rows), :] for r in range(rows)]
+    for state, picks, where in ((own, kept, side), (mirror, taken, 1 - side)):
+        lines = normed(state)
+        for slot in range(slots):
+            chosen = lines[0] * picks[0][slot : slot + 1, :]
+            for r in range(1, rows):
+                chosen = chosen + lines[r] * picks[r][slot : slot + 1, :]
+            chosen = chosen.astype(BF16)
+            e, s = divmod(slot, cap)
+            for c in range(2):
+                out_ref[2 * e + c, where, s * half : (s + 1) * half, :] = chosen[
+                    c * half : (c + 1) * half
+                ]
 
 
 def width_of(chunks):
     return chunks * LANE
 
 
-def norm_dispatch(sums, h32, gain, pick, cap):
-    devices = sums.shape[0]
+def norm_dispatch(part, pay, h32, gain, pick, devices, cap):
     total = gain.shape[0]
     state = jax.ShapeDtypeStruct(h32.shape, F32)
     return pl.pallas_call(
         functools.partial(norm_kernel, cap),
-        in_specs=[vmem_spec()] * 4,
+        in_specs=[vmem_spec()] * 5,
         out_specs=[vmem_spec()] * 3,
         out_shape=[
             state,
             state,
-            jax.ShapeDtypeStruct((devices, cap * total // 2, LANE), BF16),
+            jax.ShapeDtypeStruct((devices // 2, 2, cap * total // 2, LANE), BF16),
         ],
         compiler_params=pltpu.CompilerParams(vmem_limit_bytes=6 << 20),
-    )(sums, h32, gain, pick)
+    )(part, pay, h32, gain, pick)
 
 
 def rows_from_chunks(ref, x32, x16):
@@ -325,7 +384,10 @@
     half = width // LANE
     for t in range(half):
         x32[pl.ds(t, arrived, stride=half), :] = result[:, t * LANE : (t + 1) * LANE]
-    ref[...] = x32[...].reshape(ref.shape).astype(BF16)
+    devices, per, _ = ref.shape
+    blocks = x32[...].reshape(devices // 2, 2, per, LANE).astype(BF16)
+    for side in range(2):
+        ref[side * (devices // 2) : (side + 1) * (devices // 2)] = blocks[:, side]
 
 
 def half_of(which, size):
@@ -365,10 +427,10 @@
 
 def experts(own, swap, w_gate, w_up, w_down, cap):
     devices, per, _ = own.shape
-    half = per // cap * LANE
-    arrived = devices * cap
+    half = per // (2 * cap) * LANE
+    arrived = devices * 2 * cap
     hidden = w_gate.shape[2]
-    chunked = jax.ShapeDtypeStruct(own.shape, BF16)
+    chunked = jax.ShapeDtypeStruct((2 * devices, per // 2, LANE), BF16)
     sums = jax.ShapeDtypeStruct((arrived, hidden), F32)
     wide = pltpu.VMEM((devices * per, LANE), F32)
     narrow = pltpu.VMEM((arrived, half), BF16)
@@ -468,6 +530,14 @@
     def exchange(array):
         return lax.all_to_all(array, "node", split_axis=0, concat_axis=0, tiled=True)
 
+    side = devices // 2
+    sides = [list(range(side)), list(range(side, devices))]
+
+    def exchange_inside(array):
+        return lax.all_to_all(
+            array, "node", split_axis=0, concat_axis=0, tiled=True, axis_index_groups=sides
+        )
+
     gain = mlp_gain.reshape(width // LANE, LANE)
     context, weights, pick, h32, gain, w_keep = attention(
         queries,
@@ -484,9 +554,12 @@
     )
     w_peer = swap(w_out)
     gathered = exchange(context)
-    sums = exchange(project(gathered, w_keep, w_peer))
-    a32, mixed, outgoing = norm_dispatch(sums, h32, gain, pick, cap)
-    arrived = exchange(outgoing)
+    sums = exchange_inside(project(gathered, w_keep, w_peer))
+    part, pay = share(sums, h32, pick, expert_count // 2 * cap)
+    pay = lax.ppermute(pay, "node", [(i, i ^ side) for i in range(devices)])
+    a32, mixed, outgoing = norm_dispatch(part, pay, h32, gain, pick, devices, cap)
+    arrived = exchange_inside(outgoing)
+    arrived = arrived.reshape(side, -1, LANE)
     back = exchange(experts(arrived, swap, w_gate, w_up, w_down, cap))
     return combine(weights, back, mixed, a32, rows, width, cap)
 

time: 68.9 us -> 67.5 us (0.980)
  blocking collectives: 58.6 us -> 51.1 us
  waiting for transfers between devices: 1.69 us -> 6.83 us
  starting transfers between devices: 0.72 us -> 1.58 us
    all_to_all x4 -> x2, blocking collectives: 58.6 us -> 27.3 us  [exchange(): lax.all_to_all(array, 'node', split_axis=0, concat_axis=0, tiled=True)]
    all_to_all x0 -> x2, blocking collectives: none -> 23.8 us  [exchange_inside(): lax.all_to_all(array, 'node', split_axis=0, concat_axis=0, tiled=True, ax...]
    ppermute x0 -> x1, waiting for transfers between devices: none -> 5.15 us  [body(): pay = lax.ppermute(pay, 'node', [(i, i ^ side) for i in range(devices)])]
    ppermute x0 -> x1, starting transfers between devices: none -> 0.86 us  [body(): pay = lax.ppermute(pay, 'node', [(i, i ^ side) for i in range(devices)])]
  transfers between devices with their start and end apart: 3 -> 4, of which waited for: 2 -> 3; matrix products, arithmetic and copies ran while one was open for 0% -> 0% of each run, Pallas kernels for 6% -> 6%
where the time goes in v5:
time: 67.5 us; the launch traced here: 67.3 us
  blocking collectives  51.1 us (76%)
  Pallas kernels  6.99 us (10%)
  waiting for transfers between devices  6.83 us (10%)
  starting transfers between devices  1.58 us (2%)
  between operations  0.71 us (1%)
    all_to_all x2, blocking collectives, exchange(): lax.all_to_all(array, 'node', split_axis=0, concat_axis=0, tiled=True)  27.3 us
    all_to_all x2, blocking collectives, exchange_inside(): lax.all_to_all(array, 'node', split_axis=0, concat_axis=0, tiled=True, ax...  23.8 us
    ppermute x1, waiting for transfers between devices, body(): pay = lax.ppermute(pay, 'node', [(i, i ^ side) for i in range(devices)])  5.15 us
    pallas_call x1, Pallas kernels, attention(): pl.pallas_call(functools.partial(attention_kernel, cap), in_specs=[pl.Blo...  2.76 us
    ppermute x3, waiting for transfers between devices, swap(): return lax.ppermute(array, 'node', pairs)  1.68 us
  transfers between devices with their start and end apart: 4, of which 3 were waited for; matrix products, arithmetic and copies ran while one was open for 0% of the time, Pallas kernels for 6%

profile of v5, /device:TPU:0, one launch (start us, length us, event | category | flops | bytes accessed | tf_op | source)
XLA Modules:
  0.0 67.3 jit_solution(7157922411169317813)
XLA Ops:
  0.6 0.5 collective-permute-start
  1.2 0.0 copy-start.2
  1.2 2.8 %shard_map.131 = (bf16[32,16,128]{2,1,0:T(8,128)(2,1)S(1)}, f32[128,128]{1,0:T(8,128)S(1)}, f32[128,128]{1,0:T(8,128)S(1)}, f32[128,128]{1,0:T(8,128)S(1)}, f32[...) custom-call(bf16[4,8192]{1,0:T(4,128)(2,1)} %q_hbm.1, bf16[4,2,512]{2,1,0:T(2,128)(2,1)} %new_hbm.1, ...), custom_call_target="tpu_custom_call" | custom-call | tf_op jit(solution)/shard_map/pallas_call | solution.py:179
  3.9 15.0 %all_to_all.20.ctx_ref = bf16[32,16,128]{2,1,0:T(8,128)(2,1)S(1)} all-to-all(bf16[32,16,128]{2,1,0:T(8,128)(2,1)S(1)} %get-tuple-element.18), channel_id=1, replica_groups=mesh['groups'=1,'node'=32] {'node'}, dimensions={0} | all-to-all | bytes 262144 | tf_op jit(solution)/shard_map/all_to_all | solution.py:531
  18.9 0.0 collective-permute-done.peer_ref
  18.9 0.0 copy-start
  18.9 0.0 copy-start.1
  18.9 0.6 shard_map.132
  19.6 13.4 %all_to_all.21.sums_ref = bf16[16,2,64,128]{3,2,1,0:T(8,128)(2,1)S(1)} all-to-all(bf16[16,2,64,128]{3,2,1,0:T(8,128)(2,1)S(1)} %shard_map.132), channel_id=1, replica_groups={{0,1,2,3,4,5,6,7,8,9,10,11,12,13,14,15},{16,17,18,19,20,21,22,23,24,25,..., dimensions={0} | all-to-all | bytes 1048576 | tf_op jit(solution)/shard_map/all_to_all | solution.py:537
  33.0 0.1 shard_map.133
  33.1 0.9 %collective-permute-start.1 = (bf16[272,128]{1,0:T(8,128)(2,1)S(1)}, bf16[272,128]{1,0:T(8,128)(2,1)S(1)}, u32[]{:S(2)}, u32[]{:S(2)}) collective-permute-start(bf16[272,128]{1,0:T(8,128)(2,1)S(1)} %get-tuple-element.23), channel_id=1, source_target_pairs={{0,16},{1,17},{2,18},{3,19},{4,20},{5,21},{6,22},{7,23},{8,24},{9,... | collective-permute-start | bytes 208904 | tf_op jit(solution)/shard_map/ppermute | solution.py:559
  33.9 5.1 %collective-permute-done.1.pay_ref = bf16[272,128]{1,0:T(8,128)(2,1)S(1)} collective-permute-done((bf16[272,128]{1,0:T(8,128)(2,1)S(1)}, bf16[272,128]{1,0:T(8,128)(2,1)S(1)}, u32[]{:S(2)}, u32[]{:S(2)}) %collective-permute-start.1) | collective-permute-done | bytes 69664 | tf_op jit(solution)/shard_map/ppermute | solution.py:559
  39.1 0.3 shard_map.134
  39.3 10.3 %all_to_all.22 = bf16[16,2,32,128]{3,2,1,0:T(8,128)(2,1)S(1)} all-to-all(bf16[16,2,32,128]{3,2,1,0:T(8,128)(2,1)S(1)} %get-tuple-element.25), channel_id=1, replica_groups={{0,1,2,3,4,5,6,7,8,9,10,11,12,13,14,15},{16,17,18,19,20,21,22,23,24,25,..., dimensions={0} | all-to-all | bytes 524288 | tf_op jit(solution)/shard_map/all_to_all | solution.py:537
  49.7 0.0 collective-permute-start.2
  49.7 0.0 copy-done.2
  49.7 0.0 copy-done
  49.7 0.0 copy-done.1
  49.7 0.8 %shard_map.135 = (f32[64,384]{1,0:T(8,128)S(1)}, f32[64,384]{1,0:T(8,128)S(1)}) custom-call(bf16[16,64,128]{2,1,0:T(8,128)(2,1)S(1)} %bitcast.3, bf16[1,4096,384]{2,1,0:T(8,128)(2,1)S(1)} %copy-done.1, bf16[1,4096,384]{2,1,0:T(8,128)(2,1)S(1)} %copy-done.2, bf16[1,384,4096]{2,1,0:T(8,128)(2,1)S(1)} %copy-done), custom_call_target="tpu_custom_call" | custom-call | flops 201326592 | bytes 3145728 | tf_op jit(solution)/shard_map/pallas_call | solution.py:439
  50.5 0.7 %collective-permute-done.2.peer_ref = bf16[16,64,128]{2,1,0:T(8,128)(2,1)S(1)} collective-permute-done((bf16[16,64,128]{2,1,0:T(8,128)(2,1)S(1)}, bf16[16,64,128]{2,1,0:T(8,128)(2,1)S(1)}, u32[]{:S(2)}, u32[]{:S(2)}) %collective-permute-start.2) | collective-permute-done | bytes 262176 | tf_op jit(solution)/shard_map/ppermute | solution.py:528
  51.2 1.2 %shard_map.136 = (bf16[64,384]{1,0:T(8,128)(2,1)S(1)}, bf16[32,32,128]{2,1,0:T(8,128)(2,1)S(1)}) custom-call(bf16[16,64,128]{2,1,0:T(8,128)(2,1)S(1)} %collective-permute-done.2.peer_ref, f32[64,384]{1,0:T(8,128)S(1)} %get-tuple-element.26.gate_in, f32[64,384]{1,0:T(8,128)S(1)} %get-tuple-element.27.up_in, bf16[1,4096,384]{2,1,0:T(8,128)(2,1)S(1)} %copy-done.1, ...), custom_call_target="tpu_custom_call" | custom-call | flops 301989888 | bytes 4718592 | tf_op jit(solution)/shard_map/pallas_call | solution.py:448
  52.4 0.2 collective-permute-start.3
  52.6 0.4 shard_map.137
  53.1 0.9 %collective-permute-done.3 = bf16[32,32,128]{2,1,0:T(8,128)(2,1)S(1)} collective-permute-done((bf16[32,32,128]{2,1,0:T(8,128)(2,1)S(1)}, bf16[32,32,128]{2,1,0:T(8,128)(2,1)S(1)}, u32[]{:S(2)}, u32[]{:S(2)}) %collective-permute-start.3) | collective-permute-done | bytes 262176 | tf_op jit(solution)/shard_map/ppermute | solution.py:528
  54.0 0.1 add_convert_fusion
  54.1 12.3 %all_to_all.23.back_ref = bf16[32,32,128]{2,1,0:T(8,128)(2,1)S(1)} all-to-all(bf16[32,32,128]{2,1,0:T(8,128)(2,1)S(1)} %add_convert_fusion), channel_id=1, replica_groups=mesh['groups'=1,'node'=32] {'node'}, dimensions={0} | all-to-all | bytes 524288 | tf_op jit(solution)/shard_map/all_to_all | solution.py:531
  66.4 0.9 %shard_map.138 = (bf16[4,4096]{1,0:T(4,128)(2,1)}, bf16[4,4096]{1,0:T(4,128)(2,1)}) custom-call(f32[128,128]{1,0:T(8,128)S(1)} %get-tuple-element.17.weight_ref, bf16[32,32,128]{2,1,0:T(8,128)(2,1)S(1)} %all_to_all.23.back_ref, f32[128,128]{1,0:T(8,128)S(1)} %get-tuple-element.30.mixed_ref, f32[128,128]{1,0:T(8,128)S(1)} %get-tuple-element.31.a32_ref), custom_call_target="tpu_custom_call" | custom-call | tf_op jit(solution)/shard_map/pallas_call | solution.py:497
Async XLA Ops:
  0.6 18.3 %collective-permute-start = (bf16[256,4096]{1,0:T(8,128)(2,1)}, bf16[256,4096]{1,0:T(8,128)(2,1)S(1)}, u32[]{:S(2)}, u32[]{:S(2)}) collective-permute-start(bf16[256,4096]{1,0:T(8,128)(2,1)} %w_hbm.1), channel_id=1, source_target_pairs={{0,1},{1,0},{2,3},{3,2},{4,5},{5,4},{6,7},{7,6},{8,9},{9,8},{10,11... | collective-permute-start | bytes 6291464 | tf_op jit(solution)/shard_map/ppermute | solution.py:528
  1.2 48.5 %copy-start.2 = (bf16[1,4096,384]{2,1,0:T(8,128)(2,1)S(1)}, bf16[1,4096,384]{2,1,0:T(8,128)(2,1)}, u32[]{:S(2)}) copy-start(bf16[1,4096,384]{2,1,0:T(8,128)(2,1)} %up_ref.3) | copy-start | bytes 9437188
  18.9 30.8 %copy-start = (bf16[1,384,4096]{2,1,0:T(8,128)(2,1)S(1)}, bf16[1,384,4096]{2,1,0:T(8,128)(2,1)}, u32[]{:S(2)}) copy-start(bf16[1,384,4096]{2,1,0:T(8,128)(2,1)} %down_ref.5) | copy-start | bytes 9437188
  18.9 30.8 %copy-start.1 = (bf16[1,4096,384]{2,1,0:T(8,128)(2,1)S(1)}, bf16[1,4096,384]{2,1,0:T(8,128)(2,1)}, u32[]{:S(2)}) copy-start(bf16[1,4096,384]{2,1,0:T(8,128)(2,1)} %gate_ref.3) | copy-start | bytes 9437188
  33.1 6.0 %collective-permute-start.1 = (bf16[272,128]{1,0:T(8,128)(2,1)S(1)}, bf16[272,128]{1,0:T(8,128)(2,1)S(1)}, u32[]{:S(2)}, u32[]{:S(2)}) collective-permute-start(bf16[272,128]{1,0:T(8,128)(2,1)S(1)} %get-tuple-element.23), channel_id=1, source_target_pairs={{0,16},{1,17},{2,18},{3,19},{4,20},{5,21},{6,22},{7,23},{8,24},{9,... | collective-permute-start | bytes 208904 | tf_op jit(solution)/shard_map/ppermute | solution.py:559
  49.7 1.5 %collective-permute-start.2 = (bf16[16,64,128]{2,1,0:T(8,128)(2,1)S(1)}, bf16[16,64,128]{2,1,0:T(8,128)(2,1)S(1)}, u32[]{:S(2)}, u32[]{:S(2)}) collective-permute-start(bf16[16,64,128]{2,1,0:T(8,128)(2,1)S(1)} %bitcast.2), channel_id=1, source_target_pairs={{0,1},{1,0},{2,3},{3,2},{4,5},{5,4},{6,7},{7,6},{8,9},{9,8},{10,11... | collective-permute-start | bytes 786440 | tf_op jit(solution)/shard_map/ppermute | solution.py:528
  52.4 1.6 %collective-permute-start.3 = (bf16[32,32,128]{2,1,0:T(8,128)(2,1)S(1)}, bf16[32,32,128]{2,1,0:T(8,128)(2,1)S(1)}, u32[]{:S(2)}, u32[]{:S(2)}) collective-permute-start(bf16[32,32,128]{2,1,0:T(8,128)(2,1)S(1)} %get-tuple-element.29), channel_id=1, source_target_pairs={{0,1},{1,0},{2,3},{3,2},{4,5},{5,4},{6,7},{7,6},{8,9},{9,8},{10,11... | collective-permute-start | bytes 786440 | tf_op jit(solution)/shard_map/ppermute | solution.py:528

commit v6 on v5

--- a/solution.py
+++ b/solution.py
@@ -306,7 +306,7 @@
 
 
 def norm_kernel(
-    cap, part_ref, pay_ref, h32_ref, gain_ref, pick_ref, attn_ref, mixed_ref, out_ref
+    cap, part_ref, pay_ref, h32_ref, gain_ref, pick_ref, down_ref, attn_ref, mixed_ref, out_ref
 ):
     total = gain_ref.shape[0]
     size = h32_ref.shape[0]
@@ -354,12 +354,12 @@
     return chunks * LANE
 
 
-def norm_dispatch(part, pay, h32, gain, pick, devices, cap):
+def norm_dispatch(part, pay, h32, gain, pick, w_down, devices, cap):
     total = gain.shape[0]
     state = jax.ShapeDtypeStruct(h32.shape, F32)
     return pl.pallas_call(
         functools.partial(norm_kernel, cap),
-        in_specs=[vmem_spec()] * 5,
+        in_specs=[vmem_spec()] * 6,
         out_specs=[vmem_spec()] * 3,
         out_shape=[
             state,
@@ -367,7 +367,7 @@
             jax.ShapeDtypeStruct((devices // 2, 2, cap * total // 2, LANE), BF16),
         ],
         compiler_params=pltpu.CompilerParams(vmem_limit_bytes=6 << 20),
-    )(part, pay, h32, gain, pick)
+    )(part, pay, h32, gain, pick, w_down)
 
 
 def rows_from_chunks(ref, x32, x16):
@@ -394,7 +394,7 @@
     return pl.ds(pl.multiple_of(which * size, size), size)
 
 
-def own_kernel(own_ref, gate_ref, up_ref, down_ref, gate_out, up_out, x32, x16):
+def own_kernel(own_ref, gate_ref, up_ref, gate_out, up_out, x32, x16):
     rows_from_chunks(own_ref, x32, x16)
     span = half_of(lax.axis_index("node") % 2, x16.shape[1])
     gate_out[...] = jnp.dot(x16[...], gate_ref[0, span, :], preferred_element_type=F32)
@@ -414,18 +414,25 @@
     chunks_from_rows(result, x32, send_ref)
 
 
-def keep_kernel(act_ref, down_ref, keep_ref, x32):
+def keep_kernel(act_ref, down_ref, a32_ref, keep_ref, attn_hbm, x32, attn, sem):
+    rows, width = attn.shape
+    total = width // LANE
+    for t in range(total):
+        attn[:, t * LANE : (t + 1) * LANE] = a32_ref[pl.ds(t, rows, stride=total), :].astype(BF16)
+    copy = pltpu.make_async_copy(attn, attn_hbm, sem)
+    copy.start()
     size = down_ref.shape[2] // 2
     span = half_of(lax.axis_index("node") % 2, size)
     result = jnp.dot(act_ref[...], down_ref[0, :, span], preferred_element_type=F32)
     chunks_from_rows(result, x32, keep_ref)
+    copy.wait()
 
 
 def estimate(flops, moved):
     return pl.CostEstimate(flops=flops, bytes_accessed=moved, transcendentals=0)
 
 
-def experts(own, swap, w_gate, w_up, w_down, cap):
+def experts(own, swap, w_gate, w_up, w_down, a32, cap):
     devices, per, _ = own.shape
     half = per // (2 * cap) * LANE
     arrived = devices * 2 * cap
@@ -438,13 +445,13 @@
     peer = swap(own)
     gate, up = pl.pallas_call(
         own_kernel,
-        in_specs=[vmem_spec()] * 4,
+        in_specs=[vmem_spec()] * 3,
         out_specs=[vmem_spec()] * 2,
         out_shape=[sums, sums],
         scratch_shapes=[wide, narrow],
         compiler_params=params,
         cost_estimate=estimate(4 * arrived * half * hidden, 4 * half * hidden),
-    )(own, w_gate, w_up, w_down)
+    )(own, w_gate, w_up)
     act, send = pl.pallas_call(
         peer_kernel,
         in_specs=[vmem_spec()] * 6,
@@ -455,26 +462,29 @@
         cost_estimate=estimate(6 * arrived * half * hidden, 6 * half * hidden),
     )(peer, gate, up, w_gate, w_up, w_down)
     received = swap(send)
-    keep = pl.pallas_call(
+    width = 2 * half
+    attn_out = jax.ShapeDtypeStruct((a32.shape[0] * LANE // width, width), BF16)
+    keep, attn_out = pl.pallas_call(
         keep_kernel,
-        in_specs=[vmem_spec()] * 2,
-        out_specs=vmem_spec(),
-        out_shape=chunked,
-        scratch_shapes=[wide],
+        in_specs=[vmem_spec()] * 3,
+        out_specs=[vmem_spec(), pl.BlockSpec(memory_space=pltpu.HBM)],
+        out_shape=[chunked, attn_out],
+        scratch_shapes=[
+            wide,
+            pltpu.VMEM(attn_out.shape, BF16),
+            pltpu.SemaphoreType.DMA(()),
+        ],
         compiler_params=params,
         cost_estimate=estimate(2 * arrived * half * hidden, 2 * half * hidden),
-    )(act, w_down)
-    return (keep.astype(F32) + received.astype(F32)).astype(BF16)
-
-
-def combine_kernel(cap, weight_ref, back_ref, mixed_ref, a32_ref, attn_ref, out_ref, total32):
+    )(act, w_down, a32)
+    return (attn_out, (keep.astype(F32) + received.astype(F32)).astype(BF16))
+
+
+def combine_kernel(cap, weight_ref, back_ref, mixed_ref, out_ref, total32):
     rows, width = out_ref.shape
     total = width // LANE
     half = total // 2
     slots = weight_ref.shape[0] // rows
-    for t in range(total):
-        cols = slice(t * LANE, (t + 1) * LANE)
-        attn_ref[:, cols] = a32_ref[pl.ds(t, rows, stride=total), :].astype(BF16)
     for c in range(2):
         acc = [
             mixed_ref[r * total + c * half : r * total + (c + 1) * half, :] for r in range(rows)
@@ -492,16 +502,15 @@
         )
 
 
-def combine(weights, back, mixed, a32, rows, width, cap):
-    shape = jax.ShapeDtypeStruct((rows, width), BF16)
+def combine(weights, back, mixed, rows, width, cap):
     return pl.pallas_call(
         functools.partial(combine_kernel, cap),
-        in_specs=[vmem_spec()] * 4,
-        out_specs=[vmem_spec()] * 2,
-        out_shape=[shape, shape],
+        in_specs=[vmem_spec()] * 3,
+        out_specs=vmem_spec(),
+        out_shape=jax.ShapeDtypeStruct((rows, width), BF16),
         scratch_shapes=[pltpu.VMEM(mixed.shape, F32)],
         compiler_params=pltpu.CompilerParams(vmem_limit_bytes=6 << 20),
-    )(weights, back, mixed, a32)
+    )(weights, back, mixed)
 
 
 def body(
@@ -557,11 +566,12 @@
     sums = exchange_inside(project(gathered, w_keep, w_peer))
     part, pay = share(sums, h32, pick, expert_count // 2 * cap)
     pay = lax.ppermute(pay, "node", [(i, i ^ side) for i in range(devices)])
-    a32, mixed, outgoing = norm_dispatch(part, pay, h32, gain, pick, devices, cap)
+    a32, mixed, outgoing = norm_dispatch(part, pay, h32, gain, pick, w_down, devices, cap)
     arrived = exchange_inside(outgoing)
     arrived = arrived.reshape(side, -1, LANE)
-    back = exchange(experts(arrived, swap, w_gate, w_up, w_down, cap))
-    return combine(weights, back, mixed, a32, rows, width, cap)
+    attn_out, paired = experts(arrived, swap, w_gate, w_up, w_down, a32, cap)
+    layer_out = combine(weights, exchange(paired), mixed, rows, width, cap)
+    return (attn_out, layer_out)
 
 
 def solution(mesh):

time: 67.5 us -> 67.3 us (level)
  transfers between devices with their start and end apart: 4 -> 4, of which waited for: 3 -> 3; matrix products, arithmetic and copies ran while one was open for 0% -> 0% of each run, Pallas kernels for 6% -> 7%
where the time goes in v6:
time: 67.3 us; the launch traced here: 67.1 us
  blocking collectives  51.1 us (76%)
  Pallas kernels  7.4 us (11%)
  waiting for transfers between devices  6.26 us (9%)
  starting transfers between devices  1.57 us (2%)
  between operations  0.71 us (1%)
    all_to_all x2, blocking collectives, exchange(): lax.all_to_all(array, 'node', split_axis=0, concat_axis=0, tiled=True)  27.3 us
    all_to_all x2, blocking collectives, exchange_inside(): lax.all_to_all(array, 'node', split_axis=0, concat_axis=0, tiled=True, ax...  23.8 us
    ppermute x1, waiting for transfers between devices, body(): pay = lax.ppermute(pay, 'node', [(i, i ^ side) for i in range(devices)])  5.16 us
    pallas_call x1, Pallas kernels, attention(): pl.pallas_call(functools.partial(attention_kernel, cap), in_specs=[pl.Blo...  2.61 us
  transfers between devices with their start and end apart: 4, of which 3 were waited for; matrix products, arithmetic and copies ran while one was open for 0% of the time, Pallas kernels for 7%

profile of v6, /device:TPU:0, one launch (start us, length us, event | category | flops | bytes accessed | tf_op | source)
XLA Modules:
  0.0 67.1 jit_solution(8598447484504810886)
XLA Ops:
  0.6 0.5 collective-permute-start
  1.2 2.6 %shard_map.131 = (bf16[32,16,128]{2,1,0:T(8,128)(2,1)S(1)}, f32[128,128]{1,0:T(8,128)S(1)}, f32[128,128]{1,0:T(8,128)S(1)}, f32[128,128]{1,0:T(8,128)S(1)}, f32[...) custom-call(bf16[4,8192]{1,0:T(4,128)(2,1)} %q_hbm.1, bf16[4,2,512]{2,1,0:T(2,128)(2,1)} %new_hbm.1, ...), custom_call_target="tpu_custom_call" | custom-call | tf_op jit(solution)/shard_map/pallas_call | solution.py:179
  3.8 0.0 copy-start
  3.8 15.0 %all_to_all.20.ctx_ref = bf16[32,16,128]{2,1,0:T(8,128)(2,1)S(1)} all-to-all(bf16[32,16,128]{2,1,0:T(8,128)(2,1)S(1)} %get-tuple-element.19), channel_id=1, replica_groups=mesh['groups'=1,'node'=32] {'node'}, dimensions={0} | all-to-all | bytes 262144 | tf_op jit(solution)/shard_map/all_to_all | solution.py:540
  18.8 0.0 collective-permute-done.peer_ref
  18.8 0.0 copy-start.2
  18.8 0.6 shard_map.132
  19.4 0.0 copy-start.1
  19.4 13.4 %all_to_all.21.sums_ref = bf16[16,2,64,128]{3,2,1,0:T(8,128)(2,1)S(1)} all-to-all(bf16[16,2,64,128]{3,2,1,0:T(8,128)(2,1)S(1)} %shard_map.132), channel_id=1, replica_groups={{0,1,2,3,4,5,6,7,8,9,10,11,12,13,14,15},{16,17,18,19,20,21,22,23,24,25,..., dimensions={0} | all-to-all | bytes 1048576 | tf_op jit(solution)/shard_map/all_to_all | solution.py:546
  32.9 0.1 shard_map.133
  32.9 0.8 %collective-permute-start.1 = (bf16[272,128]{1,0:T(8,128)(2,1)S(1)}, bf16[272,128]{1,0:T(8,128)(2,1)S(1)}, u32[]{:S(2)}, u32[]{:S(2)}) collective-permute-start(bf16[272,128]{1,0:T(8,128)(2,1)S(1)} %get-tuple-element.24), channel_id=1, source_target_pairs={{0,16},{1,17},{2,18},{3,19},{4,20},{5,21},{6,22},{7,23},{8,24},{9,... | collective-permute-start | bytes 208904 | tf_op jit(solution)/shard_map/ppermute | solution.py:568
  33.8 5.2 %collective-permute-done.1.pay_ref = bf16[272,128]{1,0:T(8,128)(2,1)S(1)} collective-permute-done((bf16[272,128]{1,0:T(8,128)(2,1)S(1)}, bf16[272,128]{1,0:T(8,128)(2,1)S(1)}, u32[]{:S(2)}, u32[]{:S(2)}) %collective-permute-start.1) | collective-permute-done | bytes 69664 | tf_op jit(solution)/shard_map/ppermute | solution.py:568
  39.0 0.0 copy-done
  39.0 0.3 shard_map.134
  39.2 10.3 %all_to_all.22 = bf16[16,2,32,128]{3,2,1,0:T(8,128)(2,1)S(1)} all-to-all(bf16[16,2,32,128]{3,2,1,0:T(8,128)(2,1)S(1)} %get-tuple-element.26), channel_id=1, replica_groups={{0,1,2,3,4,5,6,7,8,9,10,11,12,13,14,15},{16,17,18,19,20,21,22,23,24,25,..., dimensions={0} | all-to-all | bytes 524288 | tf_op jit(solution)/shard_map/all_to_all | solution.py:546
  49.6 0.0 collective-permute-start.2
  49.6 0.0 copy-done.2
  49.6 0.0 copy-done.1
  49.6 0.8 %shard_map.135 = (f32[64,384]{1,0:T(8,128)S(1)}, f32[64,384]{1,0:T(8,128)S(1)}) custom-call(bf16[16,64,128]{2,1,0:T(8,128)(2,1)S(1)} %bitcast.3, bf16[1,4096,384]{2,1,0:T(8,128)(2,1)S(1)} %copy-done.1, bf16[1,4096,384]{2,1,0:T(8,128)(2,1)S(1)} %copy-done.2), custom_call_target="tpu_custom_call" | custom-call | flops 201326592 | bytes 3145728 | tf_op jit(solution)/shard_map/pallas_call | solution.py:446
  50.4 0.7 %collective-permute-done.2.peer_ref = bf16[16,64,128]{2,1,0:T(8,128)(2,1)S(1)} collective-permute-done((bf16[16,64,128]{2,1,0:T(8,128)(2,1)S(1)}, bf16[16,64,128]{2,1,0:T(8,128)(2,1)S(1)}, u32[]{:S(2)}, u32[]{:S(2)}) %collective-permute-start.2) | collective-permute-done | bytes 262176 | tf_op jit(solution)/shard_map/ppermute | solution.py:537
  51.1 1.2 %shard_map.136 = (bf16[64,384]{1,0:T(8,128)(2,1)S(1)}, bf16[32,32,128]{2,1,0:T(8,128)(2,1)S(1)}) custom-call(bf16[16,64,128]{2,1,0:T(8,128)(2,1)S(1)} %collective-permute-done.2.peer_ref, f32[64,384]{1,0:T(8,128)S(1)} %get-tuple-element.27.gate_in, f32[64,384]{1,0:T(8,128)S(1)} %get-tuple-element.28.up_in, bf16[1,4096,384]{2,1,0:T(8,128)(2,1)S(1)} %copy-done.1, ...), custom_call_target="tpu_custom_call" | custom-call | flops 301989888 | bytes 4718592 | tf_op jit(solution)/shard_map/pallas_call | solution.py:455
  52.3 0.2 collective-permute-start.3
  52.5 1.0 %shard_map.137 = (bf16[32,32,128]{2,1,0:T(8,128)(2,1)S(1)}, bf16[4,4096]{1,0:T(4,128)(2,1)}) custom-call(bf16[64,384]{1,0:T(8,128)(2,1)S(1)} %get-tuple-element.29.act_ref, bf16[1,384,4096]{2,1,0:T(8,128)(2,1)S(1)} %copy-done, f32[128,128]{1,0:T(8,128)S(1)} %get-tuple-element.30.a32_ref), custom_call_target="tpu_custom_call" | custom-call | flops 100663296 | bytes 1572864 | tf_op jit(solution)/shard_map/pallas_call | solution.py:467
  53.5 0.4 collective-permute-done.3
  53.9 0.1 add_convert_fusion
  54.0 12.3 %all_to_all.23.back_ref = bf16[32,32,128]{2,1,0:T(8,128)(2,1)S(1)} all-to-all(bf16[32,32,128]{2,1,0:T(8,128)(2,1)S(1)} %add_convert_fusion), channel_id=1, replica_groups=mesh['groups'=1,'node'=32] {'node'}, dimensions={0} | all-to-all | bytes 524288 | tf_op jit(solution)/shard_map/all_to_all | solution.py:540
  66.3 0.8 %shard_map.138 = bf16[4,4096]{1,0:T(4,128)(2,1)} custom-call(f32[128,128]{1,0:T(8,128)S(1)} %get-tuple-element.32.weight_ref, bf16[32,32,128]{2,1,0:T(8,128)(2,1)S(1)} %all_to_all.23.back_ref, f32[128,128]{1,0:T(8,128)S(1)} %get-tuple-element.35.mixed_ref), custom_call_target="tpu_custom_call" | custom-call | tf_op jit(solution)/shard_map/pallas_call | solution.py:506
Async XLA Ops:
  0.6 18.1 %collective-permute-start = (bf16[256,4096]{1,0:T(8,128)(2,1)}, bf16[256,4096]{1,0:T(8,128)(2,1)S(1)}, u32[]{:S(2)}, u32[]{:S(2)}) collective-permute-start(bf16[256,4096]{1,0:T(8,128)(2,1)} %w_hbm.1), channel_id=1, source_target_pairs={{0,1},{1,0},{2,3},{3,2},{4,5},{5,4},{6,7},{7,6},{8,9},{9,8},{10,11... | collective-permute-start | bytes 6291464 | tf_op jit(solution)/shard_map/ppermute | solution.py:537
  3.8 35.2 %copy-start = (bf16[1,384,4096]{2,1,0:T(8,128)(2,1)S(1)}, bf16[1,384,4096]{2,1,0:T(8,128)(2,1)}, u32[]{:S(2)}) copy-start(bf16[1,384,4096]{2,1,0:T(8,128)(2,1)} %down_ref.5) | copy-start | bytes 9437188
  18.8 30.8 %copy-start.2 = (bf16[1,4096,384]{2,1,0:T(8,128)(2,1)S(1)}, bf16[1,4096,384]{2,1,0:T(8,128)(2,1)}, u32[]{:S(2)}) copy-start(bf16[1,4096,384]{2,1,0:T(8,128)(2,1)} %up_ref.3) | copy-start | bytes 9437188
  19.4 30.2 %copy-start.1 = (bf16[1,4096,384]{2,1,0:T(8,128)(2,1)S(1)}, bf16[1,4096,384]{2,1,0:T(8,128)(2,1)}, u32[]{:S(2)}) copy-start(bf16[1,4096,384]{2,1,0:T(8,128)(2,1)} %gate_ref.3) | copy-start | bytes 9437188
  32.9 6.0 %collective-permute-start.1 = (bf16[272,128]{1,0:T(8,128)(2,1)S(1)}, bf16[272,128]{1,0:T(8,128)(2,1)S(1)}, u32[]{:S(2)}, u32[]{:S(2)}) collective-permute-start(bf16[272,128]{1,0:T(8,128)(2,1)S(1)} %get-tuple-element.24), channel_id=1, source_target_pairs={{0,16},{1,17},{2,18},{3,19},{4,20},{5,21},{6,22},{7,23},{8,24},{9,... | collective-permute-start | bytes 208904 | tf_op jit(solution)/shard_map/ppermute | solution.py:568
  49.6 1.5 %collective-permute-start.2 = (bf16[16,64,128]{2,1,0:T(8,128)(2,1)S(1)}, bf16[16,64,128]{2,1,0:T(8,128)(2,1)S(1)}, u32[]{:S(2)}, u32[]{:S(2)}) collective-permute-start(bf16[16,64,128]{2,1,0:T(8,128)(2,1)S(1)} %bitcast.2), channel_id=1, source_target_pairs={{0,1},{1,0},{2,3},{3,2},{4,5},{5,4},{6,7},{7,6},{8,9},{9,8},{10,11... | collective-permute-start | bytes 786440 | tf_op jit(solution)/shard_map/ppermute | solution.py:537
  52.3 1.6 %collective-permute-start.3 = (bf16[32,32,128]{2,1,0:T(8,128)(2,1)S(1)}, bf16[32,32,128]{2,1,0:T(8,128)(2,1)S(1)}, u32[]{:S(2)}, u32[]{:S(2)}) collective-permute-start(bf16[32,32,128]{2,1,0:T(8,128)(2,1)S(1)} %get-tuple-element.34), channel_id=1, source_target_pairs={{0,1},{1,0},{2,3},{3,2},{4,5},{5,4},{6,7},{7,6},{8,9},{9,8},{10,11... | collective-permute-start | bytes 786440 | tf_op jit(solution)/shard_map/ppermute | solution.py:537

commit v7 on v6

--- a/solution.py
+++ b/solution.py
@@ -56,18 +56,16 @@
     half = w_hbm.shape[1] // 2
     mine = pl.ds(pl.multiple_of(core * half, half), half)
     pairs = [(ids_hbm, ids), (len_hbm, lens), (q_hbm, qv), (new_hbm, nv)]
-    pairs += [(kv_hbm.at[r], kv.at[r]) for r in range(rows)]
+    pairs += [(kv_hbm.at[r, i], kv.at[r, i]) for i in range(2) for r in range(rows)]
     pairs += [(hidden_hbm, hv), (gain_hbm, gain_ref), (route_hbm, route)]
     pairs += [(w_hbm.at[:, mine], keep_ref)]
     copies = [
         pltpu.make_async_copy(source, target, sems.at[i])
         for i, (source, target) in enumerate(pairs)
     ]
-    for copy in copies[: 7 + rows]:
+    for copy in copies:
         copy.start()
     copies[2].wait()
-    for copy in copies[7 + rows :]:
-        copy.start()
     for h in range(heads):
         q32[pl.ds(h, rows, stride=heads), :] = qv[:, h * HEAD : (h + 1) * HEAD].astype(F32)
     weight_ref[...] = jnp.zeros(weight_ref.shape, F32)
@@ -75,7 +73,7 @@
     for e in range(slots // cap):
         count[e] = 0
     copies[0].wait()
-    copies[6 + rows].wait()
+    copies[6 + 2 * rows].wait()
     for row in range(rows):
         for k in range(ids.shape[1]):
             expert = ids[row, k]
@@ -124,6 +122,8 @@
         share = 1.0 / (jnp.sum(old, axis=1, keepdims=True) + new)
         probs = (old * share).astype(BF16)
         new = (new * share).astype(BF16).astype(F32)
+        for r in chosen:
+            copies[4 + rows + r].wait()
         for i, r in enumerate(chosen):
             for g in range(kv_heads):
                 first = i * heads + g * group
@@ -146,13 +146,13 @@
         ).astype(BF16)
         out_ref[2 * i] = block
         out_ref[2 * i + 1] = block
-    copies[4 + rows].wait()
+    copies[4 + 2 * rows].wait()
     total = h32_ref.shape[0] // rows
     for t in range(total):
         cols = slice(t * LANE, (t + 1) * LANE)
         h32_ref[pl.ds(t, rows, stride=total), :] = hv[:, cols].astype(F32)
-    copies[5 + rows].wait()
-    for copy in copies[7 + rows :]:
+    copies[5 + 2 * rows].wait()
+    for copy in copies[7 + 2 * rows :]:
         copy.wait()
 
 
@@ -199,7 +199,7 @@
             pltpu.VMEM((rows * heads, LANE), F32),
             pltpu.VMEM((rows, heads, LANE), F32),
             pltpu.SMEM((experts,), jnp.int32),
-            pltpu.SemaphoreType.DMA((8 + rows,)),
+            pltpu.SemaphoreType.DMA((8 + 2 * rows,)),
         ],
         compiler_params=pltpu.CompilerParams(vmem_limit_bytes=12 << 20),
     )(*(pltpu.with_memory_space_constraint(array, pltpu.HBM) for array in arrays))

time: 67.3 us -> 67.2 us (level)
  transfers between devices with their start and end apart: 4 -> 4, of which waited for: 3 -> 3; matrix products, arithmetic and copies ran while one was open for 0% -> 0% of each run, Pallas kernels for 7% -> 6%
where the time goes in v7:
time: 67.2 us; the launch traced here: 66.9 us
  blocking collectives  51.1 us (76%)
  Pallas kernels  7.21 us (11%)
  waiting for transfers between devices  6.25 us (9%)
  starting transfers between devices  1.58 us (2%)
  between operations  0.71 us (1%)
    all_to_all x2, blocking collectives, exchange(): lax.all_to_all(array, 'node', split_axis=0, concat_axis=0, tiled=True)  27.3 us
    all_to_all x2, blocking collectives, exchange_inside(): lax.all_to_all(array, 'node', split_axis=0, concat_axis=0, tiled=True, ax...  23.8 us
    ppermute x1, waiting for transfers between devices, body(): pay = lax.ppermute(pay, 'node', [(i, i ^ side) for i in range(devices)])  5.15 us
    pallas_call x1, Pallas kernels, attention(): pl.pallas_call(functools.partial(attention_kernel, cap), in_specs=[pl.Blo...  2.44 us
  transfers between devices with their start and end apart: 4, of which 3 were waited for; matrix products, arithmetic and copies ran while one was open for 0% of the time, Pallas kernels for 6%

profile of v7, /device:TPU:0, one launch (start us, length us, event | category | flops | bytes accessed | tf_op | source)
XLA Modules:
  0.0 66.9 jit_solution(11758604960418084671)
XLA Ops:
  0.6 0.5 collective-permute-start
  1.2 2.4 %shard_map.131 = (bf16[32,16,128]{2,1,0:T(8,128)(2,1)S(1)}, f32[128,128]{1,0:T(8,128)S(1)}, f32[128,128]{1,0:T(8,128)S(1)}, f32[128,128]{1,0:T(8,128)S(1)}, f32[...) custom-call(bf16[4,8192]{1,0:T(4,128)(2,1)} %q_hbm.1, bf16[4,2,512]{2,1,0:T(2,128)(2,1)} %new_hbm.1, ...), custom_call_target="tpu_custom_call" | custom-call | tf_op jit(solution)/shard_map/pallas_call | solution.py:179
  3.6 0.0 copy-start
  3.6 15.0 %all_to_all.20.ctx_ref = bf16[32,16,128]{2,1,0:T(8,128)(2,1)S(1)} all-to-all(bf16[32,16,128]{2,1,0:T(8,128)(2,1)S(1)} %get-tuple-element.19), channel_id=1, replica_groups=mesh['groups'=1,'node'=32] {'node'}, dimensions={0} | all-to-all | bytes 262144 | tf_op jit(solution)/shard_map/all_to_all | solution.py:540
  18.6 0.0 collective-permute-done.peer_ref
  18.6 0.0 copy-start.2
  18.6 0.6 shard_map.132
  19.2 0.0 copy-start.1
  19.3 13.4 %all_to_all.21.sums_ref = bf16[16,2,64,128]{3,2,1,0:T(8,128)(2,1)S(1)} all-to-all(bf16[16,2,64,128]{3,2,1,0:T(8,128)(2,1)S(1)} %shard_map.132), channel_id=1, replica_groups={{0,1,2,3,4,5,6,7,8,9,10,11,12,13,14,15},{16,17,18,19,20,21,22,23,24,25,..., dimensions={0} | all-to-all | bytes 1048576 | tf_op jit(solution)/shard_map/all_to_all | solution.py:546
  32.7 0.1 shard_map.133
  32.8 0.9 %collective-permute-start.1 = (bf16[272,128]{1,0:T(8,128)(2,1)S(1)}, bf16[272,128]{1,0:T(8,128)(2,1)S(1)}, u32[]{:S(2)}, u32[]{:S(2)}) collective-permute-start(bf16[272,128]{1,0:T(8,128)(2,1)S(1)} %get-tuple-element.24), channel_id=1, source_target_pairs={{0,16},{1,17},{2,18},{3,19},{4,20},{5,21},{6,22},{7,23},{8,24},{9,... | collective-permute-start | bytes 208904 | tf_op jit(solution)/shard_map/ppermute | solution.py:568
  33.6 5.1 %collective-permute-done.1.pay_ref = bf16[272,128]{1,0:T(8,128)(2,1)S(1)} collective-permute-done((bf16[272,128]{1,0:T(8,128)(2,1)S(1)}, bf16[272,128]{1,0:T(8,128)(2,1)S(1)}, u32[]{:S(2)}, u32[]{:S(2)}) %collective-permute-start.1) | collective-permute-done | bytes 69664 | tf_op jit(solution)/shard_map/ppermute | solution.py:568
  38.8 0.0 copy-done
  38.8 0.3 shard_map.134
  39.1 10.3 %all_to_all.22 = bf16[16,2,32,128]{3,2,1,0:T(8,128)(2,1)S(1)} all-to-all(bf16[16,2,32,128]{3,2,1,0:T(8,128)(2,1)S(1)} %get-tuple-element.26), channel_id=1, replica_groups={{0,1,2,3,4,5,6,7,8,9,10,11,12,13,14,15},{16,17,18,19,20,21,22,23,24,25,..., dimensions={0} | all-to-all | bytes 524288 | tf_op jit(solution)/shard_map/all_to_all | solution.py:546
  49.4 0.0 collective-permute-start.2
  49.4 0.0 copy-done.2
  49.4 0.0 copy-done.1
  49.4 0.8 %shard_map.135 = (f32[64,384]{1,0:T(8,128)S(1)}, f32[64,384]{1,0:T(8,128)S(1)}) custom-call(bf16[16,64,128]{2,1,0:T(8,128)(2,1)S(1)} %bitcast.3, bf16[1,4096,384]{2,1,0:T(8,128)(2,1)S(1)} %copy-done.1, bf16[1,4096,384]{2,1,0:T(8,128)(2,1)S(1)} %copy-done.2), custom_call_target="tpu_custom_call" | custom-call | flops 201326592 | bytes 3145728 | tf_op jit(solution)/shard_map/pallas_call | solution.py:446
  50.2 0.7 %collective-permute-done.2.peer_ref = bf16[16,64,128]{2,1,0:T(8,128)(2,1)S(1)} collective-permute-done((bf16[16,64,128]{2,1,0:T(8,128)(2,1)S(1)}, bf16[16,64,128]{2,1,0:T(8,128)(2,1)S(1)}, u32[]{:S(2)}, u32[]{:S(2)}) %collective-permute-start.2) | collective-permute-done | bytes 262176 | tf_op jit(solution)/shard_map/ppermute | solution.py:537
  50.9 1.2 %shard_map.136 = (bf16[64,384]{1,0:T(8,128)(2,1)S(1)}, bf16[32,32,128]{2,1,0:T(8,128)(2,1)S(1)}) custom-call(bf16[16,64,128]{2,1,0:T(8,128)(2,1)S(1)} %collective-permute-done.2.peer_ref, f32[64,384]{1,0:T(8,128)S(1)} %get-tuple-element.27.gate_in, f32[64,384]{1,0:T(8,128)S(1)} %get-tuple-element.28.up_in, bf16[1,4096,384]{2,1,0:T(8,128)(2,1)S(1)} %copy-done.1, ...), custom_call_target="tpu_custom_call" | custom-call | flops 301989888 | bytes 4718592 | tf_op jit(solution)/shard_map/pallas_call | solution.py:455
  52.1 0.2 collective-permute-start.3
  52.3 1.0 %shard_map.137 = (bf16[32,32,128]{2,1,0:T(8,128)(2,1)S(1)}, bf16[4,4096]{1,0:T(4,128)(2,1)}) custom-call(bf16[64,384]{1,0:T(8,128)(2,1)S(1)} %get-tuple-element.29.act_ref, bf16[1,384,4096]{2,1,0:T(8,128)(2,1)S(1)} %copy-done, f32[128,128]{1,0:T(8,128)S(1)} %get-tuple-element.30.a32_ref), custom_call_target="tpu_custom_call" | custom-call | flops 100663296 | bytes 1572864 | tf_op jit(solution)/shard_map/pallas_call | solution.py:467
  53.4 0.4 collective-permute-done.3
  53.7 0.1 add_convert_fusion
  53.8 12.3 %all_to_all.23.back_ref = bf16[32,32,128]{2,1,0:T(8,128)(2,1)S(1)} all-to-all(bf16[32,32,128]{2,1,0:T(8,128)(2,1)S(1)} %add_convert_fusion), channel_id=1, replica_groups=mesh['groups'=1,'node'=32] {'node'}, dimensions={0} | all-to-all | bytes 524288 | tf_op jit(solution)/shard_map/all_to_all | solution.py:540
  66.1 0.8 %shard_map.138 = bf16[4,4096]{1,0:T(4,128)(2,1)} custom-call(f32[128,128]{1,0:T(8,128)S(1)} %get-tuple-element.32.weight_ref, bf16[32,32,128]{2,1,0:T(8,128)(2,1)S(1)} %all_to_all.23.back_ref, f32[128,128]{1,0:T(8,128)S(1)} %get-tuple-element.35.mixed_ref), custom_call_target="tpu_custom_call" | custom-call | tf_op jit(solution)/shard_map/pallas_call | solution.py:506
Async XLA Ops:
  0.6 18.0 %collective-permute-start = (bf16[256,4096]{1,0:T(8,128)(2,1)}, bf16[256,4096]{1,0:T(8,128)(2,1)S(1)}, u32[]{:S(2)}, u32[]{:S(2)}) collective-permute-start(bf16[256,4096]{1,0:T(8,128)(2,1)} %w_hbm.1), channel_id=1, source_target_pairs={{0,1},{1,0},{2,3},{3,2},{4,5},{5,4},{6,7},{7,6},{8,9},{9,8},{10,11... | collective-permute-start | bytes 6291464 | tf_op jit(solution)/shard_map/ppermute | solution.py:537
  3.6 35.2 %copy-start = (bf16[1,384,4096]{2,1,0:T(8,128)(2,1)S(1)}, bf16[1,384,4096]{2,1,0:T(8,128)(2,1)}, u32[]{:S(2)}) copy-start(bf16[1,384,4096]{2,1,0:T(8,128)(2,1)} %down_ref.5) | copy-start | bytes 9437188
  18.6 30.8 %copy-start.2 = (bf16[1,4096,384]{2,1,0:T(8,128)(2,1)S(1)}, bf16[1,4096,384]{2,1,0:T(8,128)(2,1)}, u32[]{:S(2)}) copy-start(bf16[1,4096,384]{2,1,0:T(8,128)(2,1)} %up_ref.3) | copy-start | bytes 9437188
  19.2 30.2 %copy-start.1 = (bf16[1,4096,384]{2,1,0:T(8,128)(2,1)S(1)}, bf16[1,4096,384]{2,1,0:T(8,128)(2,1)}, u32[]{:S(2)}) copy-start(bf16[1,4096,384]{2,1,0:T(8,128)(2,1)} %gate_ref.3) | copy-start | bytes 9437188
  32.8 6.0 %collective-permute-start.1 = (bf16[272,128]{1,0:T(8,128)(2,1)S(1)}, bf16[272,128]{1,0:T(8,128)(2,1)S(1)}, u32[]{:S(2)}, u32[]{:S(2)}) collective-permute-start(bf16[272,128]{1,0:T(8,128)(2,1)S(1)} %get-tuple-element.24), channel_id=1, source_target_pairs={{0,16},{1,17},{2,18},{3,19},{4,20},{5,21},{6,22},{7,23},{8,24},{9,... | collective-permute-start | bytes 208904 | tf_op jit(solution)/shard_map/ppermute | solution.py:568
  49.4 1.5 %collective-permute-start.2 = (bf16[16,64,128]{2,1,0:T(8,128)(2,1)S(1)}, bf16[16,64,128]{2,1,0:T(8,128)(2,1)S(1)}, u32[]{:S(2)}, u32[]{:S(2)}) collective-permute-start(bf16[16,64,128]{2,1,0:T(8,128)(2,1)S(1)} %bitcast.2), channel_id=1, source_target_pairs={{0,1},{1,0},{2,3},{3,2},{4,5},{5,4},{6,7},{7,6},{8,9},{9,8},{10,11... | collective-permute-start | bytes 786440 | tf_op jit(solution)/shard_map/ppermute | solution.py:537
  52.1 1.6 %collective-permute-start.3 = (bf16[32,32,128]{2,1,0:T(8,128)(2,1)S(1)}, bf16[32,32,128]{2,1,0:T(8,128)(2,1)S(1)}, u32[]{:S(2)}, u32[]{:S(2)}) collective-permute-start(bf16[32,32,128]{2,1,0:T(8,128)(2,1)S(1)} %get-tuple-element.34), channel_id=1, source_target_pairs={{0,1},{1,0},{2,3},{3,2},{4,5},{5,4},{6,7},{7,6},{8,9},{9,8},{10,11... | collective-permute-start | bytes 786440 | tf_op jit(solution)/shard_map/ppermute | solution.py:537

commit v8 on v7

--- a/solution.py
+++ b/solution.py
@@ -63,8 +63,11 @@
         pltpu.make_async_copy(source, target, sems.at[i])
         for i, (source, target) in enumerate(pairs)
     ]
-    for copy in copies:
+    for copy in copies[2:3] + copies[:1] + copies[4 : 4 + rows] + copies[1:2] + copies[3:4]:
         copy.start()
+    for copy in copies[4 + 2 * rows : 7 + 2 * rows] + copies[4 + rows : 4 + 2 * rows]:
+        copy.start()
+    copies[7 + 2 * rows].start()
     copies[2].wait()
     for h in range(heads):
         q32[pl.ds(h, rows, stride=heads), :] = qv[:, h * HEAD : (h + 1) * HEAD].astype(F32)
@@ -82,6 +85,11 @@
             slot = expert * cap + used
             weight_ref[pl.ds(row * slots + slot, 1), :] = jnp.full((1, LANE), route[row, k], F32)
             pick_ref[pl.ds(slot * rows + row, 1), :] = jnp.ones((1, LANE), F32)
+    copies[4 + 2 * rows].wait()
+    total = h32_ref.shape[0] // rows
+    for t in range(total):
+        cols = slice(t * LANE, (t + 1) * LANE)
+        h32_ref[pl.ds(t, rows, stride=total), :] = hv[:, cols].astype(F32)
     copies[1].wait()
     copies[3].wait()
 
@@ -146,11 +154,6 @@
         ).astype(BF16)
         out_ref[2 * i] = block
         out_ref[2 * i + 1] = block
-    copies[4 + 2 * rows].wait()
-    total = h32_ref.shape[0] // rows
-    for t in range(total):
-        cols = slice(t * LANE, (t + 1) * LANE)
-        h32_ref[pl.ds(t, rows, stride=total), :] = hv[:, cols].astype(F32)
     copies[5 + 2 * rows].wait()
     for copy in copies[7 + 2 * rows :]:
         copy.wait()

time: 67.2 us -> 67.1 us (level)
  no operation moved by 1% of the time
where the time goes in v8:
time: 67.1 us; the launch traced here: 66.9 us
  blocking collectives  51.1 us (76%)
  Pallas kernels  7.15 us (11%)
  waiting for transfers between devices  6.25 us (9%)
  starting transfers between devices  1.58 us (2%)
  between operations  0.71 us (1%)
    all_to_all x2, blocking collectives, exchange(): lax.all_to_all(array, 'node', split_axis=0, concat_axis=0, tiled=True)  27.3 us
    all_to_all x2, blocking collectives, exchange_inside(): lax.all_to_all(array, 'node', split_axis=0, concat_axis=0, tiled=True, ax...  23.8 us
    ppermute x1, waiting for transfers between devices, body(): pay = lax.ppermute(pay, 'node', [(i, i ^ side) for i in range(devices)])  5.15 us
    pallas_call x1, Pallas kernels, attention(): pl.pallas_call(functools.partial(attention_kernel, cap), in_specs=[pl.Blo...  2.38 us
  transfers between devices with their start and end apart: 4, of which 3 were waited for; matrix products, arithmetic and copies ran while one was open for 0% of the time, Pallas kernels for 6%

profile of v8, /device:TPU:0, one launch (start us, length us, event | category | flops | bytes accessed | tf_op | source)
XLA Modules:
  0.0 66.9 jit_solution(11256841539395178414)
XLA Ops:
  0.6 0.5 collective-permute-start
  1.2 2.4 %shard_map.131 = (bf16[32,16,128]{2,1,0:T(8,128)(2,1)S(1)}, f32[128,128]{1,0:T(8,128)S(1)}, f32[128,128]{1,0:T(8,128)S(1)}, f32[128,128]{1,0:T(8,128)S(1)}, f32[...) custom-call(bf16[4,8192]{1,0:T(4,128)(2,1)} %q_hbm.1, bf16[4,2,512]{2,1,0:T(2,128)(2,1)} %new_hbm.1, ...), custom_call_target="tpu_custom_call" | custom-call | tf_op jit(solution)/shard_map/pallas_call | solution.py:182
  3.5 0.0 copy-start
  3.5 15.0 %all_to_all.20.ctx_ref = bf16[32,16,128]{2,1,0:T(8,128)(2,1)S(1)} all-to-all(bf16[32,16,128]{2,1,0:T(8,128)(2,1)S(1)} %get-tuple-element.19), channel_id=1, replica_groups=mesh['groups'=1,'node'=32] {'node'}, dimensions={0} | all-to-all | bytes 262144 | tf_op jit(solution)/shard_map/all_to_all | solution.py:543
  18.5 0.0 collective-permute-done.peer_ref
  18.5 0.0 copy-start.2
  18.6 0.6 shard_map.132
  19.2 0.0 copy-start.1
  19.2 13.4 %all_to_all.21.sums_ref = bf16[16,2,64,128]{3,2,1,0:T(8,128)(2,1)S(1)} all-to-all(bf16[16,2,64,128]{3,2,1,0:T(8,128)(2,1)S(1)} %shard_map.132), channel_id=1, replica_groups={{0,1,2,3,4,5,6,7,8,9,10,11,12,13,14,15},{16,17,18,19,20,21,22,23,24,25,..., dimensions={0} | all-to-all | bytes 1048576 | tf_op jit(solution)/shard_map/all_to_all | solution.py:549
  32.6 0.1 shard_map.133
  32.7 0.9 %collective-permute-start.1 = (bf16[272,128]{1,0:T(8,128)(2,1)S(1)}, bf16[272,128]{1,0:T(8,128)(2,1)S(1)}, u32[]{:S(2)}, u32[]{:S(2)}) collective-permute-start(bf16[272,128]{1,0:T(8,128)(2,1)S(1)} %get-tuple-element.24), channel_id=1, source_target_pairs={{0,16},{1,17},{2,18},{3,19},{4,20},{5,21},{6,22},{7,23},{8,24},{9,... | collective-permute-start | bytes 208904 | tf_op jit(solution)/shard_map/ppermute | solution.py:571
  33.6 5.1 %collective-permute-done.1.pay_ref = bf16[272,128]{1,0:T(8,128)(2,1)S(1)} collective-permute-done((bf16[272,128]{1,0:T(8,128)(2,1)S(1)}, bf16[272,128]{1,0:T(8,128)(2,1)S(1)}, u32[]{:S(2)}, u32[]{:S(2)}) %collective-permute-start.1) | collective-permute-done | bytes 69664 | tf_op jit(solution)/shard_map/ppermute | solution.py:571
  38.7 0.0 copy-done
  38.7 0.3 shard_map.134
  39.0 10.3 %all_to_all.22 = bf16[16,2,32,128]{3,2,1,0:T(8,128)(2,1)S(1)} all-to-all(bf16[16,2,32,128]{3,2,1,0:T(8,128)(2,1)S(1)} %get-tuple-element.26), channel_id=1, replica_groups={{0,1,2,3,4,5,6,7,8,9,10,11,12,13,14,15},{16,17,18,19,20,21,22,23,24,25,..., dimensions={0} | all-to-all | bytes 524288 | tf_op jit(solution)/shard_map/all_to_all | solution.py:549
  49.3 0.0 collective-permute-start.2
  49.3 0.0 copy-done.2
  49.3 0.0 copy-done.1
  49.3 0.8 %shard_map.135 = (f32[64,384]{1,0:T(8,128)S(1)}, f32[64,384]{1,0:T(8,128)S(1)}) custom-call(bf16[16,64,128]{2,1,0:T(8,128)(2,1)S(1)} %bitcast.3, bf16[1,4096,384]{2,1,0:T(8,128)(2,1)S(1)} %copy-done.1, bf16[1,4096,384]{2,1,0:T(8,128)(2,1)S(1)} %copy-done.2), custom_call_target="tpu_custom_call" | custom-call | flops 201326592 | bytes 3145728 | tf_op jit(solution)/shard_map/pallas_call | solution.py:449
  50.1 0.7 %collective-permute-done.2.peer_ref = bf16[16,64,128]{2,1,0:T(8,128)(2,1)S(1)} collective-permute-done((bf16[16,64,128]{2,1,0:T(8,128)(2,1)S(1)}, bf16[16,64,128]{2,1,0:T(8,128)(2,1)S(1)}, u32[]{:S(2)}, u32[]{:S(2)}) %collective-permute-start.2) | collective-permute-done | bytes 262176 | tf_op jit(solution)/shard_map/ppermute | solution.py:540
  50.9 1.2 %shard_map.136 = (bf16[64,384]{1,0:T(8,128)(2,1)S(1)}, bf16[32,32,128]{2,1,0:T(8,128)(2,1)S(1)}) custom-call(bf16[16,64,128]{2,1,0:T(8,128)(2,1)S(1)} %collective-permute-done.2.peer_ref, f32[64,384]{1,0:T(8,128)S(1)} %get-tuple-element.27.gate_in, f32[64,384]{1,0:T(8,128)S(1)} %get-tuple-element.28.up_in, bf16[1,4096,384]{2,1,0:T(8,128)(2,1)S(1)} %copy-done.1, ...), custom_call_target="tpu_custom_call" | custom-call | flops 301989888 | bytes 4718592 | tf_op jit(solution)/shard_map/pallas_call | solution.py:458
  52.1 0.2 collective-permute-start.3
  52.3 1.0 %shard_map.137 = (bf16[32,32,128]{2,1,0:T(8,128)(2,1)S(1)}, bf16[4,4096]{1,0:T(4,128)(2,1)}) custom-call(bf16[64,384]{1,0:T(8,128)(2,1)S(1)} %get-tuple-element.29.act_ref, bf16[1,384,4096]{2,1,0:T(8,128)(2,1)S(1)} %copy-done, f32[128,128]{1,0:T(8,128)S(1)} %get-tuple-element.30.a32_ref), custom_call_target="tpu_custom_call" | custom-call | flops 100663296 | bytes 1572864 | tf_op jit(solution)/shard_map/pallas_call | solution.py:470
  53.3 0.4 collective-permute-done.3
  53.7 0.1 add_convert_fusion
  53.7 12.3 %all_to_all.23.back_ref = bf16[32,32,128]{2,1,0:T(8,128)(2,1)S(1)} all-to-all(bf16[32,32,128]{2,1,0:T(8,128)(2,1)S(1)} %add_convert_fusion), channel_id=1, replica_groups=mesh['groups'=1,'node'=32] {'node'}, dimensions={0} | all-to-all | bytes 524288 | tf_op jit(solution)/shard_map/all_to_all | solution.py:543
  66.0 0.8 %shard_map.138 = bf16[4,4096]{1,0:T(4,128)(2,1)} custom-call(f32[128,128]{1,0:T(8,128)S(1)} %get-tuple-element.32.weight_ref, bf16[32,32,128]{2,1,0:T(8,128)(2,1)S(1)} %all_to_all.23.back_ref, f32[128,128]{1,0:T(8,128)S(1)} %get-tuple-element.35.mixed_ref), custom_call_target="tpu_custom_call" | custom-call | tf_op jit(solution)/shard_map/pallas_call | solution.py:509
Async XLA Ops:
  0.6 17.9 %collective-permute-start = (bf16[256,4096]{1,0:T(8,128)(2,1)}, bf16[256,4096]{1,0:T(8,128)(2,1)S(1)}, u32[]{:S(2)}, u32[]{:S(2)}) collective-permute-start(bf16[256,4096]{1,0:T(8,128)(2,1)} %w_hbm.1), channel_id=1, source_target_pairs={{0,1},{1,0},{2,3},{3,2},{4,5},{5,4},{6,7},{7,6},{8,9},{9,8},{10,11... | collective-permute-start | bytes 6291464 | tf_op jit(solution)/shard_map/ppermute | solution.py:540
  3.5 35.2 %copy-start = (bf16[1,384,4096]{2,1,0:T(8,128)(2,1)S(1)}, bf16[1,384,4096]{2,1,0:T(8,128)(2,1)}, u32[]{:S(2)}) copy-start(bf16[1,384,4096]{2,1,0:T(8,128)(2,1)} %down_ref.5) | copy-start | bytes 9437188
  18.5 30.8 %copy-start.2 = (bf16[1,4096,384]{2,1,0:T(8,128)(2,1)S(1)}, bf16[1,4096,384]{2,1,0:T(8,128)(2,1)}, u32[]{:S(2)}) copy-start(bf16[1,4096,384]{2,1,0:T(8,128)(2,1)} %up_ref.3) | copy-start | bytes 9437188
  19.2 30.2 %copy-start.1 = (bf16[1,4096,384]{2,1,0:T(8,128)(2,1)S(1)}, bf16[1,4096,384]{2,1,0:T(8,128)(2,1)}, u32[]{:S(2)}) copy-start(bf16[1,4096,384]{2,1,0:T(8,128)(2,1)} %gate_ref.3) | copy-start | bytes 9437188
  32.7 6.0 %collective-permute-start.1 = (bf16[272,128]{1,0:T(8,128)(2,1)S(1)}, bf16[272,128]{1,0:T(8,128)(2,1)S(1)}, u32[]{:S(2)}, u32[]{:S(2)}) collective-permute-start(bf16[272,128]{1,0:T(8,128)(2,1)S(1)} %get-tuple-element.24), channel_id=1, source_target_pairs={{0,16},{1,17},{2,18},{3,19},{4,20},{5,21},{6,22},{7,23},{8,24},{9,... | collective-permute-start | bytes 208904 | tf_op jit(solution)/shard_map/ppermute | solution.py:571
  49.3 1.5 %collective-permute-start.2 = (bf16[16,64,128]{2,1,0:T(8,128)(2,1)S(1)}, bf16[16,64,128]{2,1,0:T(8,128)(2,1)S(1)}, u32[]{:S(2)}, u32[]{:S(2)}) collective-permute-start(bf16[16,64,128]{2,1,0:T(8,128)(2,1)S(1)} %bitcast.2), channel_id=1, source_target_pairs={{0,1},{1,0},{2,3},{3,2},{4,5},{5,4},{6,7},{7,6},{8,9},{9,8},{10,11... | collective-permute-start | bytes 786440 | tf_op jit(solution)/shard_map/ppermute | solution.py:540
  52.1 1.6 %collective-permute-start.3 = (bf16[32,32,128]{2,1,0:T(8,128)(2,1)S(1)}, bf16[32,32,128]{2,1,0:T(8,128)(2,1)S(1)}, u32[]{:S(2)}, u32[]{:S(2)}) collective-permute-start(bf16[32,32,128]{2,1,0:T(8,128)(2,1)S(1)} %get-tuple-element.34), channel_id=1, source_target_pairs={{0,1},{1,0},{2,3},{3,2},{4,5},{5,4},{6,7},{7,6},{8,9},{9,8},{10,11... | collective-permute-start | bytes 786440 | tf_op jit(solution)/shard_map/ppermute | solution.py:540
